TPU v7x, 32 devices: a whole 2x2x4 slice. The times are simulated.
32 devices in a mesh: pix: 8 (over z, y), plane: 4 (over x, core).
Axes of the slice: x: 2, y: 2, z: 4, core: 2. Of those that a mesh axis runs over, the one named last changes fastest.
Arguments:
- movie: bfloat16 [4, 256, 256, 256], P('plane', 'pix'), may hold values from -6 to 6
- footprints: bfloat16 [4, 1024, 1024], P('plane', 'pix'), may hold values from 0 to 0.019897461
- traces: bfloat16 [4, 1024, 256], P('plane', 'pix'), may hold values from 0 to 2
- stripe: int32 [4, 1024, 1], P('plane', 'pix'), may hold values from 0 to 7; in each aligned block of 128 rows (0 to 127, 128 to 255, ..., all dimensions but the last counted through in order) at most 32 rows name the same one
- column: int32 [4, 1024], P('plane', 'pix'), may hold values from 0 to 224
- annulus_gain: float32 [4, 256], P('plane'), may hold values from 1 to 8
- decay_slow: float32 [4, 1024], P('plane', 'pix'), may hold values from 0.4 to 0.9
- decay_fast: float32 [4, 1024], P('plane', 'pix'), may hold values from 0.05 to 0.3
Outputs:
- background: bfloat16 [4, 256, 256, 256], P('plane', 'pix')
- traces_new: float32 [4, 1024, 256], P('plane', 'pix')
Inputs may be any that keep to these rules, and one draw needn't show every extreme that they name: Among the 128 neurons of one device (aligned blocks of 128 neurons of a plane), no stripe is named more than 32 times, and some device names one stripe exactly 32 times.
All inputs are finite; a program needn't handle non-finite values.
Results may differ from a plain program's by a relative error of at most 0.001.
The roundings to bfloat16 on the way count: a program that leaves them out, or rounds other values in their place, can miss the bound.
Values may be sent and summed in bfloat16 or wider, within the bound.
No kernel may reach another device: no remote copies, remote signals or barrier semaphores. Data moves between devices by JAX's collectives and lax.ppermute only.
A program may use at most 128 MiB of HBM per device.

v0:
```python
import functools

import jax
import jax.numpy as jnp
import ml_dtypes
import numpy as np
from jax import lax
from jax.experimental import pallas as pl
from jax.experimental.pallas import tpu as pltpu
from jax.sharding import PartitionSpec as P

FOOT = 32
RAD = 12
GR = 3
LANES = 128
PER = LANES // FOOT
NEAR = PER

lam_floor = 0.1
noise_eps = 1e-05
norm_eps = 1e-05
sigma_twice = 4.5

F32 = jnp.float32
BF16 = jnp.bfloat16
MIB = 1 << 20
HBM = pl.BlockSpec(memory_space=pltpu.HBM)
VMEM = pl.BlockSpec(memory_space=pltpu.VMEM)


def tap_values():
    offsets = np.arange(-GR, GR + 1).astype(np.float32)
    raw = np.exp(-offsets * offsets / np.float32(sigma_twice)).astype(np.float32)
    return (raw / raw.sum(dtype=np.float32)).astype(ml_dtypes.bfloat16).astype(np.float32)


def params(mib=16):
    return pltpu.CompilerParams(vmem_limit_bytes=mib * MIB)


COST = pl.CostEstimate(flops=1, bytes_accessed=1, transcendentals=0)


def dot(a, b):
    return jnp.dot(a, b, preferred_element_type=F32)


def outbox_kernel(capacity, *refs):
    sources, outbox, places, sems = refs[0:4], refs[4], refs[5:9], refs[9]
    copies = [
        pltpu.make_async_copy(source, place, sems.at[k])
        for k, (source, place) in enumerate(zip(sources, places))
    ]
    for copy in copies:
        copy.start()
    for copy in copies:
        copy.wait()
    stripe, column, foot, traces = places
    slots = outbox.shape[0]
    count, tiles = foot.shape
    frames = traces.shape[1]
    before = lax.broadcasted_iota(jnp.int32, (count, count), 0) < lax.broadcasted_iota(
        jnp.int32, (count, count), 1
    )
    named = jnp.broadcast_to(stripe[...].astype(F32), (count, count))
    same = (named == named.T) & before
    rank = jnp.sum(jnp.where(same, 1.0, 0.0), axis=0, keepdims=True).astype(jnp.int32)
    slot = stripe[...] * capacity + rank
    place = lax.broadcasted_iota(jnp.int32, (slots, count), 0)
    left = jnp.broadcast_to(column[...].astype(F32), (LANES, count)).T.astype(BF16)
    lane = lax.broadcasted_iota(jnp.int32, (slots, LANES), 1)
    edge = NEAR * FOOT
    lefts = jnp.zeros((slots, LANES), F32)
    at = 3 * frames
    for k, (shift, first, width) in enumerate(
        ((0, 0, tiles), (capacity, 0, edge), (-capacity, tiles - edge, edge))
    ):
        hot = jnp.where(place + shift == slot, 1.0, 0.0).astype(BF16)
        outbox[:, k * frames : (k + 1) * frames] = dot(hot, traces[...]).astype(BF16)
        outbox[:, at : at + width] = dot(hot, foot[:, first : first + width]).astype(BF16)
        lefts = jnp.where(lane == k, dot(hot, left), lefts)
        at += width
    outbox[:, at:] = lefts.astype(BF16)


def make_outbox(stripe, column, foot, traces, capacity, slots):
    count, tiles = foot.shape
    frames = traces.shape[1]
    width = 3 * frames + tiles + 2 * NEAR * FOOT + LANES
    args = (stripe, column, foot, traces)
    return pl.pallas_call(
        functools.partial(outbox_kernel, capacity),
        in_specs=[HBM] * len(args),
        out_shape=jax.ShapeDtypeStruct((slots, width), BF16),
        scratch_shapes=[pltpu.VMEM(a.shape, a.dtype) for a in args]
        + [pltpu.SemaphoreType.DMA((len(args),))],
        compiler_params=params(56),
        cost_estimate=COST,
        name="outbox",
    )(*args)


def spread(block, col):
    lane = lax.broadcasted_iota(jnp.int32, block.shape, 1)
    for k in range(7):
        block = jnp.where(((col >> k) & 1) == 1, pltpu.roll(block, 1 << k, 1), block)
    inside = ((lane - col) & (LANES - 1)) < FOOT
    left = inside & (lane >= col)
    right = inside & (lane < col)
    rows = []
    for q in range(PER):
        moved = block if q == 0 else pltpu.roll(block, LANES - q * FOOT, 1)
        rows.append(
            jnp.concatenate(
                [jnp.where(left, moved, 0.0), jnp.where(right, moved, 0.0)], axis=1
            ).astype(BF16)
        )
    return rows


def tile_rows(inbox, which, block, frames):
    lefts = inbox[:, inbox.shape[1] - LANES :].astype(F32)
    col = jnp.broadcast_to(lefts[:, which : which + 1], lefts.shape).astype(jnp.int32)
    start = 3 * frames + block * LANES
    if not isinstance(start, int):
        start = pl.multiple_of(start, LANES)
    return spread(inbox[:, pl.ds(start, LANES)].astype(F32), col)


def model_row(row, inbox, which, frames):
    traces = inbox[:, which * frames : (which + 1) * frames]
    return lax.dot_general(row, traces, (((0,), (0,)), ((), ())), preferred_element_type=F32)


def noise_row(left, change):
    frames = left.shape[1]
    steps = dot(left, change)
    steps = steps * steps
    part = steps[:, 0:LANES]
    for k in range(1, frames // LANES):
        part = part + steps[:, k * LANES : (k + 1) * LANES]
    return jnp.sum(part.T, axis=0, keepdims=True) / (frames - 1)


def lag_table(size):
    shape = (size, size)
    return lax.broadcasted_iota(jnp.int32, shape, 1) - lax.broadcasted_iota(jnp.int32, shape, 0)


def change_matrix(frames):
    lag = lag_table(frames)
    steps = jnp.where(lag == -1, 1.0, 0.0) - jnp.where(lag == 0, 1.0, 0.0)
    later = lax.broadcasted_iota(jnp.int32, lag.shape, 1)
    return jnp.where(later < frames - 1, steps, 0.0).astype(BF16)


def residual_kernel(pick, low, high, first, inbox, movie, *refs):
    if not first:
        refs = refs[3:]
    (foot_rows, residual, noise, up, down) = refs[0:5]
    (change, movie_slots, foot_slots, left_slots, sems) = refs[5:]
    frames = movie.shape[3]
    count = pick(None)
    change[...] = change_matrix(frames)

    def fetch(i, slot):
        rows_g = pl.ds(pick(i) * PER, PER)
        return pltpu.make_async_copy(movie.at[0, rows_g], movie_slots.at[slot], sems.at[0, slot])

    def sends(i, slot):
        rows_g = pl.ds(pick(i) * PER, PER)
        return (
            pltpu.make_async_copy(foot_slots.at[slot], foot_rows.at[rows_g], sems.at[1, slot]),
            pltpu.make_async_copy(left_slots.at[slot], residual.at[rows_g], sems.at[2, slot]),
        )

    fetch(0, 0).start()

    def group(i, carry):
        slot = lax.rem(i, 2)
        g = pick(i)

        @pl.when(i + 1 < count)
        def _():
            fetch(i + 1, 1 - slot).start()

        fetch(i, slot).wait()

        @pl.when(i >= 2)
        def _():
            for copy in sends(i - 2, slot):
                copy.wait()

        noises = []
        for q, row in enumerate(tile_rows(inbox, 0, g, frames)):
            foot_slots[slot, q] = row
            left = movie_slots[slot, q].astype(F32) - model_row(row, inbox, 0, frames)
            left = left.astype(BF16)
            left_slots[slot, q] = left
            noises.append(noise_row(left, change[...]))
        noise[i] = jnp.concatenate(noises, axis=0)
        for copy in sends(i, slot):
            copy.start()

        @pl.when(g == low)
        def _():
            down[...] = left_slots[slot]

        @pl.when(g == high)
        def _():
            up[...] = left_slots[slot]

        return carry

    lax.fori_loop(0, count, group, 0)
    for i in (count - 2, count - 1):
        for copy in sends(i, i % 2):
            copy.wait()


def make_residual(inbox, movie, earlier=None):
    slots = inbox.shape[0]
    rows, cols, frames = movie.shape[1:]
    groups = rows // PER
    mids = (1, groups - 2)
    if earlier is None:
        low, high, count = *mids, 2

        def pick(i):
            return count if i is None else mids[0] + i * (mids[1] - mids[0])
    else:
        low, high, count = 2, groups - 3, groups - 2

        def pick(i):
            if i is None:
                return count
            if isinstance(i, int):
                return i + (i >= mids[0]) + (i + 1 >= mids[1])
            return i + jnp.where(i >= mids[0], 1, 0) + jnp.where(i + 1 >= mids[1], 1, 0)

    piece = jax.ShapeDtypeStruct((PER, cols, frames), BF16)
    more = () if earlier is None else earlier
    return pl.pallas_call(
        functools.partial(residual_kernel, pick, low, high, earlier is None),
        in_specs=[VMEM, HBM] + [HBM, HBM, VMEM][: len(more)],
        out_specs=[HBM, HBM, VMEM, VMEM, VMEM],
        out_shape=(
            jax.ShapeDtypeStruct((rows, slots, cols), BF16),
            jax.ShapeDtypeStruct((rows, cols, frames), BF16),
            jax.ShapeDtypeStruct((count, PER, cols), F32),
            piece,
            piece,
        ),
        scratch_shapes=[
            pltpu.VMEM((frames, frames), BF16),
            pltpu.VMEM((2, PER, cols, frames), BF16),
            pltpu.VMEM((2, PER, slots, cols), BF16),
            pltpu.VMEM((2, PER, cols, frames), BF16),
            pltpu.SemaphoreType.DMA((3, 2)),
        ],
        input_output_aliases={} if earlier is None else {2: 0, 3: 1},
        compiler_params=params(44),
        cost_estimate=COST,
        name="residual",
    )(inbox, movie, *more)


def near_kernel(
    inbox, movie_next, movie_prev, mid_noise, other_noise, foot_rows, residual, noise
):
    frames = movie_next.shape[2]
    groups = mid_noise.shape[0] + other_noise.shape[0]
    own = FOOT // PER
    change = change_matrix(frames)
    others = [g for g in range(groups) if g not in (1, groups - 2)]
    for order, part in (((1, groups - 2), mid_noise), (others, other_noise)):
        for i, g in enumerate(order):
            noise[NEAR + g * PER : NEAR + (g + 1) * PER, :] = part[i]
    for side, (block, movie, first) in enumerate(
        ((own, movie_next, 0), (own + NEAR // PER, movie_prev, NEAR + groups * PER))
    ):
        for q, row in enumerate(tile_rows(inbox, 1 + side, block, frames)):
            y = side * NEAR + q
            foot_rows[y] = row
            left = movie[q].astype(F32) - model_row(row, inbox, 1 + side, frames)
            left = left.astype(BF16)
            residual[y] = left
            noise[first + q : first + q + 1, :] = noise_row(left, change)


def make_near(inbox, movie_next, movie_prev, noises):
    slots = inbox.shape[0]
    cols, frames = movie_next.shape[1:]
    return pl.pallas_call(
        near_kernel,
        out_shape=(
            jax.ShapeDtypeStruct((2 * NEAR, slots, cols), BF16),
            jax.ShapeDtypeStruct((2 * NEAR, cols, frames), BF16),
            jax.ShapeDtypeStruct((2 * NEAR + PER * sum(n.shape[0] for n in noises), cols), F32),
        ),
        compiler_params=params(),
        cost_estimate=COST,
        name="near",
    )(inbox, movie_next, movie_prev, *noises)


def weights_kernel(
    taps, own, near, noise, noise_before, noise_after, out, out_next, out_prev,
    own_slots, scale, band, sems,
):
    rows, slots, cols = own.shape
    part = own_slots.shape[2]
    count = slots // part

    def fetch(i, slot):
        these = pl.ds(pl.multiple_of(i * part, part), part)
        return pltpu.make_async_copy(own.at[:, these, :], own_slots.at[slot], sems.at[slot])

    fetch(0, 0).start()
    pooled = (noise_before[...] + 2.0 * noise[...] + noise_after[...]) / 4.0
    scale[...] = 1.0 / jnp.sqrt(pooled + noise_eps)
    lag = jnp.abs(lag_table(cols))
    table = jnp.zeros(lag.shape, F32)
    for k in range(GR + 1):
        table = jnp.where(lag == k, taps[GR + k], table)
    band[...] = table.astype(BF16)

    def across(foot, inv):
        scaled = (foot.astype(F32) * inv[:, None, :]).astype(BF16)
        count = foot.shape[0]
        return dot(scaled.reshape(count * part, cols), band[...]).reshape(count, part, cols)

    def some(i, carry):
        slot = lax.rem(i, 2)

        @pl.when(i + 1 < count)
        def _():
            fetch(i + 1, 1 - slot).start()

        fetch(i, slot).wait()
        these = pl.ds(pl.multiple_of(i * part, part), part)
        blurred = across(own_slots[slot], scale[NEAR : NEAR + rows])
        for r in range(rows):
            total = taps[GR] * blurred[r]
            for k in range(1, GR + 1):
                if r - k >= 0 and r + k < rows:
                    total = total + taps[GR + k] * (blurred[r - k] + blurred[r + k])
                elif r - k >= 0:
                    total = total + taps[GR + k] * blurred[r - k]
                elif r + k < rows:
                    total = total + taps[GR + k] * blurred[r + k]
            out[r, these, :] = total.astype(BF16)
        after = across(near[0:GR, these, :], scale[0:GR])
        ahead = across(near[2 * NEAR - GR : 2 * NEAR, these, :], scale[rows + 2 * NEAR - GR :])
        for a in range(GR):
            total = taps[2 * GR - a] * after[0]
            for r in range(1, a + 1):
                total = total + taps[2 * GR + r - a] * after[r]
            out_next[a, these, :] = total.astype(BF16)
            total = taps[2 * GR] * ahead[a]
            for b in range(a + 1, GR):
                total = total + taps[2 * GR + a - b] * ahead[b]
            out_prev[a, these, :] = total.astype(BF16)
        return carry

    lax.fori_loop(0, count, some, 0)


def make_weights(foot_rows, near_rows, noises):
    rows, slots, cols = foot_rows.shape
    part = 32
    return pl.pallas_call(
        functools.partial(weights_kernel, [float(t) for t in tap_values()]),
        in_specs=[HBM] + [VMEM] * (1 + len(noises)),
        out_shape=(
            jax.ShapeDtypeStruct((rows, slots, cols), BF16),
            jax.ShapeDtypeStruct((GR, slots, cols), BF16),
            jax.ShapeDtypeStruct((GR, slots, cols), BF16),
        ),
        scratch_shapes=[
            pltpu.VMEM((2, rows, part, cols), BF16),
            pltpu.VMEM(noises[0].shape, F32),
            pltpu.VMEM((cols, cols), BF16),
            pltpu.SemaphoreType.DMA((2,)),
        ],
        compiler_params=params(32),
        cost_estimate=COST,
        name="weights",
    )(foot_rows, near_rows, *noises)


def annulus_group(g, own, leaving, entering, gain, band, column, outgoing):
    cols, frames = own.shape[1:]
    top = lax.broadcasted_iota(jnp.int32, (cols // 8, 8, LANES), 1) < 4
    blank = jnp.zeros((2, 8, LANES), F32)
    outs = [leaving(q) for q in range(PER)]
    news = [entering(q) for q in range(PER)]
    levels = [dot(band, jnp.concatenate([o, n], axis=0)) for o, n in zip(outs, news)]
    column = list(column)
    dets = []
    for q in range(PER):
        det = []
        for h in range(frames // LANES):
            part = slice(h * LANES, (h + 1) * LANES)
            inner = column[h] - outs[q][:, part].astype(F32)
            column[h] = inner + news[q][:, part].astype(F32)
            turned = pltpu.roll(inner.reshape(cols // 8, 8, LANES), 4, 1)
            turned = jnp.concatenate([blank, turned, blank], axis=0)
            both = turned[0 : cols // 8 + 1] + turned[3 : cols // 8 + 4]
            sides = jnp.where(top, both[0 : cols // 8], both[1 : cols // 8 + 1])
            fit = (levels[q][:, part] + sides.reshape(cols, LANES)) * gain
            outgoing[g, q, :, part] = fit.astype(BF16)
            det.append((own[g * PER + q, :, part].astype(F32) - fit).astype(BF16))
        dets.append(jnp.concatenate(det, axis=1))
    return column, dets


def grow(total, weight, g, dets):
    weights = jnp.concatenate([weight[g * PER + q] for q in range(PER)], axis=1)
    return total + dot(weights, jnp.concatenate(dets, axis=0))


def halves(ref):
    return [ref[:, h * LANES : (h + 1) * LANES] for h in range(ref.shape[1] // LANES)]


def add_rows(column, rows, sign=1.0):
    for row in rows:
        column = [c + sign * r.astype(F32) for c, r in zip(column, halves(row))]
    return column


def put(ref, column):
    for h, value in enumerate(column):
        ref[:, h * LANES : (h + 1) * LANES] = value


def sender(outgoing, background, sems):
    def send(g):
        return pltpu.make_async_copy(
            outgoing.at[g], background.at[0, pl.ds(g * PER, PER)], sems.at[g]
        )

    return send


def tables(gain):
    cols = gain.shape[1]
    band = jnp.where(jnp.abs(lag_table(cols)) <= RAD, 1.0, 0.0).astype(BF16)
    return (
        jnp.broadcast_to(gain[...], (LANES, cols)).T / (8.0 * RAD),
        jnp.concatenate([band, band], axis=1),
    )


def middle_kernel(own, near, weight, gain, background, upper, lower, total, outgoing, sems):
    rows, cols, frames = own.shape
    groups = range((RAD - NEAR) // PER, (rows - RAD + NEAR) // PER)
    send = sender(outgoing, background, sems)
    gains, band = tables(gain)
    column = [jnp.zeros((cols, LANES), F32)] * (frames // LANES)
    column = add_rows(column, [near[NEAR + r] for r in range(NEAR)])
    column = add_rows(column, [own[r] for r in range(RAD)])
    put(upper, column)
    column = add_rows(column, [own[RAD + r] for r in range(2 * RAD - NEAR - RAD)])
    grown = jnp.zeros(total.shape, F32)
    for g in groups:
        y = g * PER
        column, dets = annulus_group(
            g,
            own,
            (lambda q: near[NEAR + y - RAD + NEAR + q])
            if y < RAD
            else (lambda q: own[y - RAD + q]),
            (lambda q: near[y + RAD - rows + q])
            if y + RAD >= rows
            else (lambda q: own[y + RAD + q]),
            gains, band, column, outgoing,
        )
        send(g).start()
        grown = grow(grown, weight, g, dets)
    put(lower, column)
    total[...] = grown
    for g in groups:
        send(g).wait()


def mid_kernel(
    own, above, below, weight, gain, before, upper, lower, total,
    background, new_upper, new_lower, new_total, outgoing, sems,
):
    del before
    rows = own.shape[0]
    low, high = RAD // PER - 2, (rows - RAD) // PER + 1
    y, z = low * PER, high * PER
    send = sender(outgoing, background, sems)
    gains, band = tables(gain)
    column = add_rows(halves(upper), [above[r] for r in range(PER)])
    put(new_upper, column)
    column = add_rows(column, [own[RAD + r] for r in range(PER)])
    _, low_dets = annulus_group(
        low, own, lambda q: above[q], lambda q: own[y + RAD + q], gains, band, column, outgoing
    )
    send(low).start()
    column, high_dets = annulus_group(
        high, own, lambda q: own[z - RAD + q], lambda q: below[q], gains, band, halves(lower),
        outgoing,
    )
    send(high).start()
    put(new_lower, column)
    new_total[...] = grow(grow(total[...], weight, low, low_dets), weight, high, high_dets)
    send(low).wait()
    send(high).wait()


def end_kernel(
    own, above, below, weight, weight_next, weight_prev, gain, before,
    upper, lower, total, background, gradient, outgoing, sems,
):
    del before
    rows, _, frames = own.shape
    low, high = 0, rows // PER - 1
    z = high * PER
    send = sender(outgoing, background, sems)
    gains, band = tables(gain)
    _, low_dets = annulus_group(
        low, own, lambda q: above[q], lambda q: own[RAD + q], gains, band,
        add_rows(halves(upper), [above[r] for r in range(PER)]), outgoing,
    )
    send(low).start()
    _, high_dets = annulus_group(
        high, own, lambda q: own[z - RAD + q], lambda q: below[q], gains, band, halves(lower),
        outgoing,
    )
    send(high).start()
    grown = grow(grow(total[...], weight, low, low_dets), weight, high, high_dets)
    edges = ((2, weight_next, high_dets[PER - GR :]), (3, weight_prev, low_dets[:GR]))
    for at, edge, parts in edges:
        value = dot(
            jnp.concatenate([edge[a] for a in range(GR)], axis=1), jnp.concatenate(parts, axis=0)
        )
        gradient[:, at * frames : (at + 1) * frames] = value.astype(BF16)
    coarse = grown.astype(BF16)
    gradient[:, 0:frames] = coarse
    gradient[:, frames : 2 * frames] = (grown - coarse.astype(F32)).astype(BF16)
    send(low).wait()
    send(high).wait()


def make_annulus(own, near, mid, far, weights, gain):
    rows, cols, frames = own.shape
    weight, weight_next, weight_prev = weights
    slots = weight.shape[1]
    background = jax.ShapeDtypeStruct((1, rows, cols, frames), BF16)
    column = jax.ShapeDtypeStruct((cols, frames), F32)
    total = jax.ShapeDtypeStruct((slots, frames), F32)
    gradient = jax.ShapeDtypeStruct((slots, 4 * frames), BF16)

    def call(kernel, name, args, outs, done, declared=COST):
        specs = [VMEM] * len(args)
        if done is not None:
            specs[done] = HBM
        return pl.pallas_call(
            kernel,
            in_specs=specs,
            out_specs=[HBM] + [VMEM] * (len(outs) - 1),
            out_shape=outs,
            scratch_shapes=[
                pltpu.VMEM((rows // PER, PER, cols, frames), BF16),
                pltpu.SemaphoreType.DMA((rows // PER,)),
            ],
            input_output_aliases={} if done is None else {done: 0},
            compiler_params=params(),
            cost_estimate=declared,
            name=name,
        )(*args)

    done, upper, lower, grown = call(
        middle_kernel, "annulus_middle", (own, near, weight, gain),
        (background, column, column, total), None,
    )
    done, upper, lower, grown = call(
        mid_kernel, "annulus_mid",
        (own, *mid, weight, gain, done, upper, lower, grown),
        (background, column, column, total), 5,
        pl.CostEstimate(
            flops=2 * rows * cols * cols * frames, bytes_accessed=5 * MIB, transcendentals=0
        ),
    )
    return call(
        end_kernel, "annulus_end",
        (own, *far, weight, weight_next, weight_prev, gain, done, upper, lower, grown),
        (background, gradient), 7,
    )


def traces_kernel(capacity, stripe, slow, fast, step, traces, inbox, out):
    count, frames = traces.shape
    slots = inbox.shape[0]

    def upended(row):
        return jnp.broadcast_to(row[...].astype(F32), (LANES, count)).T

    before = lax.broadcasted_iota(jnp.int32, (count, count), 1) < lax.broadcasted_iota(
        jnp.int32, (count, count), 0
    )
    named = upended(stripe)
    same = (named == stripe[...].astype(F32)) & before
    rank = jnp.sum(jnp.where(same, 1.0, 0.0), axis=1, keepdims=True)
    slot = (named[:, 0:1] * capacity + rank).astype(jnp.int32)
    place = lax.broadcasted_iota(jnp.int32, (count, slots), 1)

    def onehot(shift):
        return jnp.where(place + shift == slot, 1.0, 0.0).astype(BF16)

    here = onehot(0)
    gradient = (
        dot(here, inbox[:, 0:frames])
        + dot(here, inbox[:, frames : 2 * frames])
        + dot(onehot(capacity), inbox[:, 2 * frames : 3 * frames])
        + dot(onehot(-capacity), inbox[:, 3 * frames : 4 * frames])
    )

    def wide(row):
        return jnp.concatenate([upended(row)] * (frames // LANES), axis=1)

    updated = traces[...].astype(F32) + wide(step) * gradient
    lane = lax.broadcasted_iota(jnp.int32, (count, frames), 1)

    def lagged(value, lag):
        return jnp.where(lane >= lag, pltpu.roll(value, lag, 1), 0.0)

    a, b = wide(slow), wide(fast)
    driven = updated - (a + b) * lagged(updated, 1) + (a * b) * lagged(updated, 2)
    spikes = jnp.maximum(driven - lam_floor, 0.0)
    sums = [spikes, spikes]
    roots = [a, b]
    lag = 1
    while lag < frames:
        sums = [value + root * lagged(value, lag) for value, root in zip(sums, roots)]
        roots = [root * root for root in roots]
        lag *= 2
    share = (1.0 - a) * (1.0 - b) / (a - b)
    out[...] = share * (a * sums[0] - b * sums[1])


def make_traces(stripe, slow, fast, step, traces, inbox, capacity):
    count, frames = traces.shape
    return pl.pallas_call(
        functools.partial(traces_kernel, capacity),
        out_shape=jax.ShapeDtypeStruct((count, frames), F32),
        compiler_params=params(),
        cost_estimate=COST,
        name="traces",
    )(stripe, slow, fast, step, traces, inbox)


def neighbours(axis):
    devices = lax.axis_size(axis)
    up = [(i, i + 1) for i in range(devices - 1)]
    return up, [(j, i) for i, j in up]


def on_device(movie, footprints, traces, stripe, column, annulus_gain, decay_slow, decay_fast):
    pix_count = lax.axis_size("pix")
    rows, cols, frames = movie.shape[1:]
    count = footprints.shape[1]
    capacity = max(2, 2 * count // pix_count)
    slots = pix_count * capacity
    pix_up, pix_down = neighbours("pix")
    plane_up, plane_down = neighbours("plane")

    stripe_row = stripe.reshape(1, count)
    outbox = make_outbox(stripe_row, column, footprints[0], traces[0], capacity, slots)
    def exchange(up, down):
        return (lax.ppermute(up, "pix", pix_up), lax.ppermute(down, "pix", pix_down))

    frames_in, outbox = lax.optimization_barrier((movie, outbox))
    inbox = lax.all_to_all(outbox, "pix", split_axis=0, concat_axis=0, tiled=True)
    near_prev, near_next = exchange(frames_in[0, rows - NEAR :], frames_in[0, :NEAR])
    *started, mid_noise, up, down = make_residual(inbox, movie)
    mid = exchange(up, down)
    foot_rows, residual, other_noise, up, down = make_residual(
        inbox, movie, (*started, mid_noise)
    )
    near_rows, near_residual, noise = make_near(
        inbox, near_next, near_prev, (mid_noise, other_noise)
    )
    up, down, noise = lax.optimization_barrier((up, down, noise))
    far = exchange(up, down)
    noises = (
        noise,
        lax.ppermute(noise, "plane", plane_up),
        lax.ppermute(noise, "plane", plane_down),
    )
    weights = make_weights(foot_rows, near_rows, noises)
    background, gradient = make_annulus(
        residual, near_residual, mid, far, weights, annulus_gain
    )
    home = lax.all_to_all(gradient, "pix", split_axis=0, concat_axis=0, tiled=True)
    foot_f = footprints[0].astype(F32)
    step = 1.0 / (jnp.sum(foot_f * foot_f, axis=1) + norm_eps)
    traces_new = make_traces(
        stripe_row, decay_slow, decay_fast, step[None], traces[0], home, capacity
    )
    return (background, traces_new[None])


def solution(mesh):
    placed = (
        P("plane", "pix", None, None),
        P("plane", "pix", None),
        P("plane", "pix", None),
        P("plane", "pix", None),
        P("plane", "pix"),
        P("plane", None),
        P("plane", "pix"),
        P("plane", "pix"),
    )
    return jax.shard_map(
        on_device,
        mesh=mesh,
        in_specs=placed,
        out_specs=(P("plane", "pix", None, None), P("plane", "pix", None)),
        check_vma=False,
    )
```

profile of v0, /device:TPU:0, one launch (start us, length us, event | category | flops | bytes accessed | tf_op | source)
XLA Modules:
  0.0 116.4 jit_solution(5718657121123352523)
XLA Ops:
  0.6 2.6 %outbox.1 = bf16[256,2176]{1,0:T(8,128)(2,1)} custom-call(s32[1,128]{1,0:T(1,128)} %bitcast.21, s32[1,128]{1,0:T(1,128)} %refs_1_.1, bf16[128,1024]{1,0:T(8,128)(2,1)} %bitcast.24, bf16[128,256]{1,0:T(8,128)(2,1)} %bitcast.19), custom_call_target="tpu_custom_call" | custom-call | flops 1 | bytes 1 | tf_op jit(solution)/shard_map/outbox/pallas_call | solution.py:91
  3.2 7.3 %all-to-all-start = ((bf16[8,32,2176]{2,1,0:T(8,128)(2,1)}), bf16[8,32,2176]{2,1,0:T(8,128)(2,1)S(1)}, u32[]{:S(2)}, u32[]{:S(2)}) async-start(bf16[8,32,2176]{2,1,0:T(8,128)(2,1)} %bitcast.23), calls=%async_computation | async-start | bytes 2228224 | tf_op jit(solution)/shard_map/all_to_all | solution.py:679
  10.5 1.3 %slice_bitcast_fusion = (bf16[4,256,256]{2,1,0:T(8,128)(2,1)S(1)}, bf16[4,256,256]{2,1,0:T(8,128)(2,1)S(1)}) fusion(bf16[1,32,256,256]{3,2,1,0:T(8,128)(2,1)} %movie.3), kind=kLoop, calls=%fused_computation.1 | loop fusion | bytes 2097152 | tf_op jit(solution)/shard_map/squeeze | solution.py:680
  11.8 1.3 %collective-permute-start = (bf16[4,256,256]{2,1,0:T(8,128)(2,1)S(1)}, bf16[4,256,256]{2,1,0:T(8,128)(2,1)S(1)}, u32[]{:S(2)}, u32[]{:S(2)}) collective-permute-start(bf16[4,256,256]{2,1,0:T(8,128)(2,1)S(1)} %get-tuple-element.65), channel_id=1, source_target_pairs={{4,0},{8,4},{12,8},{16,12},{20,16},{24,20},{28,24},{5,1},{9,5},{13... | collective-permute-start | bytes 1572872 | tf_op jit(solution)/shard_map/ppermute | solution.py:676
  13.1 4.6 %collective-permute-start.1 = (bf16[4,256,256]{2,1,0:T(8,128)(2,1)S(1)}, bf16[4,256,256]{2,1,0:T(8,128)(2,1)S(1)}, u32[]{:S(2)}, u32[]{:S(2)}) collective-permute-start(bf16[4,256,256]{2,1,0:T(8,128)(2,1)S(1)} %get-tuple-element.64), channel_id=1, source_target_pairs={{0,4},{4,8},{8,12},{12,16},{16,20},{20,24},{24,28},{1,5},{5,9},{9,... | collective-permute-start | bytes 1572872 | tf_op jit(solution)/shard_map/ppermute | solution.py:676
  17.7 21.5 %all-to-all-done = bf16[8,32,2176]{2,1,0:T(8,128)(2,1)S(1)} async-done(((bf16[8,32,2176]{2,1,0:T(8,128)(2,1)}), bf16[8,32,2176]{2,1,0:T(8,128)(2,1)S(1)}, u32[]{:S(2)}, u32[]{:S(2)}) %all-to-all-start) | async-done | bytes 1114144 | tf_op jit(solution)/shard_map/all_to_all | solution.py:679
  39.2 4.5 %residual.2 = (bf16[32,256,256]{2,1,0:T(8,128)(2,1)S(1)}, bf16[32,256,256]{2,1,0:T(8,128)(2,1)}, f32[2,4,256]{2,1,0:T(4,128)S(1)}, bf16[4,256,256]{2,1,0:T(8,128)(2,1)S(1)}, bf16[4,256,256]{2,1,0:T(8,128)(2,1)S(1)}) custom-call(bf16[256,2176]{1,0:T(8,128)(2,1)S(1)} %bitcast.15, bf16[1,32,256,256]{3,2,1,0:T(8,128)(2,1)} %movie.3), custom_call_target="tpu_custom_call" | custom-call | flops 1 | bytes 1 | tf_op jit(solution)/shard_map/residual/pallas_call | solution.py:243
  43.7 1.9 %collective-permute-start.6 = (bf16[4,256,256]{2,1,0:T(8,128)(2,1)S(1)}, bf16[4,256,256]{2,1,0:T(8,128)(2,1)S(1)}, u32[]{:S(2)}, u32[]{:S(2)}) collective-permute-start(bf16[4,256,256]{2,1,0:T(8,128)(2,1)S(1)} %get-tuple-element.51), channel_id=1, source_target_pairs={{0,4},{4,8},{8,12},{12,16},{16,20},{20,24},{24,28},{1,5},{5,9},{9,... | collective-permute-start | bytes 1572872 | tf_op jit(solution)/shard_map/ppermute | solution.py:676
  45.6 1.3 %collective-permute-start.7 = (bf16[4,256,256]{2,1,0:T(8,128)(2,1)S(1)}, bf16[4,256,256]{2,1,0:T(8,128)(2,1)S(1)}, u32[]{:S(2)}, u32[]{:S(2)}) collective-permute-start(bf16[4,256,256]{2,1,0:T(8,128)(2,1)S(1)} %get-tuple-element.52), channel_id=1, source_target_pairs={{4,0},{8,4},{12,8},{16,12},{20,16},{24,20},{28,24},{5,1},{9,5},{13... | collective-permute-start | bytes 1572872 | tf_op jit(solution)/shard_map/ppermute | solution.py:676
  46.9 9.8 %residual.3 = (bf16[32,256,256]{2,1,0:T(8,128)(2,1)S(1)}, bf16[32,256,256]{2,1,0:T(8,128)(2,1)}, f32[6,4,256]{2,1,0:T(4,128)S(1)}, bf16[4,256,256]{2,1,0:T(8,128)(2,1)S(1)}, bf16[4,256,256]{2,1,0:T(8,128)(2,1)S(1)}) custom-call(bf16[256,2176]{1,0:T(8,128)(2,1)S(1)} %bitcast.16, ...), custom_call_target="tpu_custom_call", output_to_operand_aliasing={{0}: (2, {}), {1}: (3, {})} | custom-call | flops 1 | bytes 1 | tf_op jit(solution)/shard_map/residual/pallas_call | solution.py:243
  56.7 0.0 copy-start
  56.7 0.0 copy-start.2
  56.7 0.0 collective-permute-done.movie_next
  56.7 0.0 collective-permute-done.1.movie_prev
  56.7 1.9 %near.1 = (bf16[8,256,256]{2,1,0:T(8,128)(2,1)S(1)}, bf16[8,256,256]{2,1,0:T(8,128)(2,1)S(1)}, f32[40,256]{1,0:T(8,128)S(1)}) custom-call(bf16[256,2176]{1,0:T(8,128)(2,1)S(1)} %bitcast.17, bf16[4,256,256]{2,1,0:T(8,128)(2,1)S(1)} %collective-permute-done.movie_next, bf16[4,256,256]{2,1,0:T(8,128)(2,1)S(1)} %collective-permute-done.1.movie_prev, ...), custom_call_target="tpu_custom_call" | custom-call | flops 1 | bytes 1 | tf_op jit(solution)/shard_map/near/pallas_call | solution.py:294
  58.6 4.6 %collective-permute-start.2 = (bf16[4,256,256]{2,1,0:T(8,128)(2,1)S(1)}, bf16[4,256,256]{2,1,0:T(8,128)(2,1)S(1)}, u32[]{:S(2)}, u32[]{:S(2)}) collective-permute-start(bf16[4,256,256]{2,1,0:T(8,128)(2,1)S(1)} %get-tuple-element.43), channel_id=1, source_target_pairs={{0,4},{4,8},{8,12},{12,16},{16,20},{20,24},{24,28},{1,5},{5,9},{9,... | collective-permute-start | bytes 1572872 | tf_op jit(solution)/shard_map/ppermute | solution.py:676
  63.2 1.3 %collective-permute-start.3 = (bf16[4,256,256]{2,1,0:T(8,128)(2,1)S(1)}, bf16[4,256,256]{2,1,0:T(8,128)(2,1)S(1)}, u32[]{:S(2)}, u32[]{:S(2)}) collective-permute-start(bf16[4,256,256]{2,1,0:T(8,128)(2,1)S(1)} %get-tuple-element.44), channel_id=1, source_target_pairs={{4,0},{8,4},{12,8},{16,12},{20,16},{24,20},{28,24},{5,1},{9,5},{13... | collective-permute-start | bytes 1572872 | tf_op jit(solution)/shard_map/ppermute | solution.py:676
  64.5 1.3 %collective-permute-start.4 = (f32[40,256]{1,0:T(8,128)S(1)}, f32[40,256]{1,0:T(8,128)S(1)}, u32[]{:S(2)}, u32[]{:S(2)}) collective-permute-start(f32[40,256]{1,0:T(8,128)S(1)} %get-tuple-element.47.noise), channel_id=1, source_target_pairs={{0,1},{1,2},{2,3},{4,5},{5,6},{6,7},{8,9},{9,10},{10,11},{12,13},{... | collective-permute-start | bytes 122888 | tf_op jit(solution)/shard_map/ppermute | solution.py:693
  65.8 0.9 collective-permute-done.4.noise_before
  66.7 1.5 %collective-permute-start.5 = (f32[40,256]{1,0:T(8,128)S(1)}, f32[40,256]{1,0:T(8,128)S(1)}, u32[]{:S(2)}, u32[]{:S(2)}) collective-permute-start(f32[40,256]{1,0:T(8,128)S(1)} %get-tuple-element.47.noise), channel_id=1, source_target_pairs={{1,0},{2,1},{3,2},{5,4},{6,5},{7,6},{9,8},{10,9},{11,10},{13,12},{... | collective-permute-start | bytes 122888 | tf_op jit(solution)/shard_map/ppermute | solution.py:694
  68.1 3.6 %collective-permute-done.5.noise_after = f32[40,256]{1,0:T(8,128)S(1)} collective-permute-done((f32[40,256]{1,0:T(8,128)S(1)}, f32[40,256]{1,0:T(8,128)S(1)}, u32[]{:S(2)}, u32[]{:S(2)}) %collective-permute-start.5) | collective-permute-done | bytes 40992 | tf_op jit(solution)/shard_map/ppermute | solution.py:694
  71.7 5.2 %weights.1 = (bf16[32,256,256]{2,1,0:T(8,128)(2,1)S(1)}, bf16[3,256,256]{2,1,0:T(8,128)(2,1)S(1)}, bf16[3,256,256]{2,1,0:T(8,128)(2,1)S(1)}) custom-call(bf16[32,256,256]{2,1,0:T(8,128)(2,1)S(1)} %get-tuple-element.45.own, bf16[8,256,256]{2,1,0:T(8,128)(2,1)S(1)} %get-tuple-element.46.near, f32[40,256]{1,0:T(8,128)S(1)} %get-tuple-element.47.noise, ...), custom_call_target="tpu_custom_call" | custom-call | flops 1 | bytes 1 | tf_op jit(solution)/shard_map/weights/pallas_call | solution.py:372
  77.0 0.0 copy-done
  77.0 0.0 copy-done.2
  77.0 3.9 %annulus_middle.1 = (bf16[1,32,256,256]{3,2,1,0:T(8,128)(2,1)}, f32[256,256]{1,0:T(8,128)S(1)}, f32[256,256]{1,0:T(8,128)S(1)}, f32[256,256]{1,0:T(8,128)S(1)}) custom-call(bf16[32,256,256]{2,1,0:T(8,128)(2,1)S(1)} %copy-done, bf16[8,256,256]{2,1,0:T(8,128)(2,1)S(1)} %get-tuple-element.53.near, bf16[32,256,256]{2,1,0:T(8,128)(2,1)S(1)} %get-tuple-element.48.weight, ...), custom_call_target="tpu_custom_call" | custom-call | flops 1 | bytes 1 | tf_op jit(solution)/shard_map/annulus_middle/pallas_call | solution.py:563
  80.8 0.0 collective-permute-done.6.above
  80.9 0.0 collective-permute-done.7.below
  80.9 2.4 %annulus_mid.1 = (bf16[1,32,256,256]{3,2,1,0:T(8,128)(2,1)}, f32[256,256]{1,0:T(8,128)S(1)}, f32[256,256]{1,0:T(8,128)S(1)}, f32[256,256]{1,0:T(8,128)S(1)}) custom-call(bf16[32,256,256]{2,1,0:T(8,128)(2,1)S(1)} %copy-done, bf16[4,256,256]{2,1,0:T(8,128)(2,1)S(1)} %collective-permute-done.6.above, ...), custom_call_target="tpu_custom_call", output_to_operand_aliasing={{0}: (5, {})} | custom-call | flops 1073741824 | bytes 5242880 | tf_op jit(solution)/shard_map/annulus_mid/pallas_call | solution.py:563
  83.3 6.8 %collective-permute-done.2.above = bf16[4,256,256]{2,1,0:T(8,128)(2,1)S(1)} collective-permute-done((bf16[4,256,256]{2,1,0:T(8,128)(2,1)S(1)}, bf16[4,256,256]{2,1,0:T(8,128)(2,1)S(1)}, u32[]{:S(2)}, u32[]{:S(2)}) %collective-permute-start.2) | collective-permute-done | bytes 524320 | tf_op jit(solution)/shard_map/ppermute | solution.py:676
  90.0 0.0 collective-permute-done.3.below
  90.0 0.0 copy-start.6
  90.0 0.0 copy-start.1
  90.0 0.0 copy-start.3
  90.0 0.0 copy-start.4
  90.1 0.0 copy-start.5
  90.1 3.2 %annulus_end.1 = (bf16[1,32,256,256]{3,2,1,0:T(8,128)(2,1)}, bf16[256,1024]{1,0:T(8,128)(2,1)}) custom-call(bf16[32,256,256]{2,1,0:T(8,128)(2,1)S(1)} %copy-done, bf16[4,256,256]{2,1,0:T(8,128)(2,1)S(1)} %collective-permute-done.2.above, bf16[4,256,256]{2,1,0:T(8,128)(2,1)S(1)} %collective-permute-done.3.below, ...), custom_call_target="tpu_custom_call", output_to_operand_aliasing={{0}: (7, {})} | custom-call | flops 1 | bytes 1 | tf_op jit(solution)/shard_map/annulus_end/pallas_call | solution.py:563
  93.3 6.7 %all-to-all-start.1 = ((bf16[8,32,1024]{2,1,0:T(8,128)(2,1)}), bf16[8,32,1024]{2,1,0:T(8,128)(2,1)S(1)}, u32[]{:S(2)}, u32[]{:S(2)}) async-start(bf16[8,32,1024]{2,1,0:T(8,128)(2,1)} %bitcast.8), calls=%async_computation.1 | async-start | bytes 1048576 | tf_op jit(solution)/shard_map/all_to_all | solution.py:700
  100.0 0.0 copy-done.6
  100.0 0.1 multiply_reduce_fusion
  100.1 14.5 %all-to-all-done.1 = bf16[8,32,1024]{2,1,0:T(8,128)(2,1)S(1)} async-done(((bf16[8,32,1024]{2,1,0:T(8,128)(2,1)}), bf16[8,32,1024]{2,1,0:T(8,128)(2,1)S(1)}, u32[]{:S(2)}, u32[]{:S(2)}) %all-to-all-start.1) | async-done | bytes 524320 | tf_op jit(solution)/shard_map/all_to_all | solution.py:700
  114.7 0.0 copy-done.1
  114.7 0.0 copy-done.3
  114.7 0.0 copy-done.4
  114.7 0.0 copy-done.5
  114.7 1.7 %traces.1 = f32[128,256]{1,0:T(8,128)} custom-call(s32[1,128]{1,0:T(1,128)S(1)} %bitcast.22, f32[1,128]{1,0:T(1,128)S(1)} %copy-done.4, f32[1,128]{1,0:T(1,128)S(1)} %copy-done.5, f32[1,128]{1,0:T(1,128)S(1)} %divide_bitcast_fusion.step, bf16[128,256]{1,0:T(8,128)(2,1)S(1)} %bitcast.20, bf16[256,1024]{1,0:T(8,128)(2,1)S(1)} %bitcast.18), custom_call_target="tpu_custom_call" | custom-call | flops 1 | bytes 1 | tf_op jit(solution)/shard_map/traces/pallas_call | solution.py:649
  (1 shorter events, 0.0 us)
Async XLA Ops:
  3.2 35.9 %all-to-all-start = ((bf16[8,32,2176]{2,1,0:T(8,128)(2,1)}), bf16[8,32,2176]{2,1,0:T(8,128)(2,1)S(1)}, u32[]{:S(2)}, u32[]{:S(2)}) async-start(bf16[8,32,2176]{2,1,0:T(8,128)(2,1)} %bitcast.23), calls=%async_computation | async-start | bytes 2228224 | tf_op jit(solution)/shard_map/all_to_all | solution.py:679
  11.8 44.9 %collective-permute-start = (bf16[4,256,256]{2,1,0:T(8,128)(2,1)S(1)}, bf16[4,256,256]{2,1,0:T(8,128)(2,1)S(1)}, u32[]{:S(2)}, u32[]{:S(2)}) collective-permute-start(bf16[4,256,256]{2,1,0:T(8,128)(2,1)S(1)} %get-tuple-element.65), channel_id=1, source_target_pairs={{4,0},{8,4},{12,8},{16,12},{20,16},{24,20},{28,24},{5,1},{9,5},{13... | collective-permute-start | bytes 1572872 | tf_op jit(solution)/shard_map/ppermute | solution.py:676
  13.1 43.6 %collective-permute-start.1 = (bf16[4,256,256]{2,1,0:T(8,128)(2,1)S(1)}, bf16[4,256,256]{2,1,0:T(8,128)(2,1)S(1)}, u32[]{:S(2)}, u32[]{:S(2)}) collective-permute-start(bf16[4,256,256]{2,1,0:T(8,128)(2,1)S(1)} %get-tuple-element.64), channel_id=1, source_target_pairs={{0,4},{4,8},{8,12},{12,16},{16,20},{20,24},{24,28},{1,5},{5,9},{9,... | collective-permute-start | bytes 1572872 | tf_op jit(solution)/shard_map/ppermute | solution.py:676
  43.7 37.2 %collective-permute-start.6 = (bf16[4,256,256]{2,1,0:T(8,128)(2,1)S(1)}, bf16[4,256,256]{2,1,0:T(8,128)(2,1)S(1)}, u32[]{:S(2)}, u32[]{:S(2)}) collective-permute-start(bf16[4,256,256]{2,1,0:T(8,128)(2,1)S(1)} %get-tuple-element.51), channel_id=1, source_target_pairs={{0,4},{4,8},{8,12},{12,16},{16,20},{20,24},{24,28},{1,5},{5,9},{9,... | collective-permute-start | bytes 1572872 | tf_op jit(solution)/shard_map/ppermute | solution.py:676
  45.6 35.3 %collective-permute-start.7 = (bf16[4,256,256]{2,1,0:T(8,128)(2,1)S(1)}, bf16[4,256,256]{2,1,0:T(8,128)(2,1)S(1)}, u32[]{:S(2)}, u32[]{:S(2)}) collective-permute-start(bf16[4,256,256]{2,1,0:T(8,128)(2,1)S(1)} %get-tuple-element.52), channel_id=1, source_target_pairs={{4,0},{8,4},{12,8},{16,12},{20,16},{24,20},{28,24},{5,1},{9,5},{13... | collective-permute-start | bytes 1572872 | tf_op jit(solution)/shard_map/ppermute | solution.py:676
  56.7 20.3 %copy-start = (bf16[32,256,256]{2,1,0:T(8,128)(2,1)S(1)}, bf16[32,256,256]{2,1,0:T(8,128)(2,1)}, u32[]{:S(2)}) copy-start(bf16[32,256,256]{2,1,0:T(8,128)(2,1)} %get-tuple-element.37.own) | copy-start | bytes 12582916
  56.7 20.3 %copy-start.2 = (f32[1,256]{1,0:T(1,128)S(1)}, f32[1,256]{1,0:T(1,128)}, u32[]{:S(2)}) copy-start(f32[1,256]{1,0:T(1,128)} %gain.5) | copy-start | bytes 3076
  58.6 31.4 %collective-permute-start.2 = (bf16[4,256,256]{2,1,0:T(8,128)(2,1)S(1)}, bf16[4,256,256]{2,1,0:T(8,128)(2,1)S(1)}, u32[]{:S(2)}, u32[]{:S(2)}) collective-permute-start(bf16[4,256,256]{2,1,0:T(8,128)(2,1)S(1)} %get-tuple-element.43), channel_id=1, source_target_pairs={{0,4},{4,8},{8,12},{12,16},{16,20},{20,24},{24,28},{1,5},{5,9},{9,... | collective-permute-start | bytes 1572872 | tf_op jit(solution)/shard_map/ppermute | solution.py:676
  63.2 26.8 %collective-permute-start.3 = (bf16[4,256,256]{2,1,0:T(8,128)(2,1)S(1)}, bf16[4,256,256]{2,1,0:T(8,128)(2,1)S(1)}, u32[]{:S(2)}, u32[]{:S(2)}) collective-permute-start(bf16[4,256,256]{2,1,0:T(8,128)(2,1)S(1)} %get-tuple-element.44), channel_id=1, source_target_pairs={{4,0},{8,4},{12,8},{16,12},{20,16},{24,20},{28,24},{5,1},{9,5},{13... | collective-permute-start | bytes 1572872 | tf_op jit(solution)/shard_map/ppermute | solution.py:676
  64.5 2.2 %collective-permute-start.4 = (f32[40,256]{1,0:T(8,128)S(1)}, f32[40,256]{1,0:T(8,128)S(1)}, u32[]{:S(2)}, u32[]{:S(2)}) collective-permute-start(f32[40,256]{1,0:T(8,128)S(1)} %get-tuple-element.47.noise), channel_id=1, source_target_pairs={{0,1},{1,2},{2,3},{4,5},{5,6},{6,7},{8,9},{9,10},{10,11},{12,13},{... | collective-permute-start | bytes 122888 | tf_op jit(solution)/shard_map/ppermute | solution.py:693
  66.7 5.1 %collective-permute-start.5 = (f32[40,256]{1,0:T(8,128)S(1)}, f32[40,256]{1,0:T(8,128)S(1)}, u32[]{:S(2)}, u32[]{:S(2)}) collective-permute-start(f32[40,256]{1,0:T(8,128)S(1)} %get-tuple-element.47.noise), channel_id=1, source_target_pairs={{1,0},{2,1},{3,2},{5,4},{6,5},{7,6},{9,8},{10,9},{11,10},{13,12},{... | collective-permute-start | bytes 122888 | tf_op jit(solution)/shard_map/ppermute | solution.py:694
  90.0 10.0 %copy-start.6 = (bf16[1,128,1024]{2,1,0:T(8,128)(2,1)S(1)}, bf16[1,128,1024]{2,1,0:T(8,128)(2,1)}, u32[]{:S(2)}) copy-start(bf16[1,128,1024]{2,1,0:T(8,128)(2,1)} %param.9) | copy-start | bytes 786436
  90.0 24.6 %copy-start.1 = (bf16[1,128,256]{2,1,0:T(8,128)(2,1)S(1)}, bf16[1,128,256]{2,1,0:T(8,128)(2,1)}, u32[]{:S(2)}) copy-start(bf16[1,128,256]{2,1,0:T(8,128)(2,1)} %param.10) | copy-start | bytes 196612
  90.0 24.6 %copy-start.3 = (s32[1,128,1]{1,2,0:T(1,128)S(1)}, s32[1,128,1]{1,2,0:T(1,128)}, u32[]{:S(2)}) copy-start(s32[1,128,1]{1,2,0:T(1,128)} %param.11) | copy-start | bytes 1540
  90.0 24.6 %copy-start.4 = (f32[1,128]{1,0:T(1,128)S(1)}, f32[1,128]{1,0:T(1,128)}, u32[]{:S(2)}) copy-start(f32[1,128]{1,0:T(1,128)} %slow.1) | copy-start | bytes 1540
  90.1 24.6 %copy-start.5 = (f32[1,128]{1,0:T(1,128)S(1)}, f32[1,128]{1,0:T(1,128)}, u32[]{:S(2)}) copy-start(f32[1,128]{1,0:T(1,128)} %fast.1) | copy-start | bytes 1540
  93.3 21.4 %all-to-all-start.1 = ((bf16[8,32,1024]{2,1,0:T(8,128)(2,1)}), bf16[8,32,1024]{2,1,0:T(8,128)(2,1)S(1)}, u32[]{:S(2)}, u32[]{:S(2)}) async-start(bf16[8,32,1024]{2,1,0:T(8,128)(2,1)} %bitcast.8), calls=%async_computation.1 | async-start | bytes 1048576 | tf_op jit(solution)/shard_map/all_to_all | solution.py:700
where the time goes:
time: 117 us; the launch traced here: 116 us
  waiting for transfers between devices  47.2 us (40%)
  Pallas kernels  35.2 us (30%)
  starting transfers between devices  31.7 us (27%)
  local copies, waits for them, and re-layouts  1.3 us (1%)
    all_to_all x1, waiting for transfers between devices, on_device(): lax.all_to_all(outbox, 'pix', split_axis=0, concat_axis=0, tiled=True)  21.5 us
    all_to_all x1, waiting for transfers between devices, on_device(): lax.all_to_all(gradient, 'pix', split_axis=0, concat_axis=0, tiled=True)  14.5 us
    pallas_call x2, Pallas kernels, make_residual(): pl.pallas_call(functools.partial(residual_kernel, pick, low, high, earlie...  14.3 us
    ppermute x3, starting transfers between devices, exchange(): lax.ppermute(up, 'pix', pix_up)  11.1 us
    pallas_call x3, Pallas kernels, call(): pl.pallas_call(kernel, in_specs=specs, out_specs=[HBM] + [VMEM] * (len(ou...  9.44 us
    all_to_all x1, starting transfers between devices, on_device(): lax.all_to_all(outbox, 'pix', split_axis=0, concat_axis=0, tiled=True)  7.29 us
    ppermute x3, waiting for transfers between devices, exchange(): lax.ppermute(up, 'pix', pix_up)  6.76 us
    all_to_all x1, starting transfers between devices, on_device(): lax.all_to_all(gradient, 'pix', split_axis=0, concat_axis=0, tiled=True)  6.73 us
  transfers between devices with their start and end apart: 10, of which 5 were waited for; matrix products, arithmetic and copies ran while one was open for 1% of the time, Pallas kernels for 24%

commit v1 on v0

--- a/solution.py
+++ b/solution.py
@@ -53,7 +53,7 @@
     ]
     for copy in copies:
         copy.start()
-    for copy in copies:
+    for copy in copies[0:2]:
         copy.wait()
     stripe, column, foot, traces = places
     slots = outbox.shape[0]
@@ -72,10 +72,15 @@
     edge = NEAR * FOOT
     lefts = jnp.zeros((slots, LANES), F32)
     at = 3 * frames
-    for k, (shift, first, width) in enumerate(
-        ((0, 0, tiles), (capacity, 0, edge), (-capacity, tiles - edge, edge))
+    hots = [
+        jnp.where(place + shift == slot, 1.0, 0.0).astype(BF16)
+        for shift in (0, capacity, -capacity)
+    ]
+    for copy in copies[2:]:
+        copy.wait()
+    for k, (hot, first, width) in enumerate(
+        zip(hots, (0, 0, tiles - edge), (tiles, edge, edge))
     ):
-        hot = jnp.where(place + shift == slot, 1.0, 0.0).astype(BF16)
         outbox[:, k * frames : (k + 1) * frames] = dot(hot, traces[...]).astype(BF16)
         outbox[:, at : at + width] = dot(hot, foot[:, first : first + width]).astype(BF16)
         lefts = jnp.where(lane == k, dot(hot, left), lefts)
@@ -389,10 +394,11 @@
     )(foot_rows, near_rows, *noises)
 
 
-def annulus_group(g, own, leaving, entering, gain, band, column, outgoing):
+def annulus_group(g, own, leaving, entering, gain, band, column, outgoing, slot=None):
     cols, frames = own.shape[1:]
     top = lax.broadcasted_iota(jnp.int32, (cols // 8, 8, LANES), 1) < 4
     blank = jnp.zeros((2, 8, LANES), F32)
+    slot = g if slot is None else slot
     outs = [leaving(q) for q in range(PER)]
     news = [entering(q) for q in range(PER)]
     levels = [dot(band, jnp.concatenate([o, n], axis=0)) for o, n in zip(outs, news)]
@@ -409,7 +415,7 @@
             both = turned[0 : cols // 8 + 1] + turned[3 : cols // 8 + 4]
             sides = jnp.where(top, both[0 : cols // 8], both[1 : cols // 8 + 1])
             fit = (levels[q][:, part] + sides.reshape(cols, LANES)) * gain
-            outgoing[g, q, :, part] = fit.astype(BF16)
+            outgoing[slot, q, :, part] = fit.astype(BF16)
             det.append((own[g * PER + q, :, part].astype(F32) - fit).astype(BF16))
         dets.append(jnp.concatenate(det, axis=1))
     return column, dets
@@ -514,25 +520,21 @@
 
 
 def end_kernel(
-    own, above, below, weight, weight_next, weight_prev, gain, before,
-    upper, lower, total, background, gradient, outgoing, sems,
+    own, above, below, weight, weight_next, weight_prev, gain, upper, lower, total,
+    gradient, late,
 ):
-    del before
     rows, _, frames = own.shape
     low, high = 0, rows // PER - 1
     z = high * PER
-    send = sender(outgoing, background, sems)
     gains, band = tables(gain)
     _, low_dets = annulus_group(
         low, own, lambda q: above[q], lambda q: own[RAD + q], gains, band,
-        add_rows(halves(upper), [above[r] for r in range(PER)]), outgoing,
-    )
-    send(low).start()
+        add_rows(halves(upper), [above[r] for r in range(PER)]), late, 0,
+    )
     _, high_dets = annulus_group(
         high, own, lambda q: own[z - RAD + q], lambda q: below[q], gains, band, halves(lower),
-        outgoing,
-    )
-    send(high).start()
+        late, 1,
+    )
     grown = grow(grow(total[...], weight, low, low_dets), weight, high, high_dets)
     edges = ((2, weight_next, high_dets[PER - GR :]), (3, weight_prev, low_dets[:GR]))
     for at, edge, parts in edges:
@@ -543,8 +545,19 @@
     coarse = grown.astype(BF16)
     gradient[:, 0:frames] = coarse
     gradient[:, frames : 2 * frames] = (grown - coarse.astype(F32)).astype(BF16)
-    send(low).wait()
-    send(high).wait()
+
+
+def late_kernel(late, before, background, sems):
+    del before
+    rows = background.shape[1]
+    copies = [
+        pltpu.make_async_copy(late.at[k], background.at[0, pl.ds(first, PER)], sems.at[k])
+        for k, first in enumerate((0, rows - PER))
+    ]
+    for copy in copies:
+        copy.start()
+    for copy in copies:
+        copy.wait()
 
 
 def make_annulus(own, near, mid, far, weights, gain):
@@ -587,16 +600,33 @@
             flops=2 * rows * cols * cols * frames, bytes_accessed=5 * MIB, transcendentals=0
         ),
     )
-    return call(
-        end_kernel, "annulus_end",
-        (own, *far, weight, weight_next, weight_prev, gain, done, upper, lower, grown),
-        (background, gradient), 7,
-    )
-
-
-def traces_kernel(capacity, stripe, slow, fast, step, traces, inbox, out):
-    count, frames = traces.shape
-    slots = inbox.shape[0]
+    args = (own, *far, weight, weight_next, weight_prev, gain, upper, lower, grown)
+    gradient, late = pl.pallas_call(
+        end_kernel,
+        in_specs=[VMEM] * len(args),
+        out_shape=(gradient, jax.ShapeDtypeStruct((2, PER, cols, frames), BF16)),
+        compiler_params=params(),
+        cost_estimate=COST,
+        name="annulus_end",
+    )(*args)
+    background = pl.pallas_call(
+        late_kernel,
+        in_specs=[VMEM, HBM],
+        out_specs=HBM,
+        out_shape=background,
+        scratch_shapes=[pltpu.SemaphoreType.DMA((2,))],
+        input_output_aliases={1: 0},
+        compiler_params=params(),
+        cost_estimate=COST,
+        name="late_rows",
+    )(late, done)
+    return background, gradient
+
+
+def prepare_kernel(capacity, stripe, slow, fast, step, hots, tables):
+    count = stripe.shape[1]
+    frames = tables.shape[2]
+    slots = hots.shape[1] // 4
 
     def upended(row):
         return jnp.broadcast_to(row[...].astype(F32), (LANES, count)).T
@@ -609,28 +639,40 @@
     rank = jnp.sum(jnp.where(same, 1.0, 0.0), axis=1, keepdims=True)
     slot = (named[:, 0:1] * capacity + rank).astype(jnp.int32)
     place = lax.broadcasted_iota(jnp.int32, (count, slots), 1)
-
-    def onehot(shift):
-        return jnp.where(place + shift == slot, 1.0, 0.0).astype(BF16)
-
-    here = onehot(0)
-    gradient = (
-        dot(here, inbox[:, 0:frames])
-        + dot(here, inbox[:, frames : 2 * frames])
-        + dot(onehot(capacity), inbox[:, 2 * frames : 3 * frames])
-        + dot(onehot(-capacity), inbox[:, 3 * frames : 4 * frames])
-    )
-
-    def wide(row):
-        return jnp.concatenate([upended(row)] * (frames // LANES), axis=1)
-
-    updated = traces[...].astype(F32) + wide(step) * gradient
+    for k, shift in enumerate((0, 0, capacity, -capacity)):
+        hots[:, k * slots : (k + 1) * slots] = jnp.where(place + shift == slot, 1.0, 0.0).astype(
+            BF16
+        )
+    a, b = upended(slow), upended(fast)
+    for k, part in enumerate((upended(step), a, b, (1.0 - a) * (1.0 - b) / (a - b))):
+        tables[k] = jnp.concatenate([part] * (frames // LANES), axis=1)
+
+
+def prepare_traces(stripe, slow, fast, step, frames, slots, capacity):
+    count = stripe.shape[1]
+    return pl.pallas_call(
+        functools.partial(prepare_kernel, capacity),
+        out_shape=(
+            jax.ShapeDtypeStruct((count, 4 * slots), BF16),
+            jax.ShapeDtypeStruct((4, count, frames), F32),
+        ),
+        compiler_params=params(),
+        cost_estimate=COST,
+        name="prepare",
+    )(stripe, slow, fast, step)
+
+
+def traces_kernel(hots, tables, traces, inbox, out):
+    count, frames = traces.shape
+    parts = [inbox[:, k * frames : (k + 1) * frames] for k in range(4)]
+    gradient = dot(hots[...], jnp.concatenate(parts, axis=0))
+    updated = traces[...].astype(F32) + tables[0] * gradient
     lane = lax.broadcasted_iota(jnp.int32, (count, frames), 1)
 
     def lagged(value, lag):
         return jnp.where(lane >= lag, pltpu.roll(value, lag, 1), 0.0)
 
-    a, b = wide(slow), wide(fast)
+    a, b = tables[1], tables[2]
     driven = updated - (a + b) * lagged(updated, 1) + (a * b) * lagged(updated, 2)
     spikes = jnp.maximum(driven - lam_floor, 0.0)
     sums = [spikes, spikes]
@@ -640,19 +682,18 @@
         sums = [value + root * lagged(value, lag) for value, root in zip(sums, roots)]
         roots = [root * root for root in roots]
         lag *= 2
-    share = (1.0 - a) * (1.0 - b) / (a - b)
-    out[...] = share * (a * sums[0] - b * sums[1])
-
-
-def make_traces(stripe, slow, fast, step, traces, inbox, capacity):
+    out[...] = tables[3] * (a * sums[0] - b * sums[1])
+
+
+def make_traces(hots, tables, traces, inbox):
     count, frames = traces.shape
     return pl.pallas_call(
-        functools.partial(traces_kernel, capacity),
+        traces_kernel,
         out_shape=jax.ShapeDtypeStruct((count, frames), F32),
         compiler_params=params(),
         cost_estimate=COST,
         name="traces",
-    )(stripe, slow, fast, step, traces, inbox)
+    )(hots, tables, traces, inbox)
 
 
 def neighbours(axis):
@@ -686,23 +727,24 @@
     near_rows, near_residual, noise = make_near(
         inbox, near_next, near_prev, (mid_noise, other_noise)
     )
-    up, down, noise = lax.optimization_barrier((up, down, noise))
+    foot_f = footprints[0].astype(F32)
+    step = 1.0 / (jnp.sum(foot_f * foot_f, axis=1) + norm_eps)
+    step_row, up, down, noise = lax.optimization_barrier((step[None], up, down, noise))
     far = exchange(up, down)
     noises = (
         noise,
         lax.ppermute(noise, "plane", plane_up),
         lax.ppermute(noise, "plane", plane_down),
     )
+    hots, tables = prepare_traces(
+        stripe_row, decay_slow, decay_fast, step_row, frames, slots, capacity
+    )
     weights = make_weights(foot_rows, near_rows, noises)
     background, gradient = make_annulus(
         residual, near_residual, mid, far, weights, annulus_gain
     )
     home = lax.all_to_all(gradient, "pix", split_axis=0, concat_axis=0, tiled=True)
-    foot_f = footprints[0].astype(F32)
-    step = 1.0 / (jnp.sum(foot_f * foot_f, axis=1) + norm_eps)
-    traces_new = make_traces(
-        stripe_row, decay_slow, decay_fast, step[None], traces[0], home, capacity
-    )
+    traces_new = make_traces(hots, tables, traces[0], home)
     return (background, traces_new[None])
 
 

time: 117 us -> 116 us (level)
  waiting for transfers between devices: 47.2 us -> 45.6 us
    pallas_call x1 -> x4, Pallas kernels: 1.73 us -> 5.58 us  [the longest x1 2.74 us: make_annulus(): pl.pallas_call(end_kernel, in_specs=[VMEM] * len(args), out_shape=(gradie...]
    pallas_call x3 -> x2, Pallas kernels: 9.44 us -> 6.47 us  [call(): pl.pallas_call(kernel, in_specs=specs, out_specs=[HBM] + [VMEM] * (len(ou...]
    all_to_all x1, waiting for transfers between devices: 14.5 us -> 13.3 us  [on_device(): lax.all_to_all(gradient, 'pix', split_axis=0, concat_axis=0, tiled=True)]
  transfers between devices with their start and end apart: 10 -> 10, of which waited for: 5 -> 5; matrix products, arithmetic and copies ran while one was open for 1% -> 1% of each run, Pallas kernels for 24% -> 25%
where the time goes in v1:
time: 116 us
  waiting for transfers between devices  45.6 us (39%)
  Pallas kernels  36 us (31%)
  starting transfers between devices  31.7 us (27%)
  local copies, waits for them, and re-layouts  1.3 us (1%)
    all_to_all x1, waiting for transfers between devices, on_device(): lax.all_to_all(outbox, 'pix', split_axis=0, concat_axis=0, tiled=True)  21.3 us
    pallas_call x2, Pallas kernels, make_residual(): pl.pallas_call(functools.partial(residual_kernel, pick, low, high, earlie...  14.4 us
    all_to_all x1, waiting for transfers between devices, on_device(): lax.all_to_all(gradient, 'pix', split_axis=0, concat_axis=0, tiled=True)  13.3 us
    ppermute x3, starting transfers between devices, exchange(): lax.ppermute(up, 'pix', pix_up)  11.1 us
    all_to_all x1, starting transfers between devices, on_device(): lax.all_to_all(outbox, 'pix', split_axis=0, concat_axis=0, tiled=True)  7.29 us
    all_to_all x1, starting transfers between devices, on_device(): lax.all_to_all(gradient, 'pix', split_axis=0, concat_axis=0, tiled=True)  6.73 us
    ppermute x3, waiting for transfers between devices, exchange(): lax.ppermute(up, 'pix', pix_up)  6.52 us
    pallas_call x2, Pallas kernels, call(): pl.pallas_call(kernel, in_specs=specs, out_specs=[HBM] + [VMEM] * (len(ou...  6.47 us
  transfers between devices with their start and end apart: 10, of which 5 were waited for; matrix products, arithmetic and copies ran while one was open for 1% of the time, Pallas kernels for 25%

profile of v1, /device:TPU:0, one launch (start us, length us, event | category | flops | bytes accessed | tf_op | source)
XLA Modules:
  0.0 115.7 jit_solution(17278380918540384939)
XLA Ops:
  0.6 0.0 copy-start.6
  0.6 2.5 %outbox.1 = bf16[256,2176]{1,0:T(8,128)(2,1)} custom-call(s32[1,128]{1,0:T(1,128)} %bitcast.21, s32[1,128]{1,0:T(1,128)} %refs_1_.1, bf16[128,1024]{1,0:T(8,128)(2,1)} %bitcast.24, bf16[128,256]{1,0:T(8,128)(2,1)} %bitcast.19), custom_call_target="tpu_custom_call" | custom-call | flops 1 | bytes 1 | tf_op jit(solution)/shard_map/outbox/pallas_call | solution.py:96
  3.2 7.3 %all-to-all-start = ((bf16[8,32,2176]{2,1,0:T(8,128)(2,1)}), bf16[8,32,2176]{2,1,0:T(8,128)(2,1)S(1)}, u32[]{:S(2)}, u32[]{:S(2)}) async-start(bf16[8,32,2176]{2,1,0:T(8,128)(2,1)} %bitcast.23), calls=%async_computation | async-start | bytes 2228224 | tf_op jit(solution)/shard_map/all_to_all | solution.py:720
  10.5 1.3 %slice_bitcast_fusion = (bf16[4,256,256]{2,1,0:T(8,128)(2,1)S(1)}, bf16[4,256,256]{2,1,0:T(8,128)(2,1)S(1)}) fusion(bf16[1,32,256,256]{3,2,1,0:T(8,128)(2,1)} %movie.3), kind=kLoop, calls=%fused_computation | loop fusion | bytes 2097152 | tf_op jit(solution)/shard_map/squeeze | solution.py:721
  11.7 1.3 %collective-permute-start = (bf16[4,256,256]{2,1,0:T(8,128)(2,1)S(1)}, bf16[4,256,256]{2,1,0:T(8,128)(2,1)S(1)}, u32[]{:S(2)}, u32[]{:S(2)}) collective-permute-start(bf16[4,256,256]{2,1,0:T(8,128)(2,1)S(1)} %get-tuple-element.71), channel_id=1, source_target_pairs={{4,0},{8,4},{12,8},{16,12},{20,16},{24,20},{28,24},{5,1},{9,5},{13... | collective-permute-start | bytes 1572872 | tf_op jit(solution)/shard_map/ppermute | solution.py:717
  13.0 4.6 %collective-permute-start.1 = (bf16[4,256,256]{2,1,0:T(8,128)(2,1)S(1)}, bf16[4,256,256]{2,1,0:T(8,128)(2,1)S(1)}, u32[]{:S(2)}, u32[]{:S(2)}) collective-permute-start(bf16[4,256,256]{2,1,0:T(8,128)(2,1)S(1)} %get-tuple-element.70), channel_id=1, source_target_pairs={{0,4},{4,8},{8,12},{12,16},{16,20},{20,24},{24,28},{1,5},{5,9},{9,... | collective-permute-start | bytes 1572872 | tf_op jit(solution)/shard_map/ppermute | solution.py:717
  17.6 0.0 copy-done.6
  17.7 0.1 multiply_reduce_fusion
  17.8 21.3 %all-to-all-done = bf16[8,32,2176]{2,1,0:T(8,128)(2,1)S(1)} async-done(((bf16[8,32,2176]{2,1,0:T(8,128)(2,1)}), bf16[8,32,2176]{2,1,0:T(8,128)(2,1)S(1)}, u32[]{:S(2)}, u32[]{:S(2)}) %all-to-all-start) | async-done | bytes 1114144 | tf_op jit(solution)/shard_map/all_to_all | solution.py:720
  39.1 4.5 %residual.2 = (bf16[32,256,256]{2,1,0:T(8,128)(2,1)S(1)}, bf16[32,256,256]{2,1,0:T(8,128)(2,1)}, f32[2,4,256]{2,1,0:T(4,128)S(1)}, bf16[4,256,256]{2,1,0:T(8,128)(2,1)S(1)}, bf16[4,256,256]{2,1,0:T(8,128)(2,1)S(1)}) custom-call(bf16[256,2176]{1,0:T(8,128)(2,1)S(1)} %bitcast.15, bf16[1,32,256,256]{3,2,1,0:T(8,128)(2,1)} %movie.3), custom_call_target="tpu_custom_call" | custom-call | flops 1 | bytes 1 | tf_op jit(solution)/shard_map/residual/pallas_call | solution.py:248
  43.6 1.9 %collective-permute-start.6 = (bf16[4,256,256]{2,1,0:T(8,128)(2,1)S(1)}, bf16[4,256,256]{2,1,0:T(8,128)(2,1)S(1)}, u32[]{:S(2)}, u32[]{:S(2)}) collective-permute-start(bf16[4,256,256]{2,1,0:T(8,128)(2,1)S(1)} %get-tuple-element.54), channel_id=1, source_target_pairs={{0,4},{4,8},{8,12},{12,16},{16,20},{20,24},{24,28},{1,5},{5,9},{9,... | collective-permute-start | bytes 1572872 | tf_op jit(solution)/shard_map/ppermute | solution.py:717
  45.5 1.3 %collective-permute-start.7 = (bf16[4,256,256]{2,1,0:T(8,128)(2,1)S(1)}, bf16[4,256,256]{2,1,0:T(8,128)(2,1)S(1)}, u32[]{:S(2)}, u32[]{:S(2)}) collective-permute-start(bf16[4,256,256]{2,1,0:T(8,128)(2,1)S(1)} %get-tuple-element.55), channel_id=1, source_target_pairs={{4,0},{8,4},{12,8},{16,12},{20,16},{24,20},{28,24},{5,1},{9,5},{13... | collective-permute-start | bytes 1572872 | tf_op jit(solution)/shard_map/ppermute | solution.py:717
  46.9 9.9 %residual.3 = (bf16[32,256,256]{2,1,0:T(8,128)(2,1)S(1)}, bf16[32,256,256]{2,1,0:T(8,128)(2,1)}, f32[6,4,256]{2,1,0:T(4,128)S(1)}, bf16[4,256,256]{2,1,0:T(8,128)(2,1)S(1)}, bf16[4,256,256]{2,1,0:T(8,128)(2,1)S(1)}) custom-call(bf16[256,2176]{1,0:T(8,128)(2,1)S(1)} %bitcast.16, ...), custom_call_target="tpu_custom_call", output_to_operand_aliasing={{0}: (2, {}), {1}: (3, {})} | custom-call | flops 1 | bytes 1 | tf_op jit(solution)/shard_map/residual/pallas_call | solution.py:248
  56.7 0.0 copy-start
  56.7 0.0 copy-start.2
  56.7 0.0 collective-permute-done.movie_next
  56.8 0.0 collective-permute-done.1.movie_prev
  56.8 1.9 %near.1 = (bf16[8,256,256]{2,1,0:T(8,128)(2,1)S(1)}, bf16[8,256,256]{2,1,0:T(8,128)(2,1)S(1)}, f32[40,256]{1,0:T(8,128)S(1)}) custom-call(bf16[256,2176]{1,0:T(8,128)(2,1)S(1)} %bitcast.17, bf16[4,256,256]{2,1,0:T(8,128)(2,1)S(1)} %collective-permute-done.movie_next, bf16[4,256,256]{2,1,0:T(8,128)(2,1)S(1)} %collective-permute-done.1.movie_prev, ...), custom_call_target="tpu_custom_call" | custom-call | flops 1 | bytes 1 | tf_op jit(solution)/shard_map/near/pallas_call | solution.py:299
  58.7 4.6 %collective-permute-start.2 = (bf16[4,256,256]{2,1,0:T(8,128)(2,1)S(1)}, bf16[4,256,256]{2,1,0:T(8,128)(2,1)S(1)}, u32[]{:S(2)}, u32[]{:S(2)}) collective-permute-start(bf16[4,256,256]{2,1,0:T(8,128)(2,1)S(1)} %get-tuple-element.46), channel_id=1, source_target_pairs={{0,4},{4,8},{8,12},{12,16},{16,20},{20,24},{24,28},{1,5},{5,9},{9,... | collective-permute-start | bytes 1572872 | tf_op jit(solution)/shard_map/ppermute | solution.py:717
  63.3 1.3 %collective-permute-start.3 = (bf16[4,256,256]{2,1,0:T(8,128)(2,1)S(1)}, bf16[4,256,256]{2,1,0:T(8,128)(2,1)S(1)}, u32[]{:S(2)}, u32[]{:S(2)}) collective-permute-start(bf16[4,256,256]{2,1,0:T(8,128)(2,1)S(1)} %get-tuple-element.47), channel_id=1, source_target_pairs={{4,0},{8,4},{12,8},{16,12},{20,16},{24,20},{28,24},{5,1},{9,5},{13... | collective-permute-start | bytes 1572872 | tf_op jit(solution)/shard_map/ppermute | solution.py:717
  64.6 1.3 %collective-permute-start.4 = (f32[40,256]{1,0:T(8,128)S(1)}, f32[40,256]{1,0:T(8,128)S(1)}, u32[]{:S(2)}, u32[]{:S(2)}) collective-permute-start(f32[40,256]{1,0:T(8,128)S(1)} %get-tuple-element.50.noise), channel_id=1, source_target_pairs={{0,1},{1,2},{2,3},{4,5},{5,6},{6,7},{8,9},{9,10},{10,11},{12,13},{... | collective-permute-start | bytes 122888 | tf_op jit(solution)/shard_map/ppermute | solution.py:736
  65.9 0.9 collective-permute-done.4.noise_before
  66.7 1.5 %collective-permute-start.5 = (f32[40,256]{1,0:T(8,128)S(1)}, f32[40,256]{1,0:T(8,128)S(1)}, u32[]{:S(2)}, u32[]{:S(2)}) collective-permute-start(f32[40,256]{1,0:T(8,128)S(1)} %get-tuple-element.50.noise), channel_id=1, source_target_pairs={{1,0},{2,1},{3,2},{5,4},{6,5},{7,6},{9,8},{10,9},{11,10},{13,12},{... | collective-permute-start | bytes 122888 | tf_op jit(solution)/shard_map/ppermute | solution.py:737
  68.2 3.6 %collective-permute-done.5.noise_after = f32[40,256]{1,0:T(8,128)S(1)} collective-permute-done((f32[40,256]{1,0:T(8,128)S(1)}, f32[40,256]{1,0:T(8,128)S(1)}, u32[]{:S(2)}, u32[]{:S(2)}) %collective-permute-start.5) | collective-permute-done | bytes 40992 | tf_op jit(solution)/shard_map/ppermute | solution.py:737
  71.8 5.2 %weights.1 = (bf16[32,256,256]{2,1,0:T(8,128)(2,1)S(1)}, bf16[3,256,256]{2,1,0:T(8,128)(2,1)S(1)}, bf16[3,256,256]{2,1,0:T(8,128)(2,1)S(1)}) custom-call(bf16[32,256,256]{2,1,0:T(8,128)(2,1)S(1)} %get-tuple-element.48.own, bf16[8,256,256]{2,1,0:T(8,128)(2,1)S(1)} %get-tuple-element.49.near, f32[40,256]{1,0:T(8,128)S(1)} %get-tuple-element.50.noise, ...), custom_call_target="tpu_custom_call" | custom-call | flops 1 | bytes 1 | tf_op jit(solution)/shard_map/weights/pallas_call | solution.py:377
  76.9 0.0 copy-done
  76.9 0.0 copy-done.2
  77.0 4.0 %annulus_middle.1 = (bf16[1,32,256,256]{3,2,1,0:T(8,128)(2,1)}, f32[256,256]{1,0:T(8,128)S(1)}, f32[256,256]{1,0:T(8,128)S(1)}, f32[256,256]{1,0:T(8,128)S(1)}) custom-call(bf16[32,256,256]{2,1,0:T(8,128)(2,1)S(1)} %copy-done, bf16[8,256,256]{2,1,0:T(8,128)(2,1)S(1)} %get-tuple-element.56.near, bf16[32,256,256]{2,1,0:T(8,128)(2,1)S(1)} %get-tuple-element.51.weight, ...), custom_call_target="tpu_custom_call" | custom-call | flops 1 | bytes 1 | tf_op jit(solution)/shard_map/annulus_middle/pallas_call | solution.py:576
  81.0 0.0 collective-permute-done.6.above
  81.0 0.0 collective-permute-done.7.below
  81.0 2.4 %annulus_mid.1 = (bf16[1,32,256,256]{3,2,1,0:T(8,128)(2,1)}, f32[256,256]{1,0:T(8,128)S(1)}, f32[256,256]{1,0:T(8,128)S(1)}, f32[256,256]{1,0:T(8,128)S(1)}) custom-call(bf16[32,256,256]{2,1,0:T(8,128)(2,1)S(1)} %copy-done, bf16[4,256,256]{2,1,0:T(8,128)(2,1)S(1)} %collective-permute-done.6.above, ...), custom_call_target="tpu_custom_call", output_to_operand_aliasing={{0}: (5, {})} | custom-call | flops 1073741824 | bytes 5242880 | tf_op jit(solution)/shard_map/annulus_mid/pallas_call | solution.py:576
  83.5 6.5 %collective-permute-done.2.above = bf16[4,256,256]{2,1,0:T(8,128)(2,1)S(1)} collective-permute-done((bf16[4,256,256]{2,1,0:T(8,128)(2,1)S(1)}, bf16[4,256,256]{2,1,0:T(8,128)(2,1)S(1)}, u32[]{:S(2)}, u32[]{:S(2)}) %collective-permute-start.2) | collective-permute-done | bytes 524320 | tf_op jit(solution)/shard_map/ppermute | solution.py:717
  90.0 0.0 collective-permute-done.3.below
  90.0 0.0 copy-start.3
  90.0 0.0 copy-start.4
  90.0 0.0 copy-start.5
  90.0 2.7 %annulus_end.1 = (bf16[256,1024]{1,0:T(8,128)(2,1)}, bf16[2,4,256,256]{3,2,1,0:T(8,128)(2,1)S(1)}) custom-call(bf16[32,256,256]{2,1,0:T(8,128)(2,1)S(1)} %copy-done, bf16[4,256,256]{2,1,0:T(8,128)(2,1)S(1)} %collective-permute-done.2.above, bf16[4,256,256]{2,1,0:T(8,128)(2,1)S(1)} %collective-permute-done.3.below, ...), custom_call_target="tpu_custom_call" | custom-call | flops 1 | bytes 1 | tf_op jit(solution)/shard_map/annulus_end/pallas_call | solution.py:604
  92.7 6.7 %all-to-all-start.1 = ((bf16[8,32,1024]{2,1,0:T(8,128)(2,1)}), bf16[8,32,1024]{2,1,0:T(8,128)(2,1)S(1)}, u32[]{:S(2)}, u32[]{:S(2)}) async-start(bf16[8,32,1024]{2,1,0:T(8,128)(2,1)} %bitcast.8), calls=%async_computation.1 | async-start | bytes 1048576 | tf_op jit(solution)/shard_map/all_to_all | solution.py:746
  99.5 0.0 copy-done.3
  99.5 0.0 copy-done.4
  99.5 0.0 copy-done.5
  99.5 0.3 prepare.1
  99.8 0.0 copy-start.1
  99.8 1.0 late_rows.1
  100.8 13.3 %all-to-all-done.1 = bf16[8,32,1024]{2,1,0:T(8,128)(2,1)S(1)} async-done(((bf16[8,32,1024]{2,1,0:T(8,128)(2,1)}), bf16[8,32,1024]{2,1,0:T(8,128)(2,1)S(1)}, u32[]{:S(2)}, u32[]{:S(2)}) %all-to-all-start.1) | async-done | bytes 524320 | tf_op jit(solution)/shard_map/all_to_all | solution.py:746
  114.1 0.0 copy-done.1
  114.1 1.5 %traces.1 = f32[128,256]{1,0:T(8,128)} custom-call(bf16[128,1024]{1,0:T(8,128)(2,1)S(1)} %get-tuple-element.67.hots, f32[4,128,256]{2,1,0:T(8,128)S(1)} %get-tuple-element.68.tables, bf16[128,256]{1,0:T(8,128)(2,1)S(1)} %bitcast.20, bf16[256,1024]{1,0:T(8,128)(2,1)S(1)} %bitcast.18), custom_call_target="tpu_custom_call" | custom-call | flops 1 | bytes 1 | tf_op jit(solution)/shard_map/traces/pallas_call | solution.py:690
  (1 shorter events, 0.0 us)
Async XLA Ops:
  0.6 17.0 %copy-start.6 = (bf16[1,128,1024]{2,1,0:T(8,128)(2,1)S(1)}, bf16[1,128,1024]{2,1,0:T(8,128)(2,1)}, u32[]{:S(2)}) copy-start(bf16[1,128,1024]{2,1,0:T(8,128)(2,1)} %param.9) | copy-start | bytes 786436
  3.2 35.9 %all-to-all-start = ((bf16[8,32,2176]{2,1,0:T(8,128)(2,1)}), bf16[8,32,2176]{2,1,0:T(8,128)(2,1)S(1)}, u32[]{:S(2)}, u32[]{:S(2)}) async-start(bf16[8,32,2176]{2,1,0:T(8,128)(2,1)} %bitcast.23), calls=%async_computation | async-start | bytes 2228224 | tf_op jit(solution)/shard_map/all_to_all | solution.py:720
  11.7 45.0 %collective-permute-start = (bf16[4,256,256]{2,1,0:T(8,128)(2,1)S(1)}, bf16[4,256,256]{2,1,0:T(8,128)(2,1)S(1)}, u32[]{:S(2)}, u32[]{:S(2)}) collective-permute-start(bf16[4,256,256]{2,1,0:T(8,128)(2,1)S(1)} %get-tuple-element.71), channel_id=1, source_target_pairs={{4,0},{8,4},{12,8},{16,12},{20,16},{24,20},{28,24},{5,1},{9,5},{13... | collective-permute-start | bytes 1572872 | tf_op jit(solution)/shard_map/ppermute | solution.py:717
  13.0 43.7 %collective-permute-start.1 = (bf16[4,256,256]{2,1,0:T(8,128)(2,1)S(1)}, bf16[4,256,256]{2,1,0:T(8,128)(2,1)S(1)}, u32[]{:S(2)}, u32[]{:S(2)}) collective-permute-start(bf16[4,256,256]{2,1,0:T(8,128)(2,1)S(1)} %get-tuple-element.70), channel_id=1, source_target_pairs={{0,4},{4,8},{8,12},{12,16},{16,20},{20,24},{24,28},{1,5},{5,9},{9,... | collective-permute-start | bytes 1572872 | tf_op jit(solution)/shard_map/ppermute | solution.py:717
  43.6 37.4 %collective-permute-start.6 = (bf16[4,256,256]{2,1,0:T(8,128)(2,1)S(1)}, bf16[4,256,256]{2,1,0:T(8,128)(2,1)S(1)}, u32[]{:S(2)}, u32[]{:S(2)}) collective-permute-start(bf16[4,256,256]{2,1,0:T(8,128)(2,1)S(1)} %get-tuple-element.54), channel_id=1, source_target_pairs={{0,4},{4,8},{8,12},{12,16},{16,20},{20,24},{24,28},{1,5},{5,9},{9,... | collective-permute-start | bytes 1572872 | tf_op jit(solution)/shard_map/ppermute | solution.py:717
  45.5 35.5 %collective-permute-start.7 = (bf16[4,256,256]{2,1,0:T(8,128)(2,1)S(1)}, bf16[4,256,256]{2,1,0:T(8,128)(2,1)S(1)}, u32[]{:S(2)}, u32[]{:S(2)}) collective-permute-start(bf16[4,256,256]{2,1,0:T(8,128)(2,1)S(1)} %get-tuple-element.55), channel_id=1, source_target_pairs={{4,0},{8,4},{12,8},{16,12},{20,16},{24,20},{28,24},{5,1},{9,5},{13... | collective-permute-start | bytes 1572872 | tf_op jit(solution)/shard_map/ppermute | solution.py:717
  56.7 20.2 %copy-start = (bf16[32,256,256]{2,1,0:T(8,128)(2,1)S(1)}, bf16[32,256,256]{2,1,0:T(8,128)(2,1)}, u32[]{:S(2)}) copy-start(bf16[32,256,256]{2,1,0:T(8,128)(2,1)} %get-tuple-element.40.own) | copy-start | bytes 12582916
  56.7 20.2 %copy-start.2 = (f32[1,256]{1,0:T(1,128)S(1)}, f32[1,256]{1,0:T(1,128)}, u32[]{:S(2)}) copy-start(f32[1,256]{1,0:T(1,128)} %gain.5) | copy-start | bytes 3076
  58.7 31.3 %collective-permute-start.2 = (bf16[4,256,256]{2,1,0:T(8,128)(2,1)S(1)}, bf16[4,256,256]{2,1,0:T(8,128)(2,1)S(1)}, u32[]{:S(2)}, u32[]{:S(2)}) collective-permute-start(bf16[4,256,256]{2,1,0:T(8,128)(2,1)S(1)} %get-tuple-element.46), channel_id=1, source_target_pairs={{0,4},{4,8},{8,12},{12,16},{16,20},{20,24},{24,28},{1,5},{5,9},{9,... | collective-permute-start | bytes 1572872 | tf_op jit(solution)/shard_map/ppermute | solution.py:717
  63.3 26.7 %collective-permute-start.3 = (bf16[4,256,256]{2,1,0:T(8,128)(2,1)S(1)}, bf16[4,256,256]{2,1,0:T(8,128)(2,1)S(1)}, u32[]{:S(2)}, u32[]{:S(2)}) collective-permute-start(bf16[4,256,256]{2,1,0:T(8,128)(2,1)S(1)} %get-tuple-element.47), channel_id=1, source_target_pairs={{4,0},{8,4},{12,8},{16,12},{20,16},{24,20},{28,24},{5,1},{9,5},{13... | collective-permute-start | bytes 1572872 | tf_op jit(solution)/shard_map/ppermute | solution.py:717
  64.6 2.2 %collective-permute-start.4 = (f32[40,256]{1,0:T(8,128)S(1)}, f32[40,256]{1,0:T(8,128)S(1)}, u32[]{:S(2)}, u32[]{:S(2)}) collective-permute-start(f32[40,256]{1,0:T(8,128)S(1)} %get-tuple-element.50.noise), channel_id=1, source_target_pairs={{0,1},{1,2},{2,3},{4,5},{5,6},{6,7},{8,9},{9,10},{10,11},{12,13},{... | collective-permute-start | bytes 122888 | tf_op jit(solution)/shard_map/ppermute | solution.py:736
  66.7 5.1 %collective-permute-start.5 = (f32[40,256]{1,0:T(8,128)S(1)}, f32[40,256]{1,0:T(8,128)S(1)}, u32[]{:S(2)}, u32[]{:S(2)}) collective-permute-start(f32[40,256]{1,0:T(8,128)S(1)} %get-tuple-element.50.noise), channel_id=1, source_target_pairs={{1,0},{2,1},{3,2},{5,4},{6,5},{7,6},{9,8},{10,9},{11,10},{13,12},{... | collective-permute-start | bytes 122888 | tf_op jit(solution)/shard_map/ppermute | solution.py:737
  90.0 9.5 %copy-start.3 = (s32[1,128,1]{1,2,0:T(1,128)S(1)}, s32[1,128,1]{1,2,0:T(1,128)}, u32[]{:S(2)}) copy-start(s32[1,128,1]{1,2,0:T(1,128)} %param.11) | copy-start | bytes 1540
  90.0 9.5 %copy-start.4 = (f32[1,128]{1,0:T(1,128)S(1)}, f32[1,128]{1,0:T(1,128)}, u32[]{:S(2)}) copy-start(f32[1,128]{1,0:T(1,128)} %slow.1) | copy-start | bytes 1540
  90.0 9.5 %copy-start.5 = (f32[1,128]{1,0:T(1,128)S(1)}, f32[1,128]{1,0:T(1,128)}, u32[]{:S(2)}) copy-start(f32[1,128]{1,0:T(1,128)} %fast.1) | copy-start | bytes 1540
  92.7 21.4 %all-to-all-start.1 = ((bf16[8,32,1024]{2,1,0:T(8,128)(2,1)}), bf16[8,32,1024]{2,1,0:T(8,128)(2,1)S(1)}, u32[]{:S(2)}, u32[]{:S(2)}) async-start(bf16[8,32,1024]{2,1,0:T(8,128)(2,1)} %bitcast.8), calls=%async_computation.1 | async-start | bytes 1048576 | tf_op jit(solution)/shard_map/all_to_all | solution.py:746
  99.8 14.3 %copy-start.1 = (bf16[1,128,256]{2,1,0:T(8,128)(2,1)S(1)}, bf16[1,128,256]{2,1,0:T(8,128)(2,1)}, u32[]{:S(2)}) copy-start(bf16[1,128,256]{2,1,0:T(8,128)(2,1)} %param.10) | copy-start | bytes 196612

commit v2 on v1

--- a/solution.py
+++ b/solution.py
@@ -46,7 +46,7 @@
 
 
 def outbox_kernel(capacity, *refs):
-    sources, outbox, places, sems = refs[0:4], refs[4], refs[5:9], refs[9]
+    sources, result, places, outbox, sems = refs[0:4], refs[4], refs[5:9], refs[9], refs[10]
     copies = [
         pltpu.make_async_copy(source, place, sems.at[k])
         for k, (source, place) in enumerate(zip(sources, places))
@@ -78,14 +78,30 @@
     ]
     for copy in copies[2:]:
         copy.wait()
+    leaving = []
+
+    def leave(start, width):
+        lanes = pl.ds(start, width)
+        copy = pltpu.make_async_copy(
+            outbox.at[:, lanes], result.at[:, lanes], sems.at[len(copies) + len(leaving)]
+        )
+        copy.start()
+        leaving.append(copy)
+
     for k, (hot, first, width) in enumerate(
         zip(hots, (0, 0, tiles - edge), (tiles, edge, edge))
     ):
+        outbox[:, at : at + width] = dot(hot, foot[:, first : first + width]).astype(BF16)
+        if k == 0:
+            leave(at, width)
         outbox[:, k * frames : (k + 1) * frames] = dot(hot, traces[...]).astype(BF16)
-        outbox[:, at : at + width] = dot(hot, foot[:, first : first + width]).astype(BF16)
         lefts = jnp.where(lane == k, dot(hot, left), lefts)
         at += width
+    leave(0, 3 * frames)
     outbox[:, at:] = lefts.astype(BF16)
+    leave(3 * frames + tiles, outbox.shape[1] - 3 * frames - tiles)
+    for copy in leaving:
+        copy.wait()
 
 
 def make_outbox(stripe, column, foot, traces, capacity, slots):
@@ -96,9 +112,10 @@
     return pl.pallas_call(
         functools.partial(outbox_kernel, capacity),
         in_specs=[HBM] * len(args),
+        out_specs=HBM,
         out_shape=jax.ShapeDtypeStruct((slots, width), BF16),
         scratch_shapes=[pltpu.VMEM(a.shape, a.dtype) for a in args]
-        + [pltpu.SemaphoreType.DMA((len(args),))],
+        + [pltpu.VMEM((slots, width), BF16), pltpu.SemaphoreType.DMA((len(args) + 3,))],
         compiler_params=params(56),
         cost_estimate=COST,
         name="outbox",
@@ -394,11 +411,19 @@
     )(foot_rows, near_rows, *noises)
 
 
-def annulus_group(g, own, leaving, entering, gain, band, column, outgoing, slot=None):
-    cols, frames = own.shape[1:]
+def side_sum(column):
+    cols = column.shape[0]
     top = lax.broadcasted_iota(jnp.int32, (cols // 8, 8, LANES), 1) < 4
     blank = jnp.zeros((2, 8, LANES), F32)
-    slot = g if slot is None else slot
+    turned = pltpu.roll(column.reshape(cols // 8, 8, LANES), 4, 1)
+    turned = jnp.concatenate([blank, turned, blank], axis=0)
+    both = turned[0 : cols // 8 + 1] + turned[3 : cols // 8 + 4]
+    sides = jnp.where(top, both[0 : cols // 8], both[1 : cols // 8 + 1])
+    return sides.reshape(cols, LANES)
+
+
+def annulus_group(g, own, leaving, entering, gain, band, column, outgoing):
+    frames = own.shape[2]
     outs = [leaving(q) for q in range(PER)]
     news = [entering(q) for q in range(PER)]
     levels = [dot(band, jnp.concatenate([o, n], axis=0)) for o, n in zip(outs, news)]
@@ -410,12 +435,8 @@
             part = slice(h * LANES, (h + 1) * LANES)
             inner = column[h] - outs[q][:, part].astype(F32)
             column[h] = inner + news[q][:, part].astype(F32)
-            turned = pltpu.roll(inner.reshape(cols // 8, 8, LANES), 4, 1)
-            turned = jnp.concatenate([blank, turned, blank], axis=0)
-            both = turned[0 : cols // 8 + 1] + turned[3 : cols // 8 + 4]
-            sides = jnp.where(top, both[0 : cols // 8], both[1 : cols // 8 + 1])
-            fit = (levels[q][:, part] + sides.reshape(cols, LANES)) * gain
-            outgoing[slot, q, :, part] = fit.astype(BF16)
+            fit = (levels[q][:, part] + side_sum(inner)) * gain
+            outgoing[g, q, :, part] = fit.astype(BF16)
             det.append((own[g * PER + q, :, part].astype(F32) - fit).astype(BF16))
         dets.append(jnp.concatenate(det, axis=1))
     return column, dets
@@ -493,7 +514,7 @@
 
 def mid_kernel(
     own, above, below, weight, gain, before, upper, lower, total,
-    background, new_upper, new_lower, new_total, outgoing, sems,
+    background, new_total, base, gain_table, band_table, outgoing, sems,
 ):
     del before
     rows = own.shape[0]
@@ -501,9 +522,8 @@
     y, z = low * PER, high * PER
     send = sender(outgoing, background, sems)
     gains, band = tables(gain)
-    column = add_rows(halves(upper), [above[r] for r in range(PER)])
-    put(new_upper, column)
-    column = add_rows(column, [own[RAD + r] for r in range(PER)])
+    first = add_rows(halves(upper), [above[r] for r in range(PER)])
+    column = add_rows(first, [own[RAD + r] for r in range(PER)])
     _, low_dets = annulus_group(
         low, own, lambda q: above[q], lambda q: own[y + RAD + q], gains, band, column, outgoing
     )
@@ -513,28 +533,50 @@
         outgoing,
     )
     send(high).start()
-    put(new_lower, column)
     new_total[...] = grow(grow(total[...], weight, low, low_dets), weight, high, high_dets)
+    gain_table[...] = gains
+    band_table[...] = band[:, : own.shape[1]]
+    for q in range(PER):
+        if q > 0:
+            first = add_rows(first, [own[RAD + q - 1]])
+        inner = own[z + PER - RAD + q]
+        column = add_rows(column, [inner], -1.0)
+        for k, (sums, row) in enumerate(((first, own[RAD + q]), (column, inner))):
+            level = dot(band_table[...], row)
+            for h, value in enumerate(sums):
+                part = slice(h * LANES, (h + 1) * LANES)
+                base[k, q, :, part] = level[:, part] + side_sum(value)
     send(low).wait()
     send(high).wait()
 
 
 def end_kernel(
-    own, above, below, weight, weight_next, weight_prev, gain, upper, lower, total,
-    gradient, late,
+    own, above, below, weight, weight_next, weight_prev, total, base, gain, band, gradient, late
 ):
-    rows, _, frames = own.shape
+    rows, cols, frames = own.shape
     low, high = 0, rows // PER - 1
-    z = high * PER
-    gains, band = tables(gain)
-    _, low_dets = annulus_group(
-        low, own, lambda q: above[q], lambda q: own[RAD + q], gains, band,
-        add_rows(halves(upper), [above[r] for r in range(PER)]), late, 0,
-    )
-    _, high_dets = annulus_group(
-        high, own, lambda q: own[z - RAD + q], lambda q: below[q], gains, band, halves(lower),
-        late, 1,
-    )
+    blank = [jnp.zeros((cols, LANES), F32)] * (frames // LANES)
+    dets = []
+    for k, (g, far, order) in enumerate(
+        ((low, above, range(PER - 1, -1, -1)), (high, below, range(PER)))
+    ):
+        column, mine = blank, [None] * PER
+        for i, q in enumerate(order):
+            row = far[q]
+            level = dot(band[...], row)
+            det = []
+            for h in range(frames // LANES):
+                part = slice(h * LANES, (h + 1) * LANES)
+                fit = base[k, q, :, part] + level[:, part]
+                if i > 0:
+                    fit = fit + side_sum(column[h])
+                fit = fit * gain[...]
+                late[k, q, :, part] = fit.astype(BF16)
+                det.append((own[g * PER + q, :, part].astype(F32) - fit).astype(BF16))
+            mine[q] = jnp.concatenate(det, axis=1)
+            column = add_rows(column, [row])
+        dets.append(mine)
+    low_dets, high_dets = dets
     grown = grow(grow(total[...], weight, low, low_dets), weight, high, high_dets)
     edges = ((2, weight_next, high_dets[PER - GR :]), (3, weight_prev, low_dets[:GR]))
     for at, edge, parts in edges:
@@ -592,15 +634,20 @@
         middle_kernel, "annulus_middle", (own, near, weight, gain),
         (background, column, column, total), None,
     )
-    done, upper, lower, grown = call(
+    prepared = (
+        jax.ShapeDtypeStruct((2, PER, cols, frames), F32),
+        jax.ShapeDtypeStruct((cols, LANES), F32),
+        jax.ShapeDtypeStruct((cols, cols), BF16),
+    )
+    done, grown, *prepared = call(
         mid_kernel, "annulus_mid",
         (own, *mid, weight, gain, done, upper, lower, grown),
-        (background, column, column, total), 5,
+        (background, total, *prepared), 5,
         pl.CostEstimate(
             flops=2 * rows * cols * cols * frames, bytes_accessed=5 * MIB, transcendentals=0
         ),
     )
-    args = (own, *far, weight, weight_next, weight_prev, gain, upper, lower, grown)
+    args = (own, *far, weight, weight_next, weight_prev, grown, *prepared)
     gradient, late = pl.pallas_call(
         end_kernel,
         in_specs=[VMEM] * len(args),

time: 116 us -> 116 us (level)
  no operation moved by 1% of the time
where the time goes in v2:
time: 116 us; the launch traced here: 115 us
  waiting for transfers between devices  45.7 us (39%)
  Pallas kernels  35.4 us (31%)
  starting transfers between devices  31.7 us (27%)
  local copies, waits for them, and re-layouts  1.3 us (1%)
    all_to_all x1, waiting for transfers between devices, on_device(): lax.all_to_all(outbox, 'pix', split_axis=0, concat_axis=0, tiled=True)  21.3 us
    pallas_call x2, Pallas kernels, make_residual(): pl.pallas_call(functools.partial(residual_kernel, pick, low, high, earlie...  14.4 us
    all_to_all x1, waiting for transfers between devices, on_device(): lax.all_to_all(gradient, 'pix', split_axis=0, concat_axis=0, tiled=True)  13.3 us
    ppermute x3, starting transfers between devices, exchange(): lax.ppermute(up, 'pix', pix_up)  11 us
    all_to_all x1, starting transfers between devices, on_device(): lax.all_to_all(outbox, 'pix', split_axis=0, concat_axis=0, tiled=True)  7.29 us
    all_to_all x1, starting transfers between devices, on_device(): lax.all_to_all(gradient, 'pix', split_axis=0, concat_axis=0, tiled=True)  6.73 us
    ppermute x3, waiting for transfers between devices, exchange(): lax.ppermute(up, 'pix', pix_up)  6.62 us
    pallas_call x2, Pallas kernels, call(): pl.pallas_call(kernel, in_specs=specs, out_specs=[HBM] + [VMEM] * (len(ou...  6.38 us
  transfers between devices with their start and end apart: 10, of which 5 were waited for; matrix products, arithmetic and copies ran while one was open for 1% of the time, Pallas kernels for 25%

profile of v2, /device:TPU:0, one launch (start us, length us, event | category | flops | bytes accessed | tf_op | source)
XLA Modules:
  0.0 115.1 jit_solution(4659916983062445839)
XLA Ops:
  0.6 0.0 copy-start.6
  0.6 2.4 %outbox.1 = bf16[256,2176]{1,0:T(8,128)(2,1)} custom-call(s32[1,128]{1,0:T(1,128)} %bitcast.21, s32[1,128]{1,0:T(1,128)} %refs_1_.1, bf16[128,1024]{1,0:T(8,128)(2,1)} %bitcast.24, bf16[128,256]{1,0:T(8,128)(2,1)} %bitcast.19), custom_call_target="tpu_custom_call" | custom-call | flops 1 | bytes 1 | tf_op jit(solution)/shard_map/outbox/pallas_call | solution.py:112
  3.0 7.3 %all-to-all-start = ((bf16[8,32,2176]{2,1,0:T(8,128)(2,1)}), bf16[8,32,2176]{2,1,0:T(8,128)(2,1)S(1)}, u32[]{:S(2)}, u32[]{:S(2)}) async-start(bf16[8,32,2176]{2,1,0:T(8,128)(2,1)} %bitcast.23), calls=%async_computation | async-start | bytes 2228224 | tf_op jit(solution)/shard_map/all_to_all | solution.py:767
  10.3 1.3 %slice_bitcast_fusion = (bf16[4,256,256]{2,1,0:T(8,128)(2,1)S(1)}, bf16[4,256,256]{2,1,0:T(8,128)(2,1)S(1)}) fusion(bf16[1,32,256,256]{3,2,1,0:T(8,128)(2,1)} %movie.3), kind=kLoop, calls=%fused_computation | loop fusion | bytes 2097152 | tf_op jit(solution)/shard_map/squeeze | solution.py:768
  11.6 1.3 %collective-permute-start = (bf16[4,256,256]{2,1,0:T(8,128)(2,1)S(1)}, bf16[4,256,256]{2,1,0:T(8,128)(2,1)S(1)}, u32[]{:S(2)}, u32[]{:S(2)}) collective-permute-start(bf16[4,256,256]{2,1,0:T(8,128)(2,1)S(1)} %get-tuple-element.73), channel_id=1, source_target_pairs={{4,0},{8,4},{12,8},{16,12},{20,16},{24,20},{28,24},{5,1},{9,5},{13... | collective-permute-start | bytes 1572872 | tf_op jit(solution)/shard_map/ppermute | solution.py:764
  12.9 4.6 %collective-permute-start.1 = (bf16[4,256,256]{2,1,0:T(8,128)(2,1)S(1)}, bf16[4,256,256]{2,1,0:T(8,128)(2,1)S(1)}, u32[]{:S(2)}, u32[]{:S(2)}) collective-permute-start(bf16[4,256,256]{2,1,0:T(8,128)(2,1)S(1)} %get-tuple-element.72), channel_id=1, source_target_pairs={{0,4},{4,8},{8,12},{12,16},{16,20},{20,24},{24,28},{1,5},{5,9},{9,... | collective-permute-start | bytes 1572872 | tf_op jit(solution)/shard_map/ppermute | solution.py:764
  17.5 0.0 copy-done.6
  17.5 0.1 multiply_reduce_fusion
  17.6 21.3 %all-to-all-done = bf16[8,32,2176]{2,1,0:T(8,128)(2,1)S(1)} async-done(((bf16[8,32,2176]{2,1,0:T(8,128)(2,1)}), bf16[8,32,2176]{2,1,0:T(8,128)(2,1)S(1)}, u32[]{:S(2)}, u32[]{:S(2)}) %all-to-all-start) | async-done | bytes 1114144 | tf_op jit(solution)/shard_map/all_to_all | solution.py:767
  39.0 4.5 %residual.2 = (bf16[32,256,256]{2,1,0:T(8,128)(2,1)S(1)}, bf16[32,256,256]{2,1,0:T(8,128)(2,1)}, f32[2,4,256]{2,1,0:T(4,128)S(1)}, bf16[4,256,256]{2,1,0:T(8,128)(2,1)S(1)}, bf16[4,256,256]{2,1,0:T(8,128)(2,1)S(1)}) custom-call(bf16[256,2176]{1,0:T(8,128)(2,1)S(1)} %bitcast.15, bf16[1,32,256,256]{3,2,1,0:T(8,128)(2,1)} %movie.3), custom_call_target="tpu_custom_call" | custom-call | flops 1 | bytes 1 | tf_op jit(solution)/shard_map/residual/pallas_call | solution.py:265
  43.5 1.9 %collective-permute-start.6 = (bf16[4,256,256]{2,1,0:T(8,128)(2,1)S(1)}, bf16[4,256,256]{2,1,0:T(8,128)(2,1)S(1)}, u32[]{:S(2)}, u32[]{:S(2)}) collective-permute-start(bf16[4,256,256]{2,1,0:T(8,128)(2,1)S(1)} %get-tuple-element.55), channel_id=1, source_target_pairs={{0,4},{4,8},{8,12},{12,16},{16,20},{20,24},{24,28},{1,5},{5,9},{9,... | collective-permute-start | bytes 1572872 | tf_op jit(solution)/shard_map/ppermute | solution.py:764
  45.4 1.3 %collective-permute-start.7 = (bf16[4,256,256]{2,1,0:T(8,128)(2,1)S(1)}, bf16[4,256,256]{2,1,0:T(8,128)(2,1)S(1)}, u32[]{:S(2)}, u32[]{:S(2)}) collective-permute-start(bf16[4,256,256]{2,1,0:T(8,128)(2,1)S(1)} %get-tuple-element.56), channel_id=1, source_target_pairs={{4,0},{8,4},{12,8},{16,12},{20,16},{24,20},{28,24},{5,1},{9,5},{13... | collective-permute-start | bytes 1572872 | tf_op jit(solution)/shard_map/ppermute | solution.py:764
  46.7 9.9 %residual.3 = (bf16[32,256,256]{2,1,0:T(8,128)(2,1)S(1)}, bf16[32,256,256]{2,1,0:T(8,128)(2,1)}, f32[6,4,256]{2,1,0:T(4,128)S(1)}, bf16[4,256,256]{2,1,0:T(8,128)(2,1)S(1)}, bf16[4,256,256]{2,1,0:T(8,128)(2,1)S(1)}) custom-call(bf16[256,2176]{1,0:T(8,128)(2,1)S(1)} %bitcast.16, ...), custom_call_target="tpu_custom_call", output_to_operand_aliasing={{0}: (2, {}), {1}: (3, {})} | custom-call | flops 1 | bytes 1 | tf_op jit(solution)/shard_map/residual/pallas_call | solution.py:265
  56.6 0.0 copy-start
  56.6 0.0 copy-start.2
  56.6 0.0 collective-permute-done.movie_next
  56.6 0.0 collective-permute-done.1.movie_prev
  56.6 1.9 %near.1 = (bf16[8,256,256]{2,1,0:T(8,128)(2,1)S(1)}, bf16[8,256,256]{2,1,0:T(8,128)(2,1)S(1)}, f32[40,256]{1,0:T(8,128)S(1)}) custom-call(bf16[256,2176]{1,0:T(8,128)(2,1)S(1)} %bitcast.17, bf16[4,256,256]{2,1,0:T(8,128)(2,1)S(1)} %collective-permute-done.movie_next, bf16[4,256,256]{2,1,0:T(8,128)(2,1)S(1)} %collective-permute-done.1.movie_prev, ...), custom_call_target="tpu_custom_call" | custom-call | flops 1 | bytes 1 | tf_op jit(solution)/shard_map/near/pallas_call | solution.py:316
  58.5 4.6 %collective-permute-start.2 = (bf16[4,256,256]{2,1,0:T(8,128)(2,1)S(1)}, bf16[4,256,256]{2,1,0:T(8,128)(2,1)S(1)}, u32[]{:S(2)}, u32[]{:S(2)}) collective-permute-start(bf16[4,256,256]{2,1,0:T(8,128)(2,1)S(1)} %get-tuple-element.47), channel_id=1, source_target_pairs={{0,4},{4,8},{8,12},{12,16},{16,20},{20,24},{24,28},{1,5},{5,9},{9,... | collective-permute-start | bytes 1572872 | tf_op jit(solution)/shard_map/ppermute | solution.py:764
  63.1 1.3 %collective-permute-start.3 = (bf16[4,256,256]{2,1,0:T(8,128)(2,1)S(1)}, bf16[4,256,256]{2,1,0:T(8,128)(2,1)S(1)}, u32[]{:S(2)}, u32[]{:S(2)}) collective-permute-start(bf16[4,256,256]{2,1,0:T(8,128)(2,1)S(1)} %get-tuple-element.48), channel_id=1, source_target_pairs={{4,0},{8,4},{12,8},{16,12},{20,16},{24,20},{28,24},{5,1},{9,5},{13... | collective-permute-start | bytes 1572872 | tf_op jit(solution)/shard_map/ppermute | solution.py:764
  64.4 1.3 %collective-permute-start.4 = (f32[40,256]{1,0:T(8,128)S(1)}, f32[40,256]{1,0:T(8,128)S(1)}, u32[]{:S(2)}, u32[]{:S(2)}) collective-permute-start(f32[40,256]{1,0:T(8,128)S(1)} %get-tuple-element.51.noise), channel_id=1, source_target_pairs={{0,1},{1,2},{2,3},{4,5},{5,6},{6,7},{8,9},{9,10},{10,11},{12,13},{... | collective-permute-start | bytes 122888 | tf_op jit(solution)/shard_map/ppermute | solution.py:783
  65.7 0.9 collective-permute-done.4.noise_before
  66.5 1.5 %collective-permute-start.5 = (f32[40,256]{1,0:T(8,128)S(1)}, f32[40,256]{1,0:T(8,128)S(1)}, u32[]{:S(2)}, u32[]{:S(2)}) collective-permute-start(f32[40,256]{1,0:T(8,128)S(1)} %get-tuple-element.51.noise), channel_id=1, source_target_pairs={{1,0},{2,1},{3,2},{5,4},{6,5},{7,6},{9,8},{10,9},{11,10},{13,12},{... | collective-permute-start | bytes 122888 | tf_op jit(solution)/shard_map/ppermute | solution.py:784
  68.0 3.6 %collective-permute-done.5.noise_after = f32[40,256]{1,0:T(8,128)S(1)} collective-permute-done((f32[40,256]{1,0:T(8,128)S(1)}, f32[40,256]{1,0:T(8,128)S(1)}, u32[]{:S(2)}, u32[]{:S(2)}) %collective-permute-start.5) | collective-permute-done | bytes 40992 | tf_op jit(solution)/shard_map/ppermute | solution.py:784
  71.6 5.2 %weights.1 = (bf16[32,256,256]{2,1,0:T(8,128)(2,1)S(1)}, bf16[3,256,256]{2,1,0:T(8,128)(2,1)S(1)}, bf16[3,256,256]{2,1,0:T(8,128)(2,1)S(1)}) custom-call(bf16[32,256,256]{2,1,0:T(8,128)(2,1)S(1)} %get-tuple-element.49.own, bf16[8,256,256]{2,1,0:T(8,128)(2,1)S(1)} %get-tuple-element.50.near, f32[40,256]{1,0:T(8,128)S(1)} %get-tuple-element.51.noise, ...), custom_call_target="tpu_custom_call" | custom-call | flops 1 | bytes 1 | tf_op jit(solution)/shard_map/weights/pallas_call | solution.py:394
  76.8 0.0 copy-done
  76.8 0.0 copy-done.2
  76.8 4.0 %annulus_middle.1 = (bf16[1,32,256,256]{3,2,1,0:T(8,128)(2,1)}, f32[256,256]{1,0:T(8,128)S(1)}, f32[256,256]{1,0:T(8,128)S(1)}, f32[256,256]{1,0:T(8,128)S(1)}) custom-call(bf16[32,256,256]{2,1,0:T(8,128)(2,1)S(1)} %copy-done, bf16[8,256,256]{2,1,0:T(8,128)(2,1)S(1)} %get-tuple-element.57.near, bf16[32,256,256]{2,1,0:T(8,128)(2,1)S(1)} %get-tuple-element.52.weight, ...), custom_call_target="tpu_custom_call" | custom-call | flops 1 | bytes 1 | tf_op jit(solution)/shard_map/annulus_middle/pallas_call | solution.py:618
  80.8 0.0 collective-permute-done.6.above
  80.9 0.0 collective-permute-done.7.below
  80.9 2.3 %annulus_mid.1 = (bf16[1,32,256,256]{3,2,1,0:T(8,128)(2,1)}, f32[256,256]{1,0:T(8,128)S(1)}, f32[2,4,256,256]{3,2,1,0:T(8,128)S(1)}, f32[256,128]{1,0:T(8,128)S(1)}, bf16[256,256]{1,0:T(8,128)(2,1)S(1)}) custom-call(bf16[32,256,256]{2,1,0:T(8,128)(2,1)S(1)} %copy-done, ...), custom_call_target="tpu_custom_call", output_to_operand_aliasing={{0}: (5, {})} | custom-call | flops 1073741824 | bytes 5242880 | tf_op jit(solution)/shard_map/annulus_mid/pallas_call | solution.py:618
  83.2 6.6 %collective-permute-done.2.above = bf16[4,256,256]{2,1,0:T(8,128)(2,1)S(1)} collective-permute-done((bf16[4,256,256]{2,1,0:T(8,128)(2,1)S(1)}, bf16[4,256,256]{2,1,0:T(8,128)(2,1)S(1)}, u32[]{:S(2)}, u32[]{:S(2)}) %collective-permute-start.2) | collective-permute-done | bytes 524320 | tf_op jit(solution)/shard_map/ppermute | solution.py:764
  89.8 0.0 collective-permute-done.3.below
  89.8 0.0 copy-start.3
  89.8 0.0 copy-start.4
  89.8 0.0 copy-start.5
  89.8 2.4 %annulus_end.1 = (bf16[256,1024]{1,0:T(8,128)(2,1)}, bf16[2,4,256,256]{3,2,1,0:T(8,128)(2,1)S(1)}) custom-call(bf16[32,256,256]{2,1,0:T(8,128)(2,1)S(1)} %copy-done, bf16[4,256,256]{2,1,0:T(8,128)(2,1)S(1)} %collective-permute-done.2.above, bf16[4,256,256]{2,1,0:T(8,128)(2,1)S(1)} %collective-permute-done.3.below, ...), custom_call_target="tpu_custom_call" | custom-call | flops 1 | bytes 1 | tf_op jit(solution)/shard_map/annulus_end/pallas_call | solution.py:651
  92.2 6.7 %all-to-all-start.1 = ((bf16[8,32,1024]{2,1,0:T(8,128)(2,1)}), bf16[8,32,1024]{2,1,0:T(8,128)(2,1)S(1)}, u32[]{:S(2)}, u32[]{:S(2)}) async-start(bf16[8,32,1024]{2,1,0:T(8,128)(2,1)} %bitcast.8), calls=%async_computation.1 | async-start | bytes 1048576 | tf_op jit(solution)/shard_map/all_to_all | solution.py:793
  98.9 0.0 copy-done.3
  98.9 0.0 copy-done.4
  99.0 0.0 copy-done.5
  99.0 0.3 prepare.1
  99.3 0.0 copy-start.1
  99.3 1.0 late_rows.1
  100.3 13.3 %all-to-all-done.1 = bf16[8,32,1024]{2,1,0:T(8,128)(2,1)S(1)} async-done(((bf16[8,32,1024]{2,1,0:T(8,128)(2,1)}), bf16[8,32,1024]{2,1,0:T(8,128)(2,1)S(1)}, u32[]{:S(2)}, u32[]{:S(2)}) %all-to-all-start.1) | async-done | bytes 524320 | tf_op jit(solution)/shard_map/all_to_all | solution.py:793
  113.6 0.0 copy-done.1
  113.6 1.5 %traces.1 = f32[128,256]{1,0:T(8,128)} custom-call(bf16[128,1024]{1,0:T(8,128)(2,1)S(1)} %get-tuple-element.69.hots, f32[4,128,256]{2,1,0:T(8,128)S(1)} %get-tuple-element.70.tables, bf16[128,256]{1,0:T(8,128)(2,1)S(1)} %bitcast.20, bf16[256,1024]{1,0:T(8,128)(2,1)S(1)} %bitcast.18), custom_call_target="tpu_custom_call" | custom-call | flops 1 | bytes 1 | tf_op jit(solution)/shard_map/traces/pallas_call | solution.py:737
  (1 shorter events, 0.0 us)
Async XLA Ops:
  0.6 16.9 %copy-start.6 = (bf16[1,128,1024]{2,1,0:T(8,128)(2,1)S(1)}, bf16[1,128,1024]{2,1,0:T(8,128)(2,1)}, u32[]{:S(2)}) copy-start(bf16[1,128,1024]{2,1,0:T(8,128)(2,1)} %param.9) | copy-start | bytes 786436
  3.0 35.9 %all-to-all-start = ((bf16[8,32,2176]{2,1,0:T(8,128)(2,1)}), bf16[8,32,2176]{2,1,0:T(8,128)(2,1)S(1)}, u32[]{:S(2)}, u32[]{:S(2)}) async-start(bf16[8,32,2176]{2,1,0:T(8,128)(2,1)} %bitcast.23), calls=%async_computation | async-start | bytes 2228224 | tf_op jit(solution)/shard_map/all_to_all | solution.py:767
  11.6 45.0 %collective-permute-start = (bf16[4,256,256]{2,1,0:T(8,128)(2,1)S(1)}, bf16[4,256,256]{2,1,0:T(8,128)(2,1)S(1)}, u32[]{:S(2)}, u32[]{:S(2)}) collective-permute-start(bf16[4,256,256]{2,1,0:T(8,128)(2,1)S(1)} %get-tuple-element.73), channel_id=1, source_target_pairs={{4,0},{8,4},{12,8},{16,12},{20,16},{24,20},{28,24},{5,1},{9,5},{13... | collective-permute-start | bytes 1572872 | tf_op jit(solution)/shard_map/ppermute | solution.py:764
  12.9 43.7 %collective-permute-start.1 = (bf16[4,256,256]{2,1,0:T(8,128)(2,1)S(1)}, bf16[4,256,256]{2,1,0:T(8,128)(2,1)S(1)}, u32[]{:S(2)}, u32[]{:S(2)}) collective-permute-start(bf16[4,256,256]{2,1,0:T(8,128)(2,1)S(1)} %get-tuple-element.72), channel_id=1, source_target_pairs={{0,4},{4,8},{8,12},{12,16},{16,20},{20,24},{24,28},{1,5},{5,9},{9,... | collective-permute-start | bytes 1572872 | tf_op jit(solution)/shard_map/ppermute | solution.py:764
  43.5 37.4 %collective-permute-start.6 = (bf16[4,256,256]{2,1,0:T(8,128)(2,1)S(1)}, bf16[4,256,256]{2,1,0:T(8,128)(2,1)S(1)}, u32[]{:S(2)}, u32[]{:S(2)}) collective-permute-start(bf16[4,256,256]{2,1,0:T(8,128)(2,1)S(1)} %get-tuple-element.55), channel_id=1, source_target_pairs={{0,4},{4,8},{8,12},{12,16},{16,20},{20,24},{24,28},{1,5},{5,9},{9,... | collective-permute-start | bytes 1572872 | tf_op jit(solution)/shard_map/ppermute | solution.py:764
  45.4 35.5 %collective-permute-start.7 = (bf16[4,256,256]{2,1,0:T(8,128)(2,1)S(1)}, bf16[4,256,256]{2,1,0:T(8,128)(2,1)S(1)}, u32[]{:S(2)}, u32[]{:S(2)}) collective-permute-start(bf16[4,256,256]{2,1,0:T(8,128)(2,1)S(1)} %get-tuple-element.56), channel_id=1, source_target_pairs={{4,0},{8,4},{12,8},{16,12},{20,16},{24,20},{28,24},{5,1},{9,5},{13... | collective-permute-start | bytes 1572872 | tf_op jit(solution)/shard_map/ppermute | solution.py:764
  56.6 20.2 %copy-start = (bf16[32,256,256]{2,1,0:T(8,128)(2,1)S(1)}, bf16[32,256,256]{2,1,0:T(8,128)(2,1)}, u32[]{:S(2)}) copy-start(bf16[32,256,256]{2,1,0:T(8,128)(2,1)} %get-tuple-element.41.own) | copy-start | bytes 12582916
  56.6 20.2 %copy-start.2 = (f32[1,256]{1,0:T(1,128)S(1)}, f32[1,256]{1,0:T(1,128)}, u32[]{:S(2)}) copy-start(f32[1,256]{1,0:T(1,128)} %gain.3) | copy-start | bytes 3076
  58.5 31.3 %collective-permute-start.2 = (bf16[4,256,256]{2,1,0:T(8,128)(2,1)S(1)}, bf16[4,256,256]{2,1,0:T(8,128)(2,1)S(1)}, u32[]{:S(2)}, u32[]{:S(2)}) collective-permute-start(bf16[4,256,256]{2,1,0:T(8,128)(2,1)S(1)} %get-tuple-element.47), channel_id=1, source_target_pairs={{0,4},{4,8},{8,12},{12,16},{16,20},{20,24},{24,28},{1,5},{5,9},{9,... | collective-permute-start | bytes 1572872 | tf_op jit(solution)/shard_map/ppermute | solution.py:764
  63.1 26.7 %collective-permute-start.3 = (bf16[4,256,256]{2,1,0:T(8,128)(2,1)S(1)}, bf16[4,256,256]{2,1,0:T(8,128)(2,1)S(1)}, u32[]{:S(2)}, u32[]{:S(2)}) collective-permute-start(bf16[4,256,256]{2,1,0:T(8,128)(2,1)S(1)} %get-tuple-element.48), channel_id=1, source_target_pairs={{4,0},{8,4},{12,8},{16,12},{20,16},{24,20},{28,24},{5,1},{9,5},{13... | collective-permute-start | bytes 1572872 | tf_op jit(solution)/shard_map/ppermute | solution.py:764
  64.4 2.2 %collective-permute-start.4 = (f32[40,256]{1,0:T(8,128)S(1)}, f32[40,256]{1,0:T(8,128)S(1)}, u32[]{:S(2)}, u32[]{:S(2)}) collective-permute-start(f32[40,256]{1,0:T(8,128)S(1)} %get-tuple-element.51.noise), channel_id=1, source_target_pairs={{0,1},{1,2},{2,3},{4,5},{5,6},{6,7},{8,9},{9,10},{10,11},{12,13},{... | collective-permute-start | bytes 122888 | tf_op jit(solution)/shard_map/ppermute | solution.py:783
  66.5 5.1 %collective-permute-start.5 = (f32[40,256]{1,0:T(8,128)S(1)}, f32[40,256]{1,0:T(8,128)S(1)}, u32[]{:S(2)}, u32[]{:S(2)}) collective-permute-start(f32[40,256]{1,0:T(8,128)S(1)} %get-tuple-element.51.noise), channel_id=1, source_target_pairs={{1,0},{2,1},{3,2},{5,4},{6,5},{7,6},{9,8},{10,9},{11,10},{13,12},{... | collective-permute-start | bytes 122888 | tf_op jit(solution)/shard_map/ppermute | solution.py:784
  89.8 9.1 %copy-start.3 = (s32[1,128,1]{1,2,0:T(1,128)S(1)}, s32[1,128,1]{1,2,0:T(1,128)}, u32[]{:S(2)}) copy-start(s32[1,128,1]{1,2,0:T(1,128)} %param.11) | copy-start | bytes 1540
  89.8 9.1 %copy-start.4 = (f32[1,128]{1,0:T(1,128)S(1)}, f32[1,128]{1,0:T(1,128)}, u32[]{:S(2)}) copy-start(f32[1,128]{1,0:T(1,128)} %slow.1) | copy-start | bytes 1540
  89.8 9.1 %copy-start.5 = (f32[1,128]{1,0:T(1,128)S(1)}, f32[1,128]{1,0:T(1,128)}, u32[]{:S(2)}) copy-start(f32[1,128]{1,0:T(1,128)} %fast.1) | copy-start | bytes 1540
  92.2 21.4 %all-to-all-start.1 = ((bf16[8,32,1024]{2,1,0:T(8,128)(2,1)}), bf16[8,32,1024]{2,1,0:T(8,128)(2,1)S(1)}, u32[]{:S(2)}, u32[]{:S(2)}) async-start(bf16[8,32,1024]{2,1,0:T(8,128)(2,1)} %bitcast.8), calls=%async_computation.1 | async-start | bytes 1048576 | tf_op jit(solution)/shard_map/all_to_all | solution.py:793
  99.3 14.3 %copy-start.1 = (bf16[1,128,256]{2,1,0:T(8,128)(2,1)S(1)}, bf16[1,128,256]{2,1,0:T(8,128)(2,1)}, u32[]{:S(2)}) copy-start(bf16[1,128,256]{2,1,0:T(8,128)(2,1)} %param.10) | copy-start | bytes 196612

commit v3 on v2

--- a/solution.py
+++ b/solution.py
@@ -288,9 +288,10 @@
 
 
 def near_kernel(
-    inbox, movie_next, movie_prev, mid_noise, other_noise, foot_rows, residual, noise
+    inbox, even, pair, diag_next, diag_prev, mid_noise, other_noise, foot_rows, residual, noise
 ):
-    frames = movie_next.shape[2]
+    frames = pair.shape[3]
+    first_of_pair = even[0] == 1
     groups = mid_noise.shape[0] + other_noise.shape[0]
     own = FOOT // PER
     change = change_matrix(frames)
@@ -298,23 +299,27 @@
     for order, part in (((1, groups - 2), mid_noise), (others, other_noise)):
         for i, g in enumerate(order):
             noise[NEAR + g * PER : NEAR + (g + 1) * PER, :] = part[i]
-    for side, (block, movie, first) in enumerate(
-        ((own, movie_next, 0), (own + NEAR // PER, movie_prev, NEAR + groups * PER))
+    for side, (block, direct, diagonal, first) in enumerate(
+        (
+            (own, first_of_pair, diag_next, 0),
+            (own + NEAR // PER, ~first_of_pair, diag_prev, NEAR + groups * PER),
+        )
     ):
         for q, row in enumerate(tile_rows(inbox, 1 + side, block, frames)):
             y = side * NEAR + q
             foot_rows[y] = row
-            left = movie[q].astype(F32) - model_row(row, inbox, 1 + side, frames)
-            left = left.astype(BF16)
+            movie = jnp.where(direct, pair[1 - side, q].astype(F32), diagonal[q].astype(F32))
+            left = (movie - model_row(row, inbox, 1 + side, frames)).astype(BF16)
             residual[y] = left
             noise[first + q : first + q + 1, :] = noise_row(left, change)
 
 
-def make_near(inbox, movie_next, movie_prev, noises):
+def make_near(inbox, even, pair, diag_next, diag_prev, noises):
     slots = inbox.shape[0]
-    cols, frames = movie_next.shape[1:]
+    cols, frames = diag_next.shape[1:]
     return pl.pallas_call(
         near_kernel,
+        in_specs=[VMEM, pl.BlockSpec(memory_space=pltpu.SMEM)] + [VMEM] * (3 + len(noises)),
         out_shape=(
             jax.ShapeDtypeStruct((2 * NEAR, slots, cols), BF16),
             jax.ShapeDtypeStruct((2 * NEAR, cols, frames), BF16),
@@ -323,7 +328,7 @@
         compiler_params=params(),
         cost_estimate=COST,
         name="near",
-    )(inbox, movie_next, movie_prev, *noises)
+    )(inbox, even, pair, diag_next, diag_prev, *noises)
 
 
 def weights_kernel(
@@ -758,6 +763,13 @@
     pix_up, pix_down = neighbours("pix")
     plane_up, plane_down = neighbours("plane")
 
+    is_even = lax.axis_index("pix") % 2 == 0
+    pair = lax.all_gather(
+        jnp.where(is_even, movie[0, rows - NEAR :], movie[0, :NEAR]),
+        "pix",
+        axis_index_groups=[[i, i + 1] for i in range(0, pix_count, 2)],
+    )
+    even = is_even.astype(jnp.int32).reshape(1)
     stripe_row = stripe.reshape(1, count)
     outbox = make_outbox(stripe_row, column, footprints[0], traces[0], capacity, slots)
     def exchange(up, down):
@@ -765,14 +777,15 @@
 
     frames_in, outbox = lax.optimization_barrier((movie, outbox))
     inbox = lax.all_to_all(outbox, "pix", split_axis=0, concat_axis=0, tiled=True)
-    near_prev, near_next = exchange(frames_in[0, rows - NEAR :], frames_in[0, :NEAR])
+    diag_prev = lax.ppermute(frames_in[0, rows - NEAR :], "pix", pix_up[1::2])
+    diag_next = lax.ppermute(frames_in[0, :NEAR], "pix", pix_down[1::2])
     *started, mid_noise, up, down = make_residual(inbox, movie)
     mid = exchange(up, down)
     foot_rows, residual, other_noise, up, down = make_residual(
         inbox, movie, (*started, mid_noise)
     )
     near_rows, near_residual, noise = make_near(
-        inbox, near_next, near_prev, (mid_noise, other_noise)
+        inbox, even, pair, diag_next, diag_prev, (mid_noise, other_noise)
     )
     foot_f = footprints[0].astype(F32)
     step = 1.0 / (jnp.sum(foot_f * foot_f, axis=1) + norm_eps)

time: 116 us -> 134 us (1.16)
  between operations: 0.88 us -> 14.3 us
  local copies, waits for them, and re-layouts: 1.3 us -> 13.5 us
  waiting for transfers between devices: 45.7 us -> 39.9 us
  starting transfers between devices: 31.7 us -> 26.3 us
  other arithmetic: 0.14 us -> 2.18 us
    unnamed x14 -> x28, local copies, waits for them, and re-layouts: 0.03 us -> 11.2 us
    ppermute x3 -> x2, waiting for transfers between devices: 6.62 us -> 0.01 us  [exchange(): lax.ppermute(up, 'pix', pix_up)]
    ppermute x3 -> x2, starting transfers between devices: 11 us -> 6.45 us  [exchange(): lax.ppermute(up, 'pix', pix_up)]
    select_n x0 -> x1, other arithmetic: none -> 2.04 us  [on_device(): jnp.where(is_even, movie[0, rows - NEAR:], movie[0, :NEAR])]
    ppermute x0 -> x2, starting transfers between devices: none -> 1.38 us  [the longest x1 0.69 us: on_device(): diag_prev = lax.ppermute(frames_in[0, rows - NEAR:], 'pix', pix_up[1::2])]
    ppermute x3 -> x2, starting transfers between devices: 3.88 us -> 2.58 us  [exchange(): lax.ppermute(down, 'pix', pix_down)]
  transfers between devices with their start and end apart: 10 -> 11, of which waited for: 5 -> 4; matrix products, arithmetic and copies ran while one was open for 1% -> 3% of each run, Pallas kernels for 25% -> 23%
where the time goes in v3:
time: 134 us; the launch traced here: 132 us
  waiting for transfers between devices  39.9 us (30%)
  Pallas kernels  36.1 us (27%)
  starting transfers between devices  26.3 us (20%)
  between operations  14.3 us (11%)
  local copies, waits for them, and re-layouts  13.5 us (10%)
  other arithmetic  2.18 us (2%)
    all_to_all x1, waiting for transfers between devices, on_device(): lax.all_to_all(outbox, 'pix', split_axis=0, concat_axis=0, tiled=True)  22.6 us
    pallas_call x2, Pallas kernels, make_residual(): pl.pallas_call(functools.partial(residual_kernel, pick, low, high, earlie...  15.3 us
    all_to_all x1, waiting for transfers between devices, on_device(): lax.all_to_all(gradient, 'pix', split_axis=0, concat_axis=0, tiled=True)  12.8 us
    unnamed x28, local copies, waits for them, and re-layouts  11.2 us
    all_to_all x1, starting transfers between devices, on_device(): lax.all_to_all(outbox, 'pix', split_axis=0, concat_axis=0, tiled=True)  7.29 us
    ppermute x2, starting transfers between devices, exchange(): lax.ppermute(up, 'pix', pix_up)  6.45 us
    pallas_call x2, Pallas kernels, call(): pl.pallas_call(kernel, in_specs=specs, out_specs=[HBM] + [VMEM] * (len(ou...  6.14 us
    all_to_all x1, starting transfers between devices, on_device(): lax.all_to_all(gradient, 'pix', split_axis=0, concat_axis=0, tiled=True)  5.84 us
  transfers between devices with their start and end apart: 11, of which 4 were waited for; matrix products, arithmetic and copies ran while one was open for 3% of the time, Pallas kernels for 23%

profile of v3, /device:TPU:0, one launch (start us, length us, event | category | flops | bytes accessed | tf_op | source)
XLA Modules:
  0.0 132.3 jit_solution(10654373094590196859)
XLA Ops:
  7.2 0.0 copy-start.13
  7.2 2.4 %outbox.1 = bf16[256,2176]{1,0:T(8,128)(2,1)} custom-call(s32[1,128]{1,0:T(1,128)} %bitcast.22, s32[1,128]{1,0:T(1,128)} %refs_1_.1, bf16[128,1024]{1,0:T(8,128)(2,1)} %bitcast.25, bf16[128,256]{1,0:T(8,128)(2,1)} %bitcast.20), custom_call_target="tpu_custom_call" | custom-call | flops 1 | bytes 1 | tf_op jit(solution)/shard_map/outbox/pallas_call | solution.py:112
  9.6 7.3 %all-to-all-start = ((bf16[8,32,2176]{2,1,0:T(8,128)(2,1)}), bf16[8,32,2176]{2,1,0:T(8,128)(2,1)S(1)}, u32[]{:S(2)}, u32[]{:S(2)}) async-start(bf16[8,32,2176]{2,1,0:T(8,128)(2,1)} %bitcast.24), calls=%async_computation | async-start | bytes 2228224 | tf_op jit(solution)/shard_map/all_to_all | solution.py:779
  16.9 0.0 all-gather.2.cloned.1.call-start
  16.9 2.0 %slice_select_fusion = bf16[1,4,256,256]{3,2,1,0:T(8,128)(2,1)} fusion(bf16[1,32,256,256]{3,2,1,0:T(8,128)(2,1)} %movie.3, pred[]{:T(512)S(6)} %eq.5), kind=kLoop, calls=%fused_computation.2 | loop fusion | flops 262144 | bytes 1572865 | tf_op jit(solution)/shard_map/jit(_where)/select_n | solution.py:768
  19.0 0.0 all-gather.2.cloned.1.call-update
  19.0 2.3 %slice_bitcast_fusion = (bf16[4,256,256]{2,1,0:T(8,128)(2,1)}, bf16[4,256,256]{2,1,0:T(8,128)(2,1)}) fusion(bf16[1,32,256,256]{3,2,1,0:T(8,128)(2,1)} %movie.3), kind=kLoop, calls=%fused_computation | loop fusion | bytes 2097152 | tf_op jit(solution)/shard_map/squeeze | solution.py:780
  21.3 0.7 collective-permute-start
  22.0 0.7 collective-permute-start.1
  22.7 0.0 copy-done.13
  22.7 0.1 multiply_reduce_fusion
  22.9 22.6 %all-to-all-done = bf16[8,32,2176]{2,1,0:T(8,128)(2,1)S(1)} async-done(((bf16[8,32,2176]{2,1,0:T(8,128)(2,1)}), bf16[8,32,2176]{2,1,0:T(8,128)(2,1)S(1)}, u32[]{:S(2)}, u32[]{:S(2)}) %all-to-all-start) | async-done | bytes 1114144 | tf_op jit(solution)/shard_map/all_to_all | solution.py:779
  45.5 5.5 %residual.2 = (bf16[32,256,256]{2,1,0:T(8,128)(2,1)S(1)}, bf16[32,256,256]{2,1,0:T(8,128)(2,1)}, f32[2,4,256]{2,1,0:T(4,128)S(1)}, bf16[4,256,256]{2,1,0:T(8,128)(2,1)}, bf16[4,256,256]{2,1,0:T(8,128)(2,1)}) custom-call(bf16[256,2176]{1,0:T(8,128)(2,1)S(1)} %bitcast.16, bf16[1,32,256,256]{3,2,1,0:T(8,128)(2,1)} %movie.3), custom_call_target="tpu_custom_call" | custom-call | flops 1 | bytes 1 | tf_op jit(solution)/shard_map/residual/pallas_call | solution.py:265
  51.0 0.0 copy-start.1
  51.0 2.0 %copy-done.1 = bf16[32,256,256]{2,1,0:T(8,128)(2,1)} copy-done((bf16[32,256,256]{2,1,0:T(8,128)(2,1)}, bf16[32,256,256]{2,1,0:T(8,128)(2,1)S(1)}, u32[]{:S(2)}) %copy-start.1) | copy-done | bytes 4194328
  53.0 1.9 %collective-permute-start.6 = (bf16[4,256,256]{2,1,0:T(8,128)(2,1)}, bf16[4,256,256]{2,1,0:T(8,128)(2,1)S(1)}, u32[]{:S(2)}, u32[]{:S(2)}) collective-permute-start(bf16[4,256,256]{2,1,0:T(8,128)(2,1)} %get-tuple-element.55), channel_id=1, source_target_pairs={{0,4},{4,8},{8,12},{12,16},{16,20},{20,24},{24,28},{1,5},{5,9},{9,... | collective-permute-start | bytes 1572872 | tf_op jit(solution)/shard_map/ppermute | solution.py:776
  54.9 1.3 collective-permute-start.7
  56.2 0.0 copy-start.2
  56.2 2.2 %copy-done.2 = bf16[32,256,256]{2,1,0:T(8,128)(2,1)S(1)} copy-done((bf16[32,256,256]{2,1,0:T(8,128)(2,1)S(1)}, bf16[32,256,256]{2,1,0:T(8,128)(2,1)}, u32[]{:S(2)}) %copy-start.2) | copy-done | bytes 4194328
  58.4 9.8 %residual.3 = (bf16[32,256,256]{2,1,0:T(8,128)(2,1)S(1)}, bf16[32,256,256]{2,1,0:T(8,128)(2,1)}, f32[6,4,256]{2,1,0:T(4,128)S(1)}, bf16[4,256,256]{2,1,0:T(8,128)(2,1)S(1)}, bf16[4,256,256]{2,1,0:T(8,128)(2,1)S(1)}) custom-call(bf16[256,2176]{1,0:T(8,128)(2,1)S(1)} %bitcast.17, ...), custom_call_target="tpu_custom_call", output_to_operand_aliasing={{0}: (2, {}), {1}: (3, {})} | custom-call | flops 1 | bytes 1 | tf_op jit(solution)/shard_map/residual/pallas_call | solution.py:265
  68.2 0.0 copy-start.3
  68.2 2.0 %copy-done.3 = bf16[32,256,256]{2,1,0:T(8,128)(2,1)} copy-done((bf16[32,256,256]{2,1,0:T(8,128)(2,1)}, bf16[32,256,256]{2,1,0:T(8,128)(2,1)S(1)}, u32[]{:S(2)}) %copy-start.3) | copy-done | bytes 4194328
  70.1 0.0 copy-start.11
  70.1 0.8 copy-done.11
  70.9 0.0 copy-start.12
  70.9 0.8 copy-done.12
  71.8 0.0 collective-permute-done.diag_next
  71.8 0.0 collective-permute-done.1.diag_prev
  71.8 0.0 copy-start.7
  71.8 0.0 copy-start.5
  71.8 1.2 copy-done.5
  73.0 0.0 copy-start
  73.0 1.9 %near.1 = (bf16[8,256,256]{2,1,0:T(8,128)(2,1)S(1)}, bf16[8,256,256]{2,1,0:T(8,128)(2,1)S(1)}, f32[40,256]{1,0:T(8,128)S(1)}) custom-call(bf16[256,2176]{1,0:T(8,128)(2,1)S(1)} %bitcast.18, s32[1]{0:T(128)} %bitcast.6.even, bf16[2,4,256,256]{3,2,1,0:T(8,128)(2,1)S(1)} %copy-done.5, bf16[4,256,256]{2,1,0:T(8,128)(2,1)S(1)} %collective-permute-done.diag_next, ...), custom_call_target="tpu_custom_call" | custom-call | flops 1 | bytes 1 | tf_op jit(solution)/shard_map/near/pallas_call | solution.py:320
  74.9 4.6 %collective-permute-start.2 = (bf16[4,256,256]{2,1,0:T(8,128)(2,1)}, bf16[4,256,256]{2,1,0:T(8,128)(2,1)S(1)}, u32[]{:S(2)}, u32[]{:S(2)}) collective-permute-start(bf16[4,256,256]{2,1,0:T(8,128)(2,1)} %copy-done.12), channel_id=1, source_target_pairs={{0,4},{4,8},{8,12},{12,16},{16,20},{20,24},{24,28},{1,5},{5,9},{9,... | collective-permute-start | bytes 1572872 | tf_op jit(solution)/shard_map/ppermute | solution.py:776
  79.5 1.3 collective-permute-start.3
  80.8 1.3 collective-permute-start.4
  82.1 0.9 collective-permute-done.4.noise_before
  83.0 1.5 %collective-permute-start.5 = (f32[40,256]{1,0:T(8,128)S(1)}, f32[40,256]{1,0:T(8,128)S(1)}, u32[]{:S(2)}, u32[]{:S(2)}) collective-permute-start(f32[40,256]{1,0:T(8,128)S(1)} %get-tuple-element.51.noise), channel_id=1, source_target_pairs={{1,0},{2,1},{3,2},{5,4},{6,5},{7,6},{9,8},{10,9},{11,10},{13,12},{... | collective-permute-start | bytes 122888 | tf_op jit(solution)/shard_map/ppermute | solution.py:797
  84.4 3.6 %collective-permute-done.5.noise_after = f32[40,256]{1,0:T(8,128)S(1)} collective-permute-done((f32[40,256]{1,0:T(8,128)S(1)}, f32[40,256]{1,0:T(8,128)S(1)}, u32[]{:S(2)}, u32[]{:S(2)}) %collective-permute-start.5) | collective-permute-done | bytes 40992 | tf_op jit(solution)/shard_map/ppermute | solution.py:797
  88.0 0.0 copy-start.4
  88.0 2.2 %copy-done.4 = bf16[32,256,256]{2,1,0:T(8,128)(2,1)S(1)} copy-done((bf16[32,256,256]{2,1,0:T(8,128)(2,1)S(1)}, bf16[32,256,256]{2,1,0:T(8,128)(2,1)}, u32[]{:S(2)}) %copy-start.4) | copy-done | bytes 4194328
  90.2 5.3 %weights.1 = (bf16[32,256,256]{2,1,0:T(8,128)(2,1)S(1)}, bf16[3,256,256]{2,1,0:T(8,128)(2,1)S(1)}, bf16[3,256,256]{2,1,0:T(8,128)(2,1)S(1)}) custom-call(bf16[32,256,256]{2,1,0:T(8,128)(2,1)S(1)} %copy-done.4, bf16[8,256,256]{2,1,0:T(8,128)(2,1)S(1)} %get-tuple-element.50.near, f32[40,256]{1,0:T(8,128)S(1)} %get-tuple-element.51.noise, ...), custom_call_target="tpu_custom_call" | custom-call | flops 1 | bytes 1 | tf_op jit(solution)/shard_map/weights/pallas_call | solution.py:399
  95.5 0.0 copy-done.7
  95.5 0.0 copy-done
  95.5 3.9 %annulus_middle.1 = (bf16[1,32,256,256]{3,2,1,0:T(8,128)(2,1)}, f32[256,256]{1,0:T(8,128)S(1)}, f32[256,256]{1,0:T(8,128)S(1)}, f32[256,256]{1,0:T(8,128)S(1)}) custom-call(bf16[32,256,256]{2,1,0:T(8,128)(2,1)S(1)} %copy-done, bf16[8,256,256]{2,1,0:T(8,128)(2,1)S(1)} %get-tuple-element.57.near, bf16[32,256,256]{2,1,0:T(8,128)(2,1)S(1)} %get-tuple-element.52.weight, ...), custom_call_target="tpu_custom_call" | custom-call | flops 1 | bytes 1 | tf_op jit(solution)/shard_map/annulus_middle/pallas_call | solution.py:623
  99.4 0.0 collective-permute-done.6.above
  99.4 0.0 collective-permute-done.7.below
  99.4 2.3 %annulus_mid.1 = (bf16[1,32,256,256]{3,2,1,0:T(8,128)(2,1)}, f32[256,256]{1,0:T(8,128)S(1)}, f32[2,4,256,256]{3,2,1,0:T(8,128)S(1)}, f32[256,128]{1,0:T(8,128)S(1)}, bf16[256,256]{1,0:T(8,128)(2,1)S(1)}) custom-call(bf16[32,256,256]{2,1,0:T(8,128)(2,1)S(1)} %copy-done, ...), custom_call_target="tpu_custom_call", output_to_operand_aliasing={{0}: (5, {})} | custom-call | flops 1073741824 | bytes 5242880 | tf_op jit(solution)/shard_map/annulus_mid/pallas_call | solution.py:623
  101.7 0.0 collective-permute-done.2.above
  101.7 0.0 collective-permute-done.3.below
  101.7 0.0 copy-start.8
  101.7 0.0 copy-start.9
  101.7 0.0 copy-start.10
  101.7 2.2 %annulus_end.1 = (bf16[256,1024]{1,0:T(8,128)(2,1)}, bf16[2,4,256,256]{3,2,1,0:T(8,128)(2,1)S(1)}) custom-call(bf16[32,256,256]{2,1,0:T(8,128)(2,1)S(1)} %copy-done, bf16[4,256,256]{2,1,0:T(8,128)(2,1)S(1)} %collective-permute-done.2.above, bf16[4,256,256]{2,1,0:T(8,128)(2,1)S(1)} %collective-permute-done.3.below, ...), custom_call_target="tpu_custom_call" | custom-call | flops 1 | bytes 1 | tf_op jit(solution)/shard_map/annulus_end/pallas_call | solution.py:656
  104.0 5.8 %all-to-all-start.1 = ((bf16[8,32,1024]{2,1,0:T(8,128)(2,1)}), bf16[8,32,1024]{2,1,0:T(8,128)(2,1)S(1)}, u32[]{:S(2)}, u32[]{:S(2)}) async-start(bf16[8,32,1024]{2,1,0:T(8,128)(2,1)} %bitcast.9), calls=%async_computation.1 | async-start | bytes 1048576 | tf_op jit(solution)/shard_map/all_to_all | solution.py:806
  109.8 0.0 copy-done.8
  109.8 0.0 copy-done.9
  109.8 0.0 copy-done.10
  109.8 0.3 prepare.1
  110.1 0.0 copy-start.6
  110.2 1.0 late_rows.1
  111.2 12.8 %all-to-all-done.1 = bf16[8,32,1024]{2,1,0:T(8,128)(2,1)S(1)} async-done(((bf16[8,32,1024]{2,1,0:T(8,128)(2,1)}), bf16[8,32,1024]{2,1,0:T(8,128)(2,1)S(1)}, u32[]{:S(2)}, u32[]{:S(2)}) %all-to-all-start.1) | async-done | bytes 524320 | tf_op jit(solution)/shard_map/all_to_all | solution.py:806
  123.9 0.0 copy-done.6
  123.9 1.5 %traces.1 = f32[128,256]{1,0:T(8,128)} custom-call(bf16[128,1024]{1,0:T(8,128)(2,1)S(1)} %get-tuple-element.69.hots, f32[4,128,256]{2,1,0:T(8,128)S(1)} %get-tuple-element.70.tables, bf16[128,256]{1,0:T(8,128)(2,1)S(1)} %bitcast.21, bf16[256,1024]{1,0:T(8,128)(2,1)S(1)} %bitcast.19), custom_call_target="tpu_custom_call" | custom-call | flops 1 | bytes 1 | tf_op jit(solution)/shard_map/traces/pallas_call | solution.py:742
  (2 shorter events, 0.0 us)
Async XLA Ops:
  7.2 15.6 %copy-start.13 = (bf16[1,128,1024]{2,1,0:T(8,128)(2,1)S(1)}, bf16[1,128,1024]{2,1,0:T(8,128)(2,1)}, u32[]{:S(2)}) copy-start(bf16[1,128,1024]{2,1,0:T(8,128)(2,1)} %param.9) | copy-start | bytes 786436
  9.6 35.9 %all-to-all-start = ((bf16[8,32,2176]{2,1,0:T(8,128)(2,1)}), bf16[8,32,2176]{2,1,0:T(8,128)(2,1)S(1)}, u32[]{:S(2)}, u32[]{:S(2)}) async-start(bf16[8,32,2176]{2,1,0:T(8,128)(2,1)} %bitcast.24), calls=%async_computation | async-start | bytes 2228224 | tf_op jit(solution)/shard_map/all_to_all | solution.py:779
  16.9 54.9 %all-gather.2.cloned.1.call-start = ((), (), s32[]{:S(2)}) async-start(), calls=%async_computation.2 | async-start | bytes 1572864 | tf_op jit(solution)/shard_map/all_gather | solution.py:767
  21.3 50.5 %collective-permute-start = (bf16[4,256,256]{2,1,0:T(8,128)(2,1)}, bf16[4,256,256]{2,1,0:T(8,128)(2,1)S(1)}, u32[]{:S(2)}, u32[]{:S(2)}) collective-permute-start(bf16[4,256,256]{2,1,0:T(8,128)(2,1)} %get-tuple-element.73), channel_id=1, source_target_pairs={{8,4},{16,12},{24,20},{9,5},{17,13},{25,21},{10,6},{18,14},{26,22}... | collective-permute-start | bytes 1572872 | tf_op jit(solution)/shard_map/ppermute | solution.py:781
  22.0 49.8 %collective-permute-start.1 = (bf16[4,256,256]{2,1,0:T(8,128)(2,1)}, bf16[4,256,256]{2,1,0:T(8,128)(2,1)S(1)}, u32[]{:S(2)}, u32[]{:S(2)}) collective-permute-start(bf16[4,256,256]{2,1,0:T(8,128)(2,1)} %get-tuple-element.72), channel_id=1, source_target_pairs={{4,8},{12,16},{20,24},{5,9},{13,17},{21,25},{6,10},{14,18},{22,26}... | collective-permute-start | bytes 1572872 | tf_op jit(solution)/shard_map/ppermute | solution.py:780
  51.0 2.0 %copy-start.1 = (bf16[32,256,256]{2,1,0:T(8,128)(2,1)}, bf16[32,256,256]{2,1,0:T(8,128)(2,1)S(1)}, u32[]{:S(2)}) copy-start(bf16[32,256,256]{2,1,0:T(8,128)(2,1)S(1)} %get-tuple-element.38.refs_0_) | copy-start | bytes 12582916
  53.0 46.4 %collective-permute-start.6 = (bf16[4,256,256]{2,1,0:T(8,128)(2,1)}, bf16[4,256,256]{2,1,0:T(8,128)(2,1)S(1)}, u32[]{:S(2)}, u32[]{:S(2)}) collective-permute-start(bf16[4,256,256]{2,1,0:T(8,128)(2,1)} %get-tuple-element.55), channel_id=1, source_target_pairs={{0,4},{4,8},{8,12},{12,16},{16,20},{20,24},{24,28},{1,5},{5,9},{9,... | collective-permute-start | bytes 1572872 | tf_op jit(solution)/shard_map/ppermute | solution.py:776
  54.9 44.5 %collective-permute-start.7 = (bf16[4,256,256]{2,1,0:T(8,128)(2,1)}, bf16[4,256,256]{2,1,0:T(8,128)(2,1)S(1)}, u32[]{:S(2)}, u32[]{:S(2)}) collective-permute-start(bf16[4,256,256]{2,1,0:T(8,128)(2,1)} %get-tuple-element.56), channel_id=1, source_target_pairs={{4,0},{8,4},{12,8},{16,12},{20,16},{24,20},{28,24},{5,1},{9,5},{13... | collective-permute-start | bytes 1572872 | tf_op jit(solution)/shard_map/ppermute | solution.py:776
  56.2 2.2 %copy-start.2 = (bf16[32,256,256]{2,1,0:T(8,128)(2,1)S(1)}, bf16[32,256,256]{2,1,0:T(8,128)(2,1)}, u32[]{:S(2)}) copy-start(bf16[32,256,256]{2,1,0:T(8,128)(2,1)} %copy-done.1) | copy-start | bytes 12582916
  68.2 2.0 %copy-start.3 = (bf16[32,256,256]{2,1,0:T(8,128)(2,1)}, bf16[32,256,256]{2,1,0:T(8,128)(2,1)S(1)}, u32[]{:S(2)}) copy-start(bf16[32,256,256]{2,1,0:T(8,128)(2,1)S(1)} %get-tuple-element.49.own) | copy-start | bytes 12582916
  70.1 0.8 copy-start.11
  70.9 0.8 copy-start.12
  71.8 23.7 %copy-start.7 = (f32[1,256]{1,0:T(1,128)S(1)}, f32[1,256]{1,0:T(1,128)}, u32[]{:S(2)}) copy-start(f32[1,256]{1,0:T(1,128)} %gain.3) | copy-start | bytes 3076
  71.8 1.2 copy-start.5
  73.0 22.5 %copy-start = (bf16[32,256,256]{2,1,0:T(8,128)(2,1)S(1)}, bf16[32,256,256]{2,1,0:T(8,128)(2,1)}, u32[]{:S(2)}) copy-start(bf16[32,256,256]{2,1,0:T(8,128)(2,1)} %get-tuple-element.41.own) | copy-start | bytes 12582916
  74.9 26.7 %collective-permute-start.2 = (bf16[4,256,256]{2,1,0:T(8,128)(2,1)}, bf16[4,256,256]{2,1,0:T(8,128)(2,1)S(1)}, u32[]{:S(2)}, u32[]{:S(2)}) collective-permute-start(bf16[4,256,256]{2,1,0:T(8,128)(2,1)} %copy-done.12), channel_id=1, source_target_pairs={{0,4},{4,8},{8,12},{12,16},{16,20},{20,24},{24,28},{1,5},{5,9},{9,... | collective-permute-start | bytes 1572872 | tf_op jit(solution)/shard_map/ppermute | solution.py:776
  79.5 22.2 %collective-permute-start.3 = (bf16[4,256,256]{2,1,0:T(8,128)(2,1)}, bf16[4,256,256]{2,1,0:T(8,128)(2,1)S(1)}, u32[]{:S(2)}, u32[]{:S(2)}) collective-permute-start(bf16[4,256,256]{2,1,0:T(8,128)(2,1)} %copy-done.11), channel_id=1, source_target_pairs={{4,0},{8,4},{12,8},{16,12},{20,16},{24,20},{28,24},{5,1},{9,5},{13... | collective-permute-start | bytes 1572872 | tf_op jit(solution)/shard_map/ppermute | solution.py:776
  80.8 2.2 %collective-permute-start.4 = (f32[40,256]{1,0:T(8,128)S(1)}, f32[40,256]{1,0:T(8,128)S(1)}, u32[]{:S(2)}, u32[]{:S(2)}) collective-permute-start(f32[40,256]{1,0:T(8,128)S(1)} %get-tuple-element.51.noise), channel_id=1, source_target_pairs={{0,1},{1,2},{2,3},{4,5},{5,6},{6,7},{8,9},{9,10},{10,11},{12,13},{... | collective-permute-start | bytes 122888 | tf_op jit(solution)/shard_map/ppermute | solution.py:796
  83.0 5.1 %collective-permute-start.5 = (f32[40,256]{1,0:T(8,128)S(1)}, f32[40,256]{1,0:T(8,128)S(1)}, u32[]{:S(2)}, u32[]{:S(2)}) collective-permute-start(f32[40,256]{1,0:T(8,128)S(1)} %get-tuple-element.51.noise), channel_id=1, source_target_pairs={{1,0},{2,1},{3,2},{5,4},{6,5},{7,6},{9,8},{10,9},{11,10},{13,12},{... | collective-permute-start | bytes 122888 | tf_op jit(solution)/shard_map/ppermute | solution.py:797
  88.0 2.2 %copy-start.4 = (bf16[32,256,256]{2,1,0:T(8,128)(2,1)S(1)}, bf16[32,256,256]{2,1,0:T(8,128)(2,1)}, u32[]{:S(2)}) copy-start(bf16[32,256,256]{2,1,0:T(8,128)(2,1)} %copy-done.3) | copy-start | bytes 12582916
  101.7 8.1 %copy-start.8 = (s32[1,128,1]{1,2,0:T(1,128)S(1)}, s32[1,128,1]{1,2,0:T(1,128)}, u32[]{:S(2)}) copy-start(s32[1,128,1]{1,2,0:T(1,128)} %param.11) | copy-start | bytes 1540
  101.7 8.1 %copy-start.9 = (f32[1,128]{1,0:T(1,128)S(1)}, f32[1,128]{1,0:T(1,128)}, u32[]{:S(2)}) copy-start(f32[1,128]{1,0:T(1,128)} %slow.1) | copy-start | bytes 1540
  101.7 8.1 %copy-start.10 = (f32[1,128]{1,0:T(1,128)S(1)}, f32[1,128]{1,0:T(1,128)}, u32[]{:S(2)}) copy-start(f32[1,128]{1,0:T(1,128)} %fast.1) | copy-start | bytes 1540
  104.0 20.0 %all-to-all-start.1 = ((bf16[8,32,1024]{2,1,0:T(8,128)(2,1)}), bf16[8,32,1024]{2,1,0:T(8,128)(2,1)S(1)}, u32[]{:S(2)}, u32[]{:S(2)}) async-start(bf16[8,32,1024]{2,1,0:T(8,128)(2,1)} %bitcast.9), calls=%async_computation.1 | async-start | bytes 1048576 | tf_op jit(solution)/shard_map/all_to_all | solution.py:806
  110.1 13.8 %copy-start.6 = (bf16[1,128,256]{2,1,0:T(8,128)(2,1)S(1)}, bf16[1,128,256]{2,1,0:T(8,128)(2,1)}, u32[]{:S(2)}) copy-start(bf16[1,128,256]{2,1,0:T(8,128)(2,1)} %param.10) | copy-start | bytes 196612
Sparse Core Ops, SparseCore 0:
  19.2 33.6 all-gather.1

commit v4 on v2

--- a/solution.py
+++ b/solution.py
@@ -776,13 +776,13 @@
     )
     foot_f = footprints[0].astype(F32)
     step = 1.0 / (jnp.sum(foot_f * foot_f, axis=1) + norm_eps)
-    step_row, up, down, noise = lax.optimization_barrier((step[None], up, down, noise))
+    noise_before = lax.ppermute(noise, "plane", plane_up)
+    noise_after = lax.ppermute(noise, "plane", plane_down)
+    step_row, up, down, noise_before = lax.optimization_barrier(
+        (step[None], up, down, noise_before)
+    )
     far = exchange(up, down)
-    noises = (
-        noise,
-        lax.ppermute(noise, "plane", plane_up),
-        lax.ppermute(noise, "plane", plane_down),
-    )
+    noises = (noise, noise_before, noise_after)
     hots, tables = prepare_traces(
         stripe_row, decay_slow, decay_fast, step_row, frames, slots, capacity
     )

time: 116 us -> 129 us (1.11)
  waiting for transfers between devices: 45.7 us -> 59.1 us
    ppermute x3, waiting for transfers between devices: 6.62 us -> 21.8 us  [exchange(): lax.ppermute(up, 'pix', pix_up)]
    ppermute x2, waiting for transfers between devices: 4.44 us -> 2.53 us  [the longest x1 2.52 us: on_device(): noise_after = lax.ppermute(noise, 'plane', plane_down)]
  transfers between devices with their start and end apart: 10 -> 10, of which waited for: 5 -> 5; matrix products, arithmetic and copies ran while one was open for 1% -> 1% of each run, Pallas kernels for 25% -> 21%
where the time goes in v4:
time: 129 us; the launch traced here: 128 us
  waiting for transfers between devices  59.1 us (46%)
  Pallas kernels  35.4 us (27%)
  starting transfers between devices  31.4 us (24%)
  local copies, waits for them, and re-layouts  1.3 us (1%)
    ppermute x3, waiting for transfers between devices, exchange(): lax.ppermute(up, 'pix', pix_up)  21.8 us
    all_to_all x1, waiting for transfers between devices, on_device(): lax.all_to_all(outbox, 'pix', split_axis=0, concat_axis=0, tiled=True)  21.3 us
    pallas_call x2, Pallas kernels, make_residual(): pl.pallas_call(functools.partial(residual_kernel, pick, low, high, earlie...  14.3 us
    all_to_all x1, waiting for transfers between devices, on_device(): lax.all_to_all(gradient, 'pix', split_axis=0, concat_axis=0, tiled=True)  13.4 us
    ppermute x3, starting transfers between devices, exchange(): lax.ppermute(up, 'pix', pix_up)  11 us
    all_to_all x1, starting transfers between devices, on_device(): lax.all_to_all(outbox, 'pix', split_axis=0, concat_axis=0, tiled=True)  7.29 us
    all_to_all x1, starting transfers between devices, on_device(): lax.all_to_all(gradient, 'pix', split_axis=0, concat_axis=0, tiled=True)  6.41 us
    pallas_call x2, Pallas kernels, call(): pl.pallas_call(kernel, in_specs=specs, out_specs=[HBM] + [VMEM] * (len(ou...  6.39 us
  transfers between devices with their start and end apart: 10, of which 5 were waited for; matrix products, arithmetic and copies ran while one was open for 1% of the time, Pallas kernels for 21%

profile of v4, /device:TPU:0, one launch (start us, length us, event | category | flops | bytes accessed | tf_op | source)
XLA Modules:
  0.0 128.1 jit_solution(12797154037773350927)
XLA Ops:
  0.6 0.0 copy-start.6
  0.6 2.4 %outbox.1 = bf16[256,2176]{1,0:T(8,128)(2,1)} custom-call(s32[1,128]{1,0:T(1,128)} %bitcast.21, s32[1,128]{1,0:T(1,128)} %refs_1_.1, bf16[128,1024]{1,0:T(8,128)(2,1)} %bitcast.24, bf16[128,256]{1,0:T(8,128)(2,1)} %bitcast.19), custom_call_target="tpu_custom_call" | custom-call | flops 1 | bytes 1 | tf_op jit(solution)/shard_map/outbox/pallas_call | solution.py:112
  3.0 7.3 %all-to-all-start = ((bf16[8,32,2176]{2,1,0:T(8,128)(2,1)}), bf16[8,32,2176]{2,1,0:T(8,128)(2,1)S(1)}, u32[]{:S(2)}, u32[]{:S(2)}) async-start(bf16[8,32,2176]{2,1,0:T(8,128)(2,1)} %bitcast.23), calls=%async_computation | async-start | bytes 2228224 | tf_op jit(solution)/shard_map/all_to_all | solution.py:767
  10.3 1.3 slice_bitcast_fusion
  11.6 1.3 %collective-permute-start = (bf16[4,256,256]{2,1,0:T(8,128)(2,1)S(1)}, bf16[4,256,256]{2,1,0:T(8,128)(2,1)S(1)}, u32[]{:S(2)}, u32[]{:S(2)}) collective-permute-start(bf16[4,256,256]{2,1,0:T(8,128)(2,1)S(1)} %get-tuple-element.73), channel_id=1, source_target_pairs={{4,0},{8,4},{12,8},{16,12},{20,16},{24,20},{28,24},{5,1},{9,5},{13... | collective-permute-start | bytes 1572872 | tf_op jit(solution)/shard_map/ppermute | solution.py:764
  12.9 4.6 %collective-permute-start.1 = (bf16[4,256,256]{2,1,0:T(8,128)(2,1)S(1)}, bf16[4,256,256]{2,1,0:T(8,128)(2,1)S(1)}, u32[]{:S(2)}, u32[]{:S(2)}) collective-permute-start(bf16[4,256,256]{2,1,0:T(8,128)(2,1)S(1)} %get-tuple-element.72), channel_id=1, source_target_pairs={{0,4},{4,8},{8,12},{12,16},{16,20},{20,24},{24,28},{1,5},{5,9},{9,... | collective-permute-start | bytes 1572872 | tf_op jit(solution)/shard_map/ppermute | solution.py:764
  17.5 0.0 copy-done.6
  17.5 0.1 multiply_reduce_fusion
  17.6 21.3 %all-to-all-done = bf16[8,32,2176]{2,1,0:T(8,128)(2,1)S(1)} async-done(((bf16[8,32,2176]{2,1,0:T(8,128)(2,1)}), bf16[8,32,2176]{2,1,0:T(8,128)(2,1)S(1)}, u32[]{:S(2)}, u32[]{:S(2)}) %all-to-all-start) | async-done | bytes 1114144 | tf_op jit(solution)/shard_map/all_to_all | solution.py:767
  39.0 4.5 %residual.2 = (bf16[32,256,256]{2,1,0:T(8,128)(2,1)S(1)}, bf16[32,256,256]{2,1,0:T(8,128)(2,1)}, f32[2,4,256]{2,1,0:T(4,128)S(1)}, bf16[4,256,256]{2,1,0:T(8,128)(2,1)S(1)}, bf16[4,256,256]{2,1,0:T(8,128)(2,1)S(1)}) custom-call(bf16[256,2176]{1,0:T(8,128)(2,1)S(1)} %bitcast.15, bf16[1,32,256,256]{3,2,1,0:T(8,128)(2,1)} %movie.3), custom_call_target="tpu_custom_call" | custom-call | flops 1 | bytes 1 | tf_op jit(solution)/shard_map/residual/pallas_call | solution.py:265
  43.5 9.8 %residual.3 = (bf16[32,256,256]{2,1,0:T(8,128)(2,1)S(1)}, bf16[32,256,256]{2,1,0:T(8,128)(2,1)}, f32[6,4,256]{2,1,0:T(4,128)S(1)}, bf16[4,256,256]{2,1,0:T(8,128)(2,1)S(1)}, bf16[4,256,256]{2,1,0:T(8,128)(2,1)S(1)}) custom-call(bf16[256,2176]{1,0:T(8,128)(2,1)S(1)} %bitcast.16, ...), custom_call_target="tpu_custom_call", output_to_operand_aliasing={{0}: (2, {}), {1}: (3, {})} | custom-call | flops 1 | bytes 1 | tf_op jit(solution)/shard_map/residual/pallas_call | solution.py:265
  53.3 0.0 copy-start
  53.3 0.0 copy-start.2
  53.3 0.0 collective-permute-done.movie_next
  53.3 0.0 collective-permute-done.1.movie_prev
  53.3 1.9 %near.1 = (bf16[8,256,256]{2,1,0:T(8,128)(2,1)S(1)}, bf16[8,256,256]{2,1,0:T(8,128)(2,1)S(1)}, f32[40,256]{1,0:T(8,128)S(1)}) custom-call(bf16[256,2176]{1,0:T(8,128)(2,1)S(1)} %bitcast.17, bf16[4,256,256]{2,1,0:T(8,128)(2,1)S(1)} %collective-permute-done.movie_next, bf16[4,256,256]{2,1,0:T(8,128)(2,1)S(1)} %collective-permute-done.1.movie_prev, ...), custom_call_target="tpu_custom_call" | custom-call | flops 1 | bytes 1 | tf_op jit(solution)/shard_map/near/pallas_call | solution.py:316
  55.2 1.3 %collective-permute-start.2 = (f32[40,256]{1,0:T(8,128)S(1)}, f32[40,256]{1,0:T(8,128)S(1)}, u32[]{:S(2)}, u32[]{:S(2)}) collective-permute-start(f32[40,256]{1,0:T(8,128)S(1)} %get-tuple-element.46.noise), channel_id=1, source_target_pairs={{0,1},{1,2},{2,3},{4,5},{5,6},{6,7},{8,9},{9,10},{10,11},{12,13},{... | collective-permute-start | bytes 122888 | tf_op jit(solution)/shard_map/ppermute | solution.py:779
  56.5 1.9 %collective-permute-start.6 = (bf16[4,256,256]{2,1,0:T(8,128)(2,1)S(1)}, bf16[4,256,256]{2,1,0:T(8,128)(2,1)S(1)}, u32[]{:S(2)}, u32[]{:S(2)}) collective-permute-start(bf16[4,256,256]{2,1,0:T(8,128)(2,1)S(1)} %get-tuple-element.55), channel_id=1, source_target_pairs={{0,4},{4,8},{8,12},{12,16},{16,20},{20,24},{24,28},{1,5},{5,9},{9,... | collective-permute-start | bytes 1572872 | tf_op jit(solution)/shard_map/ppermute | solution.py:764
  58.4 1.3 %collective-permute-start.7 = (bf16[4,256,256]{2,1,0:T(8,128)(2,1)S(1)}, bf16[4,256,256]{2,1,0:T(8,128)(2,1)S(1)}, u32[]{:S(2)}, u32[]{:S(2)}) collective-permute-start(bf16[4,256,256]{2,1,0:T(8,128)(2,1)S(1)} %get-tuple-element.56), channel_id=1, source_target_pairs={{4,0},{8,4},{12,8},{16,12},{20,16},{24,20},{28,24},{5,1},{9,5},{13... | collective-permute-start | bytes 1572872 | tf_op jit(solution)/shard_map/ppermute | solution.py:764
  59.7 0.0 collective-permute-done.2.noise_before
  59.7 4.6 %collective-permute-start.3 = (bf16[4,256,256]{2,1,0:T(8,128)(2,1)S(1)}, bf16[4,256,256]{2,1,0:T(8,128)(2,1)S(1)}, u32[]{:S(2)}, u32[]{:S(2)}) collective-permute-start(bf16[4,256,256]{2,1,0:T(8,128)(2,1)S(1)} %get-tuple-element.47), channel_id=1, source_target_pairs={{0,4},{4,8},{8,12},{12,16},{16,20},{20,24},{24,28},{1,5},{5,9},{9,... | collective-permute-start | bytes 1572872 | tf_op jit(solution)/shard_map/ppermute | solution.py:764
  64.3 1.3 %collective-permute-start.4 = (bf16[4,256,256]{2,1,0:T(8,128)(2,1)S(1)}, bf16[4,256,256]{2,1,0:T(8,128)(2,1)S(1)}, u32[]{:S(2)}, u32[]{:S(2)}) collective-permute-start(bf16[4,256,256]{2,1,0:T(8,128)(2,1)S(1)} %get-tuple-element.48), channel_id=1, source_target_pairs={{4,0},{8,4},{12,8},{16,12},{20,16},{24,20},{28,24},{5,1},{9,5},{13... | collective-permute-start | bytes 1572872 | tf_op jit(solution)/shard_map/ppermute | solution.py:764
  65.6 1.5 %collective-permute-start.5 = (f32[40,256]{1,0:T(8,128)S(1)}, f32[40,256]{1,0:T(8,128)S(1)}, u32[]{:S(2)}, u32[]{:S(2)}) collective-permute-start(f32[40,256]{1,0:T(8,128)S(1)} %get-tuple-element.46.noise), channel_id=1, source_target_pairs={{1,0},{2,1},{3,2},{5,4},{6,5},{7,6},{9,8},{10,9},{11,10},{13,12},{... | collective-permute-start | bytes 122888 | tf_op jit(solution)/shard_map/ppermute | solution.py:780
  67.1 2.5 %collective-permute-done.5.noise_after = f32[40,256]{1,0:T(8,128)S(1)} collective-permute-done((f32[40,256]{1,0:T(8,128)S(1)}, f32[40,256]{1,0:T(8,128)S(1)}, u32[]{:S(2)}, u32[]{:S(2)}) %collective-permute-start.5) | collective-permute-done | bytes 40992 | tf_op jit(solution)/shard_map/ppermute | solution.py:780
  69.6 5.2 %weights.1 = (bf16[32,256,256]{2,1,0:T(8,128)(2,1)S(1)}, bf16[3,256,256]{2,1,0:T(8,128)(2,1)S(1)}, bf16[3,256,256]{2,1,0:T(8,128)(2,1)S(1)}) custom-call(bf16[32,256,256]{2,1,0:T(8,128)(2,1)S(1)} %get-tuple-element.49.own, bf16[8,256,256]{2,1,0:T(8,128)(2,1)S(1)} %get-tuple-element.50.near, f32[40,256]{1,0:T(8,128)S(1)} %get-tuple-element.46.noise, ...), custom_call_target="tpu_custom_call" | custom-call | flops 1 | bytes 1 | tf_op jit(solution)/shard_map/weights/pallas_call | solution.py:394
  74.9 0.0 copy-done
  74.9 0.0 copy-done.2
  74.9 4.0 %annulus_middle.1 = (bf16[1,32,256,256]{3,2,1,0:T(8,128)(2,1)}, f32[256,256]{1,0:T(8,128)S(1)}, f32[256,256]{1,0:T(8,128)S(1)}, f32[256,256]{1,0:T(8,128)S(1)}) custom-call(bf16[32,256,256]{2,1,0:T(8,128)(2,1)S(1)} %copy-done, bf16[8,256,256]{2,1,0:T(8,128)(2,1)S(1)} %get-tuple-element.57.near, bf16[32,256,256]{2,1,0:T(8,128)(2,1)S(1)} %get-tuple-element.52.weight, ...), custom_call_target="tpu_custom_call" | custom-call | flops 1 | bytes 1 | tf_op jit(solution)/shard_map/annulus_middle/pallas_call | solution.py:618
  78.9 12.9 %collective-permute-done.6.above = bf16[4,256,256]{2,1,0:T(8,128)(2,1)S(1)} collective-permute-done((bf16[4,256,256]{2,1,0:T(8,128)(2,1)S(1)}, bf16[4,256,256]{2,1,0:T(8,128)(2,1)S(1)}, u32[]{:S(2)}, u32[]{:S(2)}) %collective-permute-start.6) | collective-permute-done | bytes 524320 | tf_op jit(solution)/shard_map/ppermute | solution.py:764
  91.9 0.0 collective-permute-done.7.below
  91.9 2.4 %annulus_mid.1 = (bf16[1,32,256,256]{3,2,1,0:T(8,128)(2,1)}, f32[256,256]{1,0:T(8,128)S(1)}, f32[2,4,256,256]{3,2,1,0:T(8,128)S(1)}, f32[256,128]{1,0:T(8,128)S(1)}, bf16[256,256]{1,0:T(8,128)(2,1)S(1)}) custom-call(bf16[32,256,256]{2,1,0:T(8,128)(2,1)S(1)} %copy-done, ...), custom_call_target="tpu_custom_call", output_to_operand_aliasing={{0}: (5, {})} | custom-call | flops 1073741824 | bytes 5242880 | tf_op jit(solution)/shard_map/annulus_mid/pallas_call | solution.py:618
  94.2 8.9 %collective-permute-done.3.above = bf16[4,256,256]{2,1,0:T(8,128)(2,1)S(1)} collective-permute-done((bf16[4,256,256]{2,1,0:T(8,128)(2,1)S(1)}, bf16[4,256,256]{2,1,0:T(8,128)(2,1)S(1)}, u32[]{:S(2)}, u32[]{:S(2)}) %collective-permute-start.3) | collective-permute-done | bytes 524320 | tf_op jit(solution)/shard_map/ppermute | solution.py:764
  103.1 0.0 collective-permute-done.4.below
  103.1 0.0 copy-start.3
  103.1 0.0 copy-start.4
  103.1 0.0 copy-start.5
  103.1 2.3 %annulus_end.1 = (bf16[256,1024]{1,0:T(8,128)(2,1)}, bf16[2,4,256,256]{3,2,1,0:T(8,128)(2,1)S(1)}) custom-call(bf16[32,256,256]{2,1,0:T(8,128)(2,1)S(1)} %copy-done, bf16[4,256,256]{2,1,0:T(8,128)(2,1)S(1)} %collective-permute-done.3.above, bf16[4,256,256]{2,1,0:T(8,128)(2,1)S(1)} %collective-permute-done.4.below, ...), custom_call_target="tpu_custom_call" | custom-call | flops 1 | bytes 1 | tf_op jit(solution)/shard_map/annulus_end/pallas_call | solution.py:651
  105.4 6.4 %all-to-all-start.1 = ((bf16[8,32,1024]{2,1,0:T(8,128)(2,1)}), bf16[8,32,1024]{2,1,0:T(8,128)(2,1)S(1)}, u32[]{:S(2)}, u32[]{:S(2)}) async-start(bf16[8,32,1024]{2,1,0:T(8,128)(2,1)} %bitcast.8), calls=%async_computation.1 | async-start | bytes 1048576 | tf_op jit(solution)/shard_map/all_to_all | solution.py:793
  111.8 0.0 copy-done.3
  111.8 0.0 copy-done.4
  111.8 0.0 copy-done.5
  111.9 0.3 prepare.1
  112.2 0.0 copy-start.1
  112.2 1.0 late_rows.1
  113.2 13.4 %all-to-all-done.1 = bf16[8,32,1024]{2,1,0:T(8,128)(2,1)S(1)} async-done(((bf16[8,32,1024]{2,1,0:T(8,128)(2,1)}), bf16[8,32,1024]{2,1,0:T(8,128)(2,1)S(1)}, u32[]{:S(2)}, u32[]{:S(2)}) %all-to-all-start.1) | async-done | bytes 524320 | tf_op jit(solution)/shard_map/all_to_all | solution.py:793
  126.6 0.0 copy-done.1
  126.6 1.5 %traces.1 = f32[128,256]{1,0:T(8,128)} custom-call(bf16[128,1024]{1,0:T(8,128)(2,1)S(1)} %get-tuple-element.69.hots, f32[4,128,256]{2,1,0:T(8,128)S(1)} %get-tuple-element.70.tables, bf16[128,256]{1,0:T(8,128)(2,1)S(1)} %bitcast.20, bf16[256,1024]{1,0:T(8,128)(2,1)S(1)} %bitcast.18), custom_call_target="tpu_custom_call" | custom-call | flops 1 | bytes 1 | tf_op jit(solution)/shard_map/traces/pallas_call | solution.py:737
  (1 shorter events, 0.0 us)
Async XLA Ops:
  0.6 16.9 %copy-start.6 = (bf16[1,128,1024]{2,1,0:T(8,128)(2,1)S(1)}, bf16[1,128,1024]{2,1,0:T(8,128)(2,1)}, u32[]{:S(2)}) copy-start(bf16[1,128,1024]{2,1,0:T(8,128)(2,1)} %param.9) | copy-start | bytes 786436
  3.0 35.9 %all-to-all-start = ((bf16[8,32,2176]{2,1,0:T(8,128)(2,1)}), bf16[8,32,2176]{2,1,0:T(8,128)(2,1)S(1)}, u32[]{:S(2)}, u32[]{:S(2)}) async-start(bf16[8,32,2176]{2,1,0:T(8,128)(2,1)} %bitcast.23), calls=%async_computation | async-start | bytes 2228224 | tf_op jit(solution)/shard_map/all_to_all | solution.py:767
  11.6 41.7 %collective-permute-start = (bf16[4,256,256]{2,1,0:T(8,128)(2,1)S(1)}, bf16[4,256,256]{2,1,0:T(8,128)(2,1)S(1)}, u32[]{:S(2)}, u32[]{:S(2)}) collective-permute-start(bf16[4,256,256]{2,1,0:T(8,128)(2,1)S(1)} %get-tuple-element.73), channel_id=1, source_target_pairs={{4,0},{8,4},{12,8},{16,12},{20,16},{24,20},{28,24},{5,1},{9,5},{13... | collective-permute-start | bytes 1572872 | tf_op jit(solution)/shard_map/ppermute | solution.py:764
  12.9 40.4 %collective-permute-start.1 = (bf16[4,256,256]{2,1,0:T(8,128)(2,1)S(1)}, bf16[4,256,256]{2,1,0:T(8,128)(2,1)S(1)}, u32[]{:S(2)}, u32[]{:S(2)}) collective-permute-start(bf16[4,256,256]{2,1,0:T(8,128)(2,1)S(1)} %get-tuple-element.72), channel_id=1, source_target_pairs={{0,4},{4,8},{8,12},{12,16},{16,20},{20,24},{24,28},{1,5},{5,9},{9,... | collective-permute-start | bytes 1572872 | tf_op jit(solution)/shard_map/ppermute | solution.py:764
  53.3 21.6 %copy-start = (bf16[32,256,256]{2,1,0:T(8,128)(2,1)S(1)}, bf16[32,256,256]{2,1,0:T(8,128)(2,1)}, u32[]{:S(2)}) copy-start(bf16[32,256,256]{2,1,0:T(8,128)(2,1)} %get-tuple-element.41.own) | copy-start | bytes 12582916
  53.3 21.6 %copy-start.2 = (f32[1,256]{1,0:T(1,128)S(1)}, f32[1,256]{1,0:T(1,128)}, u32[]{:S(2)}) copy-start(f32[1,256]{1,0:T(1,128)} %gain.3) | copy-start | bytes 3076
  55.2 4.5 %collective-permute-start.2 = (f32[40,256]{1,0:T(8,128)S(1)}, f32[40,256]{1,0:T(8,128)S(1)}, u32[]{:S(2)}, u32[]{:S(2)}) collective-permute-start(f32[40,256]{1,0:T(8,128)S(1)} %get-tuple-element.46.noise), channel_id=1, source_target_pairs={{0,1},{1,2},{2,3},{4,5},{5,6},{6,7},{8,9},{9,10},{10,11},{12,13},{... | collective-permute-start | bytes 122888 | tf_op jit(solution)/shard_map/ppermute | solution.py:779
  56.5 35.3 %collective-permute-start.6 = (bf16[4,256,256]{2,1,0:T(8,128)(2,1)S(1)}, bf16[4,256,256]{2,1,0:T(8,128)(2,1)S(1)}, u32[]{:S(2)}, u32[]{:S(2)}) collective-permute-start(bf16[4,256,256]{2,1,0:T(8,128)(2,1)S(1)} %get-tuple-element.55), channel_id=1, source_target_pairs={{0,4},{4,8},{8,12},{12,16},{16,20},{20,24},{24,28},{1,5},{5,9},{9,... | collective-permute-start | bytes 1572872 | tf_op jit(solution)/shard_map/ppermute | solution.py:764
  58.4 33.4 %collective-permute-start.7 = (bf16[4,256,256]{2,1,0:T(8,128)(2,1)S(1)}, bf16[4,256,256]{2,1,0:T(8,128)(2,1)S(1)}, u32[]{:S(2)}, u32[]{:S(2)}) collective-permute-start(bf16[4,256,256]{2,1,0:T(8,128)(2,1)S(1)} %get-tuple-element.56), channel_id=1, source_target_pairs={{4,0},{8,4},{12,8},{16,12},{20,16},{24,20},{28,24},{5,1},{9,5},{13... | collective-permute-start | bytes 1572872 | tf_op jit(solution)/shard_map/ppermute | solution.py:764
  59.7 43.4 %collective-permute-start.3 = (bf16[4,256,256]{2,1,0:T(8,128)(2,1)S(1)}, bf16[4,256,256]{2,1,0:T(8,128)(2,1)S(1)}, u32[]{:S(2)}, u32[]{:S(2)}) collective-permute-start(bf16[4,256,256]{2,1,0:T(8,128)(2,1)S(1)} %get-tuple-element.47), channel_id=1, source_target_pairs={{0,4},{4,8},{8,12},{12,16},{16,20},{20,24},{24,28},{1,5},{5,9},{9,... | collective-permute-start | bytes 1572872 | tf_op jit(solution)/shard_map/ppermute | solution.py:764
  64.3 38.8 %collective-permute-start.4 = (bf16[4,256,256]{2,1,0:T(8,128)(2,1)S(1)}, bf16[4,256,256]{2,1,0:T(8,128)(2,1)S(1)}, u32[]{:S(2)}, u32[]{:S(2)}) collective-permute-start(bf16[4,256,256]{2,1,0:T(8,128)(2,1)S(1)} %get-tuple-element.48), channel_id=1, source_target_pairs={{4,0},{8,4},{12,8},{16,12},{20,16},{24,20},{28,24},{5,1},{9,5},{13... | collective-permute-start | bytes 1572872 | tf_op jit(solution)/shard_map/ppermute | solution.py:764
  65.6 4.0 %collective-permute-start.5 = (f32[40,256]{1,0:T(8,128)S(1)}, f32[40,256]{1,0:T(8,128)S(1)}, u32[]{:S(2)}, u32[]{:S(2)}) collective-permute-start(f32[40,256]{1,0:T(8,128)S(1)} %get-tuple-element.46.noise), channel_id=1, source_target_pairs={{1,0},{2,1},{3,2},{5,4},{6,5},{7,6},{9,8},{10,9},{11,10},{13,12},{... | collective-permute-start | bytes 122888 | tf_op jit(solution)/shard_map/ppermute | solution.py:780
  103.1 8.7 %copy-start.3 = (s32[1,128,1]{1,2,0:T(1,128)S(1)}, s32[1,128,1]{1,2,0:T(1,128)}, u32[]{:S(2)}) copy-start(s32[1,128,1]{1,2,0:T(1,128)} %param.11) | copy-start | bytes 1540
  103.1 8.7 %copy-start.4 = (f32[1,128]{1,0:T(1,128)S(1)}, f32[1,128]{1,0:T(1,128)}, u32[]{:S(2)}) copy-start(f32[1,128]{1,0:T(1,128)} %slow.1) | copy-start | bytes 1540
  103.1 8.8 %copy-start.5 = (f32[1,128]{1,0:T(1,128)S(1)}, f32[1,128]{1,0:T(1,128)}, u32[]{:S(2)}) copy-start(f32[1,128]{1,0:T(1,128)} %fast.1) | copy-start | bytes 1540
  105.4 21.2 %all-to-all-start.1 = ((bf16[8,32,1024]{2,1,0:T(8,128)(2,1)}), bf16[8,32,1024]{2,1,0:T(8,128)(2,1)S(1)}, u32[]{:S(2)}, u32[]{:S(2)}) async-start(bf16[8,32,1024]{2,1,0:T(8,128)(2,1)} %bitcast.8), calls=%async_computation.1 | async-start | bytes 1048576 | tf_op jit(solution)/shard_map/all_to_all | solution.py:793
  112.2 14.4 %copy-start.1 = (bf16[1,128,256]{2,1,0:T(8,128)(2,1)S(1)}, bf16[1,128,256]{2,1,0:T(8,128)(2,1)}, u32[]{:S(2)}) copy-start(bf16[1,128,256]{2,1,0:T(8,128)(2,1)} %param.10) | copy-start | bytes 196612

commit v5 on v2

--- a/solution.py
+++ b/solution.py
@@ -76,8 +76,6 @@
         jnp.where(place + shift == slot, 1.0, 0.0).astype(BF16)
         for shift in (0, capacity, -capacity)
     ]
-    for copy in copies[2:]:
-        copy.wait()
     leaving = []
 
     def leave(start, width):
@@ -88,17 +86,24 @@
         copy.start()
         leaving.append(copy)
 
-    for k, (hot, first, width) in enumerate(
-        zip(hots, (0, 0, tiles - edge), (tiles, edge, edge))
+    copies[3].wait()
+    for k, hot in enumerate(hots):
+        outbox[:, k * frames : (k + 1) * frames] = dot(hot, traces[...]).astype(BF16)
+        lefts = jnp.where(lane == k, dot(hot, left), lefts)
+    outbox[:, outbox.shape[1] - LANES :] = lefts.astype(BF16)
+    leave(0, at)
+    copies[2].wait()
+    half = tiles // 2
+    for hot, first, width in (
+        (hots[0], 0, half),
+        (hots[0], half, half),
+        (hots[1], 0, edge),
+        (hots[2], tiles - edge, edge),
     ):
         outbox[:, at : at + width] = dot(hot, foot[:, first : first + width]).astype(BF16)
-        if k == 0:
+        if width == half:
             leave(at, width)
-        outbox[:, k * frames : (k + 1) * frames] = dot(hot, traces[...]).astype(BF16)
-        lefts = jnp.where(lane == k, dot(hot, left), lefts)
         at += width
-    leave(0, 3 * frames)
-    outbox[:, at:] = lefts.astype(BF16)
     leave(3 * frames + tiles, outbox.shape[1] - 3 * frames - tiles)
     for copy in leaving:
         copy.wait()
@@ -115,7 +120,7 @@
         out_specs=HBM,
         out_shape=jax.ShapeDtypeStruct((slots, width), BF16),
         scratch_shapes=[pltpu.VMEM(a.shape, a.dtype) for a in args]
-        + [pltpu.VMEM((slots, width), BF16), pltpu.SemaphoreType.DMA((len(args) + 3,))],
+        + [pltpu.VMEM((slots, width), BF16), pltpu.SemaphoreType.DMA((len(args) + 4,))],
         compiler_params=params(56),
         cost_estimate=COST,
         name="outbox",
@@ -551,7 +556,8 @@
 
 
 def end_kernel(
-    own, above, below, weight, weight_next, weight_prev, total, base, gain, band, gradient, late
+    own, above, below, weight, weight_next, weight_prev, total, base, gain, band, result, late,
+    gradient, sems,
 ):
     rows, cols, frames = own.shape
     low, high = 0, rows // PER - 1
@@ -577,16 +583,24 @@
             column = add_rows(column, [row])
         dets.append(mine)
     low_dets, high_dets = dets
-    grown = grow(grow(total[...], weight, low, low_dets), weight, high, high_dets)
     edges = ((2, weight_next, high_dets[PER - GR :]), (3, weight_prev, low_dets[:GR]))
     for at, edge, parts in edges:
         value = dot(
             jnp.concatenate([edge[a] for a in range(GR)], axis=1), jnp.concatenate(parts, axis=0)
         )
         gradient[:, at * frames : (at + 1) * frames] = value.astype(BF16)
+    copies = [
+        pltpu.make_async_copy(gradient.at[:, lanes], result.at[:, lanes], sems.at[k])
+        for k, lanes in enumerate((pl.ds(2 * frames, 2 * frames), pl.ds(0, 2 * frames)))
+    ]
+    copies[0].start()
+    grown = grow(grow(total[...], weight, low, low_dets), weight, high, high_dets)
     coarse = grown.astype(BF16)
     gradient[:, 0:frames] = coarse
     gradient[:, frames : 2 * frames] = (grown - coarse.astype(F32)).astype(BF16)
+    copies[1].start()
+    for copy in copies:
+        copy.wait()
 
 
 def late_kernel(late, before, background, sems):
@@ -651,7 +665,12 @@
     gradient, late = pl.pallas_call(
         end_kernel,
         in_specs=[VMEM] * len(args),
+        out_specs=[HBM, VMEM],
         out_shape=(gradient, jax.ShapeDtypeStruct((2, PER, cols, frames), BF16)),
+        scratch_shapes=[
+            pltpu.VMEM((slots, 4 * frames), BF16),
+            pltpu.SemaphoreType.DMA((2,)),
+        ],
         compiler_params=params(),
         cost_estimate=COST,
         name="annulus_end",

time: 116 us -> 116 us (level)
  no operation moved by 1% of the time
where the time goes in v5:
time: 116 us; the launch traced here: 115 us
  waiting for transfers between devices  45.7 us (39%)
  Pallas kernels  35.6 us (31%)
  starting transfers between devices  31.7 us (27%)
  local copies, waits for them, and re-layouts  1.3 us (1%)
    all_to_all x1, waiting for transfers between devices, on_device(): lax.all_to_all(outbox, 'pix', split_axis=0, concat_axis=0, tiled=True)  21.3 us
    pallas_call x2, Pallas kernels, make_residual(): pl.pallas_call(functools.partial(residual_kernel, pick, low, high, earlie...  14.4 us
    all_to_all x1, waiting for transfers between devices, on_device(): lax.all_to_all(gradient, 'pix', split_axis=0, concat_axis=0, tiled=True)  13.3 us
    ppermute x3, starting transfers between devices, exchange(): lax.ppermute(up, 'pix', pix_up)  11 us
    all_to_all x1, starting transfers between devices, on_device(): lax.all_to_all(outbox, 'pix', split_axis=0, concat_axis=0, tiled=True)  7.29 us
    all_to_all x1, starting transfers between devices, on_device(): lax.all_to_all(gradient, 'pix', split_axis=0, concat_axis=0, tiled=True)  6.74 us
    ppermute x3, waiting for transfers between devices, exchange(): lax.ppermute(up, 'pix', pix_up)  6.62 us
    pallas_call x2, Pallas kernels, call(): pl.pallas_call(kernel, in_specs=specs, out_specs=[HBM] + [VMEM] * (len(ou...  6.38 us
  transfers between devices with their start and end apart: 10, of which 5 were waited for; matrix products, arithmetic and copies ran while one was open for 1% of the time, Pallas kernels for 25%

profile of v5, /device:TPU:0, one launch (start us, length us, event | category | flops | bytes accessed | tf_op | source)
XLA Modules:
  0.0 115.3 jit_solution(4684584718586679194)
XLA Ops:
  0.6 0.0 copy-start.6
  0.6 2.4 %outbox.1 = bf16[256,2176]{1,0:T(8,128)(2,1)} custom-call(s32[1,128]{1,0:T(1,128)} %bitcast.21, s32[1,128]{1,0:T(1,128)} %refs_1_.1, bf16[128,1024]{1,0:T(8,128)(2,1)} %bitcast.24, bf16[128,256]{1,0:T(8,128)(2,1)} %bitcast.19), custom_call_target="tpu_custom_call" | custom-call | flops 1 | bytes 1 | tf_op jit(solution)/shard_map/outbox/pallas_call | solution.py:117
  3.1 7.3 %all-to-all-start = ((bf16[8,32,2176]{2,1,0:T(8,128)(2,1)}), bf16[8,32,2176]{2,1,0:T(8,128)(2,1)S(1)}, u32[]{:S(2)}, u32[]{:S(2)}) async-start(bf16[8,32,2176]{2,1,0:T(8,128)(2,1)} %bitcast.23), calls=%async_computation | async-start | bytes 2228224 | tf_op jit(solution)/shard_map/all_to_all | solution.py:786
  10.4 1.3 %slice_bitcast_fusion = (bf16[4,256,256]{2,1,0:T(8,128)(2,1)S(1)}, bf16[4,256,256]{2,1,0:T(8,128)(2,1)S(1)}) fusion(bf16[1,32,256,256]{3,2,1,0:T(8,128)(2,1)} %movie.3), kind=kLoop, calls=%fused_computation | loop fusion | bytes 2097152 | tf_op jit(solution)/shard_map/squeeze | solution.py:787
  11.6 1.3 %collective-permute-start = (bf16[4,256,256]{2,1,0:T(8,128)(2,1)S(1)}, bf16[4,256,256]{2,1,0:T(8,128)(2,1)S(1)}, u32[]{:S(2)}, u32[]{:S(2)}) collective-permute-start(bf16[4,256,256]{2,1,0:T(8,128)(2,1)S(1)} %get-tuple-element.73), channel_id=1, source_target_pairs={{4,0},{8,4},{12,8},{16,12},{20,16},{24,20},{28,24},{5,1},{9,5},{13... | collective-permute-start | bytes 1572872 | tf_op jit(solution)/shard_map/ppermute | solution.py:783
  12.9 4.6 %collective-permute-start.1 = (bf16[4,256,256]{2,1,0:T(8,128)(2,1)S(1)}, bf16[4,256,256]{2,1,0:T(8,128)(2,1)S(1)}, u32[]{:S(2)}, u32[]{:S(2)}) collective-permute-start(bf16[4,256,256]{2,1,0:T(8,128)(2,1)S(1)} %get-tuple-element.72), channel_id=1, source_target_pairs={{0,4},{4,8},{8,12},{12,16},{16,20},{20,24},{24,28},{1,5},{5,9},{9,... | collective-permute-start | bytes 1572872 | tf_op jit(solution)/shard_map/ppermute | solution.py:783
  17.5 0.0 copy-done.6
  17.5 0.1 multiply_reduce_fusion
  17.7 21.3 %all-to-all-done = bf16[8,32,2176]{2,1,0:T(8,128)(2,1)S(1)} async-done(((bf16[8,32,2176]{2,1,0:T(8,128)(2,1)}), bf16[8,32,2176]{2,1,0:T(8,128)(2,1)S(1)}, u32[]{:S(2)}, u32[]{:S(2)}) %all-to-all-start) | async-done | bytes 1114144 | tf_op jit(solution)/shard_map/all_to_all | solution.py:786
  39.0 4.5 %residual.2 = (bf16[32,256,256]{2,1,0:T(8,128)(2,1)S(1)}, bf16[32,256,256]{2,1,0:T(8,128)(2,1)}, f32[2,4,256]{2,1,0:T(4,128)S(1)}, bf16[4,256,256]{2,1,0:T(8,128)(2,1)S(1)}, bf16[4,256,256]{2,1,0:T(8,128)(2,1)S(1)}) custom-call(bf16[256,2176]{1,0:T(8,128)(2,1)S(1)} %bitcast.15, bf16[1,32,256,256]{3,2,1,0:T(8,128)(2,1)} %movie.3), custom_call_target="tpu_custom_call" | custom-call | flops 1 | bytes 1 | tf_op jit(solution)/shard_map/residual/pallas_call | solution.py:270
  43.5 1.9 %collective-permute-start.6 = (bf16[4,256,256]{2,1,0:T(8,128)(2,1)S(1)}, bf16[4,256,256]{2,1,0:T(8,128)(2,1)S(1)}, u32[]{:S(2)}, u32[]{:S(2)}) collective-permute-start(bf16[4,256,256]{2,1,0:T(8,128)(2,1)S(1)} %get-tuple-element.55), channel_id=1, source_target_pairs={{0,4},{4,8},{8,12},{12,16},{16,20},{20,24},{24,28},{1,5},{5,9},{9,... | collective-permute-start | bytes 1572872 | tf_op jit(solution)/shard_map/ppermute | solution.py:783
  45.4 1.3 %collective-permute-start.7 = (bf16[4,256,256]{2,1,0:T(8,128)(2,1)S(1)}, bf16[4,256,256]{2,1,0:T(8,128)(2,1)S(1)}, u32[]{:S(2)}, u32[]{:S(2)}) collective-permute-start(bf16[4,256,256]{2,1,0:T(8,128)(2,1)S(1)} %get-tuple-element.56), channel_id=1, source_target_pairs={{4,0},{8,4},{12,8},{16,12},{20,16},{24,20},{28,24},{5,1},{9,5},{13... | collective-permute-start | bytes 1572872 | tf_op jit(solution)/shard_map/ppermute | solution.py:783
  46.8 9.9 %residual.3 = (bf16[32,256,256]{2,1,0:T(8,128)(2,1)S(1)}, bf16[32,256,256]{2,1,0:T(8,128)(2,1)}, f32[6,4,256]{2,1,0:T(4,128)S(1)}, bf16[4,256,256]{2,1,0:T(8,128)(2,1)S(1)}, bf16[4,256,256]{2,1,0:T(8,128)(2,1)S(1)}) custom-call(bf16[256,2176]{1,0:T(8,128)(2,1)S(1)} %bitcast.16, ...), custom_call_target="tpu_custom_call", output_to_operand_aliasing={{0}: (2, {}), {1}: (3, {})} | custom-call | flops 1 | bytes 1 | tf_op jit(solution)/shard_map/residual/pallas_call | solution.py:270
  56.6 0.0 copy-start
  56.6 0.0 copy-start.2
  56.6 0.0 collective-permute-done.movie_next
  56.7 0.0 collective-permute-done.1.movie_prev
  56.7 1.9 %near.1 = (bf16[8,256,256]{2,1,0:T(8,128)(2,1)S(1)}, bf16[8,256,256]{2,1,0:T(8,128)(2,1)S(1)}, f32[40,256]{1,0:T(8,128)S(1)}) custom-call(bf16[256,2176]{1,0:T(8,128)(2,1)S(1)} %bitcast.17, bf16[4,256,256]{2,1,0:T(8,128)(2,1)S(1)} %collective-permute-done.movie_next, bf16[4,256,256]{2,1,0:T(8,128)(2,1)S(1)} %collective-permute-done.1.movie_prev, ...), custom_call_target="tpu_custom_call" | custom-call | flops 1 | bytes 1 | tf_op jit(solution)/shard_map/near/pallas_call | solution.py:321
  58.6 4.6 %collective-permute-start.2 = (bf16[4,256,256]{2,1,0:T(8,128)(2,1)S(1)}, bf16[4,256,256]{2,1,0:T(8,128)(2,1)S(1)}, u32[]{:S(2)}, u32[]{:S(2)}) collective-permute-start(bf16[4,256,256]{2,1,0:T(8,128)(2,1)S(1)} %get-tuple-element.47), channel_id=1, source_target_pairs={{0,4},{4,8},{8,12},{12,16},{16,20},{20,24},{24,28},{1,5},{5,9},{9,... | collective-permute-start | bytes 1572872 | tf_op jit(solution)/shard_map/ppermute | solution.py:783
  63.2 1.3 %collective-permute-start.3 = (bf16[4,256,256]{2,1,0:T(8,128)(2,1)S(1)}, bf16[4,256,256]{2,1,0:T(8,128)(2,1)S(1)}, u32[]{:S(2)}, u32[]{:S(2)}) collective-permute-start(bf16[4,256,256]{2,1,0:T(8,128)(2,1)S(1)} %get-tuple-element.48), channel_id=1, source_target_pairs={{4,0},{8,4},{12,8},{16,12},{20,16},{24,20},{28,24},{5,1},{9,5},{13... | collective-permute-start | bytes 1572872 | tf_op jit(solution)/shard_map/ppermute | solution.py:783
  64.5 1.3 %collective-permute-start.4 = (f32[40,256]{1,0:T(8,128)S(1)}, f32[40,256]{1,0:T(8,128)S(1)}, u32[]{:S(2)}, u32[]{:S(2)}) collective-permute-start(f32[40,256]{1,0:T(8,128)S(1)} %get-tuple-element.51.noise), channel_id=1, source_target_pairs={{0,1},{1,2},{2,3},{4,5},{5,6},{6,7},{8,9},{9,10},{10,11},{12,13},{... | collective-permute-start | bytes 122888 | tf_op jit(solution)/shard_map/ppermute | solution.py:802
  65.8 0.9 collective-permute-done.4.noise_before
  66.6 1.5 %collective-permute-start.5 = (f32[40,256]{1,0:T(8,128)S(1)}, f32[40,256]{1,0:T(8,128)S(1)}, u32[]{:S(2)}, u32[]{:S(2)}) collective-permute-start(f32[40,256]{1,0:T(8,128)S(1)} %get-tuple-element.51.noise), channel_id=1, source_target_pairs={{1,0},{2,1},{3,2},{5,4},{6,5},{7,6},{9,8},{10,9},{11,10},{13,12},{... | collective-permute-start | bytes 122888 | tf_op jit(solution)/shard_map/ppermute | solution.py:803
  68.1 3.6 %collective-permute-done.5.noise_after = f32[40,256]{1,0:T(8,128)S(1)} collective-permute-done((f32[40,256]{1,0:T(8,128)S(1)}, f32[40,256]{1,0:T(8,128)S(1)}, u32[]{:S(2)}, u32[]{:S(2)}) %collective-permute-start.5) | collective-permute-done | bytes 40992 | tf_op jit(solution)/shard_map/ppermute | solution.py:803
  71.7 5.2 %weights.1 = (bf16[32,256,256]{2,1,0:T(8,128)(2,1)S(1)}, bf16[3,256,256]{2,1,0:T(8,128)(2,1)S(1)}, bf16[3,256,256]{2,1,0:T(8,128)(2,1)S(1)}) custom-call(bf16[32,256,256]{2,1,0:T(8,128)(2,1)S(1)} %get-tuple-element.49.own, bf16[8,256,256]{2,1,0:T(8,128)(2,1)S(1)} %get-tuple-element.50.near, f32[40,256]{1,0:T(8,128)S(1)} %get-tuple-element.51.noise, ...), custom_call_target="tpu_custom_call" | custom-call | flops 1 | bytes 1 | tf_op jit(solution)/shard_map/weights/pallas_call | solution.py:399
  76.8 0.0 copy-done
  76.8 0.0 copy-done.2
  76.9 4.0 %annulus_middle.1 = (bf16[1,32,256,256]{3,2,1,0:T(8,128)(2,1)}, f32[256,256]{1,0:T(8,128)S(1)}, f32[256,256]{1,0:T(8,128)S(1)}, f32[256,256]{1,0:T(8,128)S(1)}) custom-call(bf16[32,256,256]{2,1,0:T(8,128)(2,1)S(1)} %copy-done, bf16[8,256,256]{2,1,0:T(8,128)(2,1)S(1)} %get-tuple-element.57.near, bf16[32,256,256]{2,1,0:T(8,128)(2,1)S(1)} %get-tuple-element.52.weight, ...), custom_call_target="tpu_custom_call" | custom-call | flops 1 | bytes 1 | tf_op jit(solution)/shard_map/annulus_middle/pallas_call | solution.py:632
  80.9 0.0 collective-permute-done.6.above
  80.9 0.0 collective-permute-done.7.below
  80.9 2.3 %annulus_mid.1 = (bf16[1,32,256,256]{3,2,1,0:T(8,128)(2,1)}, f32[256,256]{1,0:T(8,128)S(1)}, f32[2,4,256,256]{3,2,1,0:T(8,128)S(1)}, f32[256,128]{1,0:T(8,128)S(1)}, bf16[256,256]{1,0:T(8,128)(2,1)S(1)}) custom-call(bf16[32,256,256]{2,1,0:T(8,128)(2,1)S(1)} %copy-done, ...), custom_call_target="tpu_custom_call", output_to_operand_aliasing={{0}: (5, {})} | custom-call | flops 1073741824 | bytes 5242880 | tf_op jit(solution)/shard_map/annulus_mid/pallas_call | solution.py:632
  83.3 6.6 %collective-permute-done.2.above = bf16[4,256,256]{2,1,0:T(8,128)(2,1)S(1)} collective-permute-done((bf16[4,256,256]{2,1,0:T(8,128)(2,1)S(1)}, bf16[4,256,256]{2,1,0:T(8,128)(2,1)S(1)}, u32[]{:S(2)}, u32[]{:S(2)}) %collective-permute-start.2) | collective-permute-done | bytes 524320 | tf_op jit(solution)/shard_map/ppermute | solution.py:783
  89.9 0.0 collective-permute-done.3.below
  89.9 0.0 copy-start.3
  89.9 0.0 copy-start.4
  89.9 0.0 copy-start.5
  89.9 2.5 %annulus_end.1 = (bf16[256,1024]{1,0:T(8,128)(2,1)}, bf16[2,4,256,256]{3,2,1,0:T(8,128)(2,1)S(1)}) custom-call(bf16[32,256,256]{2,1,0:T(8,128)(2,1)S(1)} %copy-done, bf16[4,256,256]{2,1,0:T(8,128)(2,1)S(1)} %collective-permute-done.2.above, bf16[4,256,256]{2,1,0:T(8,128)(2,1)S(1)} %collective-permute-done.3.below, ...), custom_call_target="tpu_custom_call" | custom-call | flops 1 | bytes 1 | tf_op jit(solution)/shard_map/annulus_end/pallas_call | solution.py:665
  92.4 6.7 %all-to-all-start.1 = ((bf16[8,32,1024]{2,1,0:T(8,128)(2,1)}), bf16[8,32,1024]{2,1,0:T(8,128)(2,1)S(1)}, u32[]{:S(2)}, u32[]{:S(2)}) async-start(bf16[8,32,1024]{2,1,0:T(8,128)(2,1)} %bitcast.8), calls=%async_computation.1 | async-start | bytes 1048576 | tf_op jit(solution)/shard_map/all_to_all | solution.py:812
  99.1 0.0 copy-done.3
  99.1 0.0 copy-done.4
  99.1 0.0 copy-done.5
  99.2 0.3 prepare.1
  99.5 0.0 copy-start.1
  99.5 1.0 late_rows.1
  100.5 13.3 %all-to-all-done.1 = bf16[8,32,1024]{2,1,0:T(8,128)(2,1)S(1)} async-done(((bf16[8,32,1024]{2,1,0:T(8,128)(2,1)}), bf16[8,32,1024]{2,1,0:T(8,128)(2,1)S(1)}, u32[]{:S(2)}, u32[]{:S(2)}) %all-to-all-start.1) | async-done | bytes 524320 | tf_op jit(solution)/shard_map/all_to_all | solution.py:812
  113.8 0.0 copy-done.1
  113.8 1.5 %traces.1 = f32[128,256]{1,0:T(8,128)} custom-call(bf16[128,1024]{1,0:T(8,128)(2,1)S(1)} %get-tuple-element.69.hots, f32[4,128,256]{2,1,0:T(8,128)S(1)} %get-tuple-element.70.tables, bf16[128,256]{1,0:T(8,128)(2,1)S(1)} %bitcast.20, bf16[256,1024]{1,0:T(8,128)(2,1)S(1)} %bitcast.18), custom_call_target="tpu_custom_call" | custom-call | flops 1 | bytes 1 | tf_op jit(solution)/shard_map/traces/pallas_call | solution.py:756
  (1 shorter events, 0.0 us)
Async XLA Ops:
  0.6 16.9 %copy-start.6 = (bf16[1,128,1024]{2,1,0:T(8,128)(2,1)S(1)}, bf16[1,128,1024]{2,1,0:T(8,128)(2,1)}, u32[]{:S(2)}) copy-start(bf16[1,128,1024]{2,1,0:T(8,128)(2,1)} %param.9) | copy-start | bytes 786436
  3.1 35.9 %all-to-all-start = ((bf16[8,32,2176]{2,1,0:T(8,128)(2,1)}), bf16[8,32,2176]{2,1,0:T(8,128)(2,1)S(1)}, u32[]{:S(2)}, u32[]{:S(2)}) async-start(bf16[8,32,2176]{2,1,0:T(8,128)(2,1)} %bitcast.23), calls=%async_computation | async-start | bytes 2228224 | tf_op jit(solution)/shard_map/all_to_all | solution.py:786
  11.6 45.0 %collective-permute-start = (bf16[4,256,256]{2,1,0:T(8,128)(2,1)S(1)}, bf16[4,256,256]{2,1,0:T(8,128)(2,1)S(1)}, u32[]{:S(2)}, u32[]{:S(2)}) collective-permute-start(bf16[4,256,256]{2,1,0:T(8,128)(2,1)S(1)} %get-tuple-element.73), channel_id=1, source_target_pairs={{4,0},{8,4},{12,8},{16,12},{20,16},{24,20},{28,24},{5,1},{9,5},{13... | collective-permute-start | bytes 1572872 | tf_op jit(solution)/shard_map/ppermute | solution.py:783
  12.9 43.7 %collective-permute-start.1 = (bf16[4,256,256]{2,1,0:T(8,128)(2,1)S(1)}, bf16[4,256,256]{2,1,0:T(8,128)(2,1)S(1)}, u32[]{:S(2)}, u32[]{:S(2)}) collective-permute-start(bf16[4,256,256]{2,1,0:T(8,128)(2,1)S(1)} %get-tuple-element.72), channel_id=1, source_target_pairs={{0,4},{4,8},{8,12},{12,16},{16,20},{20,24},{24,28},{1,5},{5,9},{9,... | collective-permute-start | bytes 1572872 | tf_op jit(solution)/shard_map/ppermute | solution.py:783
  43.5 37.4 %collective-permute-start.6 = (bf16[4,256,256]{2,1,0:T(8,128)(2,1)S(1)}, bf16[4,256,256]{2,1,0:T(8,128)(2,1)S(1)}, u32[]{:S(2)}, u32[]{:S(2)}) collective-permute-start(bf16[4,256,256]{2,1,0:T(8,128)(2,1)S(1)} %get-tuple-element.55), channel_id=1, source_target_pairs={{0,4},{4,8},{8,12},{12,16},{16,20},{20,24},{24,28},{1,5},{5,9},{9,... | collective-permute-start | bytes 1572872 | tf_op jit(solution)/shard_map/ppermute | solution.py:783
  45.4 35.5 %collective-permute-start.7 = (bf16[4,256,256]{2,1,0:T(8,128)(2,1)S(1)}, bf16[4,256,256]{2,1,0:T(8,128)(2,1)S(1)}, u32[]{:S(2)}, u32[]{:S(2)}) collective-permute-start(bf16[4,256,256]{2,1,0:T(8,128)(2,1)S(1)} %get-tuple-element.56), channel_id=1, source_target_pairs={{4,0},{8,4},{12,8},{16,12},{20,16},{24,20},{28,24},{5,1},{9,5},{13... | collective-permute-start | bytes 1572872 | tf_op jit(solution)/shard_map/ppermute | solution.py:783
  56.6 20.2 %copy-start = (bf16[32,256,256]{2,1,0:T(8,128)(2,1)S(1)}, bf16[32,256,256]{2,1,0:T(8,128)(2,1)}, u32[]{:S(2)}) copy-start(bf16[32,256,256]{2,1,0:T(8,128)(2,1)} %get-tuple-element.41.own) | copy-start | bytes 12582916
  56.6 20.2 %copy-start.2 = (f32[1,256]{1,0:T(1,128)S(1)}, f32[1,256]{1,0:T(1,128)}, u32[]{:S(2)}) copy-start(f32[1,256]{1,0:T(1,128)} %gain.3) | copy-start | bytes 3076
  58.6 31.3 %collective-permute-start.2 = (bf16[4,256,256]{2,1,0:T(8,128)(2,1)S(1)}, bf16[4,256,256]{2,1,0:T(8,128)(2,1)S(1)}, u32[]{:S(2)}, u32[]{:S(2)}) collective-permute-start(bf16[4,256,256]{2,1,0:T(8,128)(2,1)S(1)} %get-tuple-element.47), channel_id=1, source_target_pairs={{0,4},{4,8},{8,12},{12,16},{16,20},{20,24},{24,28},{1,5},{5,9},{9,... | collective-permute-start | bytes 1572872 | tf_op jit(solution)/shard_map/ppermute | solution.py:783
  63.2 26.7 %collective-permute-start.3 = (bf16[4,256,256]{2,1,0:T(8,128)(2,1)S(1)}, bf16[4,256,256]{2,1,0:T(8,128)(2,1)S(1)}, u32[]{:S(2)}, u32[]{:S(2)}) collective-permute-start(bf16[4,256,256]{2,1,0:T(8,128)(2,1)S(1)} %get-tuple-element.48), channel_id=1, source_target_pairs={{4,0},{8,4},{12,8},{16,12},{20,16},{24,20},{28,24},{5,1},{9,5},{13... | collective-permute-start | bytes 1572872 | tf_op jit(solution)/shard_map/ppermute | solution.py:783
  64.5 2.2 %collective-permute-start.4 = (f32[40,256]{1,0:T(8,128)S(1)}, f32[40,256]{1,0:T(8,128)S(1)}, u32[]{:S(2)}, u32[]{:S(2)}) collective-permute-start(f32[40,256]{1,0:T(8,128)S(1)} %get-tuple-element.51.noise), channel_id=1, source_target_pairs={{0,1},{1,2},{2,3},{4,5},{5,6},{6,7},{8,9},{9,10},{10,11},{12,13},{... | collective-permute-start | bytes 122888 | tf_op jit(solution)/shard_map/ppermute | solution.py:802
  66.6 5.1 %collective-permute-start.5 = (f32[40,256]{1,0:T(8,128)S(1)}, f32[40,256]{1,0:T(8,128)S(1)}, u32[]{:S(2)}, u32[]{:S(2)}) collective-permute-start(f32[40,256]{1,0:T(8,128)S(1)} %get-tuple-element.51.noise), channel_id=1, source_target_pairs={{1,0},{2,1},{3,2},{5,4},{6,5},{7,6},{9,8},{10,9},{11,10},{13,12},{... | collective-permute-start | bytes 122888 | tf_op jit(solution)/shard_map/ppermute | solution.py:803
  89.9 9.2 %copy-start.3 = (s32[1,128,1]{1,2,0:T(1,128)S(1)}, s32[1,128,1]{1,2,0:T(1,128)}, u32[]{:S(2)}) copy-start(s32[1,128,1]{1,2,0:T(1,128)} %param.11) | copy-start | bytes 1540
  89.9 9.3 %copy-start.4 = (f32[1,128]{1,0:T(1,128)S(1)}, f32[1,128]{1,0:T(1,128)}, u32[]{:S(2)}) copy-start(f32[1,128]{1,0:T(1,128)} %slow.1) | copy-start | bytes 1540
  89.9 9.3 %copy-start.5 = (f32[1,128]{1,0:T(1,128)S(1)}, f32[1,128]{1,0:T(1,128)}, u32[]{:S(2)}) copy-start(f32[1,128]{1,0:T(1,128)} %fast.1) | copy-start | bytes 1540
  92.4 21.4 %all-to-all-start.1 = ((bf16[8,32,1024]{2,1,0:T(8,128)(2,1)}), bf16[8,32,1024]{2,1,0:T(8,128)(2,1)S(1)}, u32[]{:S(2)}, u32[]{:S(2)}) async-start(bf16[8,32,1024]{2,1,0:T(8,128)(2,1)} %bitcast.8), calls=%async_computation.1 | async-start | bytes 1048576 | tf_op jit(solution)/shard_map/all_to_all | solution.py:812
  99.5 14.3 %copy-start.1 = (bf16[1,128,256]{2,1,0:T(8,128)(2,1)S(1)}, bf16[1,128,256]{2,1,0:T(8,128)(2,1)}, u32[]{:S(2)}) copy-start(bf16[1,128,256]{2,1,0:T(8,128)(2,1)} %param.10) | copy-start | bytes 196612
